TPU v7x, 128 devices: a whole 4x4x4 slice. The times are simulated.
128 devices in a mesh: seq: 32 (over z, x, core), bkt: 4 (over y).
Axes of the slice: x: 4, y: 4, z: 4, core: 2. Of those that a mesh axis runs over, the one named last changes fastest.
Arguments:
- tokens: bfloat16 [8192, 4096], P('seq'), may hold values from -6 to 6
- weights: bfloat16 [4096, 2, 2048], P(None, None, 'bkt'), may hold values from -0.09375 to 0.09375
- cotangent: bfloat16 [8192, 2048], P('seq', 'bkt'), may hold values from -6 to 6
- buckets: int32 [2, 16, 8192], P(None, 'bkt', 'seq'), may hold values from 0 to 63, as said below
Outputs:
- token_grads: bfloat16 [8192, 4096], P(('seq', 'bkt'))
Inputs may be any that keep to these rules, and one draw needn't show every extreme that they name: In every round and head, the tokens of one seq shard that fall into the buckets b with b // 2 == k number at most 12, and for one k every shard has exactly 12; a bucket holds at most 192 tokens, and some hold exactly 192; every bucket holds tokens of every shard.
All inputs are finite; a program needn't handle non-finite values.
Results may differ from a plain program's by a relative error of at most 0.025.
Values may be sent and summed in bfloat16 or wider, within the bound.
No kernel may reach another device: no remote copies, remote signals or barrier semaphores. Data moves between devices by JAX's collectives and lax.ppermute only.
A program may use at most 128 MiB of HBM per device.

v0:
```python
import functools
import math

import jax
import jax.numpy as jnp
from jax import lax
from jax.sharding import PartitionSpec as P

NB = 64


SELF_SCORE = -100000.0
FAR_SCORE = -1000000000.0


def attend(query, values, places, present):
    head_size = query.shape[-1]
    query_half = query.astype(jnp.bfloat16)
    unit_keys = (query * lax.rsqrt(jnp.sum(query * query, axis=-1, keepdims=True) + 1e-06)).astype(
        jnp.bfloat16
    )
    scores = jnp.dot(query_half, unit_keys.T, preferred_element_type=jnp.float32) * (
        1.0 / math.sqrt(head_size)
    )
    row_ids = jnp.arange(query.shape[0], dtype=jnp.int32)
    allowed = present[None, :] & (places[None, :] <= places[:, None])
    scores = jnp.where(allowed, scores, FAR_SCORE)
    scores = jnp.where(row_ids[:, None] == row_ids[None, :], SELF_SCORE, scores)
    row_max = lax.stop_gradient(jnp.max(scores, axis=-1, keepdims=True))
    shifted = jnp.exp(scores - row_max)
    totals = jnp.sum(shifted, axis=-1, keepdims=True)
    probs = (shifted / totals).astype(jnp.bfloat16)
    outputs = jnp.dot(probs, values.astype(jnp.bfloat16), preferred_element_type=jnp.float32)
    return (outputs, row_max[:, 0] + jnp.log(totals[:, 0]))


def attend_blocks(query, values, places, present):
    block_rows = query.shape[-2]
    head_size = query.shape[-1]
    outputs, lse = jax.vmap(attend)(
        query.reshape(-1, block_rows, head_size),
        values.reshape(-1, block_rows, head_size),
        places.reshape(-1, block_rows),
        present.reshape(-1, block_rows),
    )
    return (outputs.reshape(query.shape), lse.reshape(places.shape))


def block_grads(query, values, places, present, out_grad, lse_grad):

    def forward(query_rows, value_rows):
        return attend_blocks(query_rows, value_rows, places, present)

    _, pull = jax.vjp(forward, query, values)
    return pull((out_grad, lse_grad))


def bucket_plan(keys, group_count, group_size, capacity):
    row_count = keys.shape[0]
    ordering = jnp.argsort(keys, stable=True)
    targets = keys // group_size
    matches = (targets[:, None] == jnp.arange(group_count, dtype=jnp.int32)[None, :]).astype(
        jnp.int32
    )
    counts = jnp.sum(matches, axis=0)
    starts = jnp.cumsum(counts) - counts
    slot_ids = jnp.arange(capacity, dtype=jnp.int32)
    filled = slot_ids[None, :] < counts[:, None]
    sources = ordering[jnp.clip(starts[:, None] + slot_ids[None, :], 0, row_count - 1)]
    inverse = jnp.argsort(ordering)
    returns = targets * capacity + inverse - starts[jnp.clip(targets, 0, group_count - 1)]
    return (sources, filled, returns)


def pick_rows(source_rows, sources, filled):
    picked = source_rows[sources]
    keep_mask = filled.reshape(filled.shape + (1,) * (picked.ndim - filled.ndim))
    return jnp.where(keep_mask, picked, jnp.zeros((), picked.dtype))


def put_back(flattened, positions):
    return flattened[jnp.clip(positions, 0, flattened.shape[0] - 1)]


def round_cotangents(round_out, round_lse, cotangent, round_count):
    item_count, row_count, head_size = round_out.shape
    head_count = item_count // round_count
    round_values = round_out.astype(jnp.float32).reshape(
        round_count, head_count, row_count, head_size
    )
    round_logs = round_lse.reshape(round_count, head_count, row_count)
    round_share = jax.nn.softmax(round_logs, axis=0)
    upstream = (
        cotangent.reshape(row_count, head_count, head_size).transpose(1, 0, 2).astype(jnp.float32)
    )
    inner = jnp.sum(upstream[None] * round_values, axis=-1)
    lse_grad = round_share * (inner - jnp.sum(round_share * inner, axis=0))
    out_grad = (round_share[..., None] * upstream[None]).astype(jnp.bfloat16)
    return (
        out_grad.reshape(item_count, row_count, head_size),
        lse_grad.reshape(item_count, row_count),
    )


def sum_rounds(per_round, round_count):
    item_count, row_count, head_size = per_round.shape
    head_count = item_count // round_count
    summed = (
        per_round.astype(jnp.float32)
        .reshape(round_count, head_count, row_count, head_size)
        .sum(axis=0)
    )
    return summed.astype(jnp.bfloat16).transpose(1, 0, 2).reshape(row_count, head_count * head_size)


def per_item(matrix, round_count, head_count, head_size):
    row_count = matrix.shape[0]
    heads_first = matrix.reshape(row_count, head_count, head_size).transpose(1, 0, 2)
    repeated = jnp.broadcast_to(heads_first[None], (round_count,) + heads_first.shape)
    return repeated.reshape(round_count * head_count, row_count, head_size)


def owner_layout(query_in, value_in, bucket_in, place_in, base, per_owner, bucket_cap):
    item_count = bucket_in.shape[0]
    head_size = query_in.shape[-1]
    flat_ids = bucket_in.reshape(item_count, -1)
    local_ids = jnp.where(flat_ids >= 0, flat_ids - base, per_owner).astype(jnp.int32)
    planner = functools.partial(
        bucket_plan, group_count=per_owner, group_size=1, capacity=bucket_cap
    )
    sources, present, returns = jax.vmap(planner)(local_ids)
    query_lay = jax.vmap(pick_rows)(query_in.reshape(item_count, -1, head_size), sources, present)
    value_lay = jax.vmap(pick_rows)(value_in.reshape(item_count, -1, head_size), sources, present)
    place_lay = jnp.where(
        present, jax.vmap(pick_rows)(place_in.reshape(item_count, -1), sources, present), -1
    )
    return (query_lay, value_lay, place_lay, present, sources, returns)


def to_slots(layout, returns, bucket_in):
    item_count = layout.shape[0]
    flattened = layout.reshape((item_count, -1) + layout.shape[3:])
    picked = jax.vmap(put_back)(flattened, returns)
    picked = picked.reshape(bucket_in.shape + layout.shape[3:])
    keep_mask = (bucket_in >= 0).reshape(bucket_in.shape + (1,) * (layout.ndim - 3))
    return jnp.where(keep_mask, picked, jnp.zeros((), picked.dtype))


def from_slots(received, returns):
    flattened = received.reshape((received.shape[0], -1) + received.shape[3:])
    return jax.vmap(put_back)(flattened, returns)


def owner_grads(
    query_lay, value_lay, place_lay, present, lay_sources, lay_returns, grad_in, lse_in, bucket_in
):
    item_count = grad_in.shape[0]
    head_size = grad_in.shape[-1]
    grad_lay = jax.vmap(pick_rows)(
        grad_in.reshape(item_count, -1, head_size), lay_sources, present
    ).astype(jnp.float32)
    lse_lay = jax.vmap(pick_rows)(lse_in.reshape(item_count, -1), lay_sources, present)
    query_grad, value_grad = block_grads(
        query_lay.astype(jnp.float32),
        value_lay.astype(jnp.float32),
        place_lay,
        present,
        grad_lay,
        lse_lay,
    )
    return (
        to_slots(query_grad.astype(jnp.bfloat16), lay_returns, bucket_in),
        to_slots(value_grad.astype(jnp.bfloat16), lay_returns, bucket_in),
    )


def per_device(tokens, weights, cotangent, buckets):
    tokens_here = tokens.shape[0]
    round_count, heads_here, _ = buckets.shape
    item_count = round_count * heads_here
    head_size = cotangent.shape[1] // heads_here
    owner_count = lax.axis_size("seq")
    seq_index = lax.axis_index("seq")
    per_owner = NB // owner_count
    most_bucket = 3 * tokens_here // (2 * NB)
    capacity = per_owner * most_bucket
    bucket_cap = (owner_count * most_bucket + 127) // 128 * 128
    base = seq_index * per_owner
    projected = jnp.einsum(
        "td,dcf->tcf", tokens, weights, preferred_element_type=jnp.float32
    ).astype(jnp.bfloat16)
    shared = per_item(projected[:, 0], round_count, heads_here, head_size)
    values = per_item(projected[:, 1], round_count, heads_here, head_size)
    row_ids = buckets.reshape(item_count, tokens_here)
    planner = functools.partial(
        bucket_plan, group_count=owner_count, group_size=per_owner, capacity=capacity
    )
    sources, filled, returns = jax.vmap(planner)(row_ids)
    query_send = jax.vmap(pick_rows)(shared, sources, filled)
    value_send = jax.vmap(pick_rows)(values, sources, filled)
    bucket_send = jnp.where(filled, jax.vmap(pick_rows)(row_ids, sources, filled), -1)
    place_send = jnp.where(filled, seq_index * tokens_here + sources, -1)
    query_in, value_in, bucket_in, place_in = (
        lax.all_to_all(query_send, "seq", split_axis=1, concat_axis=1, tiled=True),
        lax.all_to_all(value_send, "seq", split_axis=1, concat_axis=1, tiled=True),
        lax.all_to_all(bucket_send, "seq", split_axis=1, concat_axis=1, tiled=True),
        lax.all_to_all(place_send, "seq", split_axis=1, concat_axis=1, tiled=True),
    )
    query_lay, value_lay, place_lay, present, lay_sources, lay_returns = owner_layout(
        query_in, value_in, bucket_in, place_in, base, per_owner, bucket_cap
    )
    outputs, lse = attend_blocks(query_lay.astype(jnp.float32), value_lay, place_lay, present)
    out_slots = to_slots(outputs.astype(jnp.bfloat16), lay_returns, bucket_in)
    lse_slots = to_slots(lse, lay_returns, bucket_in)
    out_recv, lse_recv = (
        lax.all_to_all(out_slots, "seq", split_axis=1, concat_axis=1, tiled=True),
        lax.all_to_all(
            lse_slots.astype(jnp.bfloat16), "seq", split_axis=1, concat_axis=1, tiled=True
        ).astype(lse_slots.dtype),
    )
    round_out = from_slots(out_recv, returns)
    round_lse = from_slots(lse_recv, returns)
    out_grad, lse_grad = round_cotangents(round_out, round_lse, cotangent, round_count)
    grad_send = jax.vmap(pick_rows)(out_grad, sources, filled)
    lse_send = jax.vmap(pick_rows)(lse_grad, sources, filled)
    query_part = lax.all_to_all(query_send, "seq", split_axis=1, concat_axis=1, tiled=True)
    value_part = lax.all_to_all(value_send, "seq", split_axis=1, concat_axis=1, tiled=True)
    bucket_part = lax.all_to_all(bucket_send, "seq", split_axis=1, concat_axis=1, tiled=True)
    place_part = lax.all_to_all(place_send, "seq", split_axis=1, concat_axis=1, tiled=True)
    grad_part = lax.all_to_all(grad_send, "seq", split_axis=1, concat_axis=1, tiled=True)
    lse_part = lax.all_to_all(
        lse_send.astype(jnp.bfloat16), "seq", split_axis=1, concat_axis=1, tiled=True
    ).astype(lse_send.dtype)
    query_again, value_again, place_again, present_again, sources_again, returns_again = (
        owner_layout(query_part, value_part, bucket_part, place_part, base, per_owner, bucket_cap)
    )
    back_query, back_value = owner_grads(
        query_again,
        value_again,
        place_again,
        present_again,
        sources_again,
        returns_again,
        grad_part,
        lse_part,
        bucket_part,
    )
    query_recv = lax.all_to_all(back_query, "seq", split_axis=1, concat_axis=1, tiled=True)
    value_recv = lax.all_to_all(back_value, "seq", split_axis=1, concat_axis=1, tiled=True)
    query_grads = sum_rounds(from_slots(query_recv, returns), round_count)
    value_grads = sum_rounds(from_slots(value_recv, returns), round_count)
    grads = jnp.stack([query_grads, value_grads], axis=1)
    return lax.psum_scatter(
        jnp.einsum("tcf,dcf->td", grads, weights, preferred_element_type=jnp.float32).astype(
            jnp.bfloat16
        ),
        "bkt",
        scatter_dimension=0,
        tiled=True,
    )


def solution(mesh):
    in_specs = (P("seq", None), P(None, None, "bkt"), P("seq", "bkt"), P(None, "bkt", "seq"))
    out_specs = P(("seq", "bkt"), None)
    return jax.shard_map(
        per_device, mesh=mesh, in_specs=in_specs, out_specs=out_specs, check_vma=False
    )
```

profile of v0, /device:TPU:0, one launch (start us, length us, event | category | flops | bytes accessed | tf_op | source)
XLA Modules:
  0.0 665.1 jit_solution(18067941507051109924)
XLA Ops:
  6.5 1.5 reshape.490
  9.9 5.7 fusion.28
  16.2 20.1 %gather_fusion = s32[3072]{0:T(1024)S(1)} fusion(s32[8,256]{1,0:T(8,128)} %get-tuple-element.9, s32[3072]{0:T(1024)S(1)} %reshape.516), kind=kCustom, calls=%fused_computation | custom fusion | bytes 49152 | tf_op jit(solution)/shard_map/vmap()/gather | solution.py:69
  37.1 19.2 %gather_fusion.1 = s32[3072]{0:T(1024)S(1)} fusion(s32[8,256]{1,0:T(8,128)S(1)} %copy-done.2, s32[3072]{0:T(1024)S(1)} %reshape.522), kind=kCustom, calls=%fused_computation.1 | custom fusion | bytes 49152 | tf_op jit(solution)/shard_map/vmap()/gather | solution.py:76
  57.7 8.2 %all-to-all-start = ((s32[8,32,12]{2,0,1:T(8,128)}), s32[8,32,12]{2,0,1:T(8,128)S(1)}, u32[]{:S(2)}, u32[]{:S(2)}) async-start(s32[8,32,12]{2,0,1:T(8,128)} %copy.96), calls=%async_computation | async-start | bytes 262144 | tf_op jit(solution)/shard_map/all_to_all | solution.py:228
  66.0 16.4 %gather_fusion.4 = bf16[3072,128]{1,0:T(8,128)(2,1)S(1)} fusion(bf16[8,256,128]{2,1,0:T(8,128)(2,1)S(1)} %bitcast.94, s32[3072]{0:T(1024)S(1)} %reshape.522), kind=kCustom, calls=%fused_computation.4 | custom fusion | bytes 1597440 | tf_op jit(solution)/shard_map/vmap()/gather | solution.py:76
  82.7 16.4 %gather_fusion.12 = bf16[3072,128]{1,0:T(8,128)(2,1)S(1)} fusion(bf16[8,256,128]{2,1,0:T(8,128)(2,1)S(1)} %bitcast.95, s32[3072]{0:T(1024)S(1)} %reshape.522), kind=kCustom, calls=%fused_computation.12 | custom fusion | bytes 1597440 | tf_op jit(solution)/shard_map/vmap()/gather | solution.py:76
  99.1 1.2 reshape.591
  100.2 1.8 broadcast_select_fusion
  102.0 1.8 copy.110
  104.6 1.8 copy.122
  106.4 7.4 %all-to-all-start.1 = ((s32[8,32,12]{2,0,1:T(8,128)}), s32[8,32,12]{2,0,1:T(8,128)S(1)}, u32[]{:S(2)}, u32[]{:S(2)}) async-start(s32[8,32,12]{2,0,1:T(8,128)} %copy.103), calls=%async_computation.1 | async-start | bytes 262144 | tf_op jit(solution)/shard_map/all_to_all | solution.py:229
  115.8 5.8 all-to-all-done.1
  121.5 3.9 all-to-all-start.2
  126.3 13.4 %gather_fusion.6 = s32[3072]{0:T(1024)S(1)} fusion(s32[8,2]{1,0:T(8,128)S(1)} %sub.101, s32[3072]{0:T(1024)S(1)} %reshape.552), kind=kCustom, calls=%fused_computation.6 | custom fusion | bytes 49152 | tf_op jit(solution)/shard_map/vmap()/gather | solution.py:71
  139.9 26.1 %gather_fusion.2 = s32[4096]{0:T(1024)S(1)} fusion(s32[8,384]{1,0:T(8,128)} %get-tuple-element.10, s32[4096]{0:T(1024)S(1)} %bitcast.93), kind=kCustom, calls=%fused_computation.2 | custom fusion | bytes 65536 | tf_op jit(solution)/shard_map/vmap()/gather | solution.py:69
  166.1 25.3 %gather_fusion.3 = s32[4096]{0:T(1024)S(1)} fusion(s32[8,384]{1,0:T(8,128)S(1)} %reshape.491, s32[4096]{0:T(1024)S(1)} %bitcast.84), kind=kCustom, calls=%fused_computation.3 | custom fusion | bytes 65536 | tf_op jit(solution)/shard_map/vmap()/gather | solution.py:76
  192.1 3.3 sort.81.cloned.1.call-done
  196.2 7.5 %all-to-all-start.5 = ((bf16[8,32,12,128]{3,0,2,1:T(8,128)(2,1)}), bf16[8,32,12,128]{3,0,2,1:T(8,128)(2,1)}, u32[]{:S(2)}, u32[]{:S(2)}) async-start(bf16[8,32,12,128]{3,0,2,1:T(8,128)(2,1)} %copy.122), calls=%async_computation.5 | async-start | bytes 1572864 | tf_op jit(solution)/shard_map/all_to_all | solution.py:227
  203.8 21.8 %gather_fusion.5 = bf16[4096,128]{1,0:T(8,128)(2,1)S(1)} fusion(bf16[8,384,128]{2,1,0:T(8,128)(2,1)S(1)} %copy.111, s32[4096]{0:T(1024)S(1)} %bitcast.85), kind=kCustom, calls=%fused_computation.5 | custom fusion | bytes 2129920 | tf_op jit(solution)/shard_map/vmap()/gather | solution.py:76
  225.6 1.3 multiply_reduce_fusion
  227.0 2.9 fusion.17
  229.9 2.0 fusion.93
  232.0 25.1 %gather_fusion.7 = bf16[3072]{0:T(1024)(128)(2,1)S(1)} fusion(bf16[8,512]{1,0:T(8,128)(2,1)S(1)} %add.194, s32[3072]{0:T(1024)S(1)} %reshape.558), kind=kCustom, calls=%fused_computation.7 | custom fusion | bytes 36864 | tf_op jit(solution)/shard_map/vmap()/gather | solution.py:82
  258.2 5.2 divide_convert_fusion
  263.5 7.5 %all-to-all-start.3 = ((bf16[8,32,12]{2,0,1:T(8,128)(2,1)}), bf16[8,32,12]{2,0,1:T(8,128)(2,1)S(1)}, u32[]{:S(2)}, u32[]{:S(2)}) async-start(bf16[8,32,12]{2,0,1:T(8,128)(2,1)} %copy.115), calls=%async_computation.3 | async-start | bytes 131072 | tf_op jit(solution)/shard_map/all_to_all | solution.py:217
  270.9 1.2 copy.123
  272.2 40.3 %gather_fusion.13 = bf16[4096,128]{1,0:T(8,128)(2,1)} fusion(bf16[8,384,128]{2,1,0:T(8,128)(2,1)S(1)} %copy.123, s32[4096]{0:T(1024)S(1)} %bitcast.86), kind=kCustom, calls=%fused_computation.13 | custom fusion | bytes 2129920 | tf_op jit(solution)/shard_map/vmap()/gather | solution.py:76
  312.5 3.2 convolution_convert_fusion.4
  315.6 16.4 %gather_fusion.14 = bf16[3072,128]{1,0:T(8,128)(2,1)S(1)} fusion(bf16[8,512,128]{2,1,0:T(8,128)(2,1)S(1)} %bitcast.99, s32[3072]{0:T(1024)S(1)} %reshape.558), kind=kCustom, calls=%fused_computation.14 | custom fusion | bytes 1597440 | tf_op jit(solution)/shard_map/vmap()/gather | solution.py:82
  333.0 1.9 copy.125
  334.8 7.5 %all-to-all-start.6 = ((bf16[8,32,12,128]{3,0,2,1:T(8,128)(2,1)}), bf16[8,32,12,128]{3,0,2,1:T(8,128)(2,1)S(1)}, u32[]{:S(2)}, u32[]{:S(2)}) async-start(bf16[8,32,12,128]{3,0,2,1:T(8,128)(2,1)} %copy.125), calls=%async_computation.6 | async-start | bytes 1572864 | tf_op jit(solution)/shard_map/all_to_all | solution.py:216
  343.1 9.1 %gather_fusion.8 = s32[2048]{0:T(1024)S(1)} fusion(s32[8,32]{1,0:T(8,128)S(1)} %sub.98, s32[2048]{0:T(1024)S(1)} %bitcast.96), kind=kCustom, calls=%fused_computation.8 | custom fusion | bytes 32768 | tf_op jit(solution)/shard_map/vmap()/gather | solution.py:71
  353.6 12.9 %gather_fusion.9 = f32[2048]{0:T(1024)S(1)} fusion(f32[8,384]{1,0:T(8,128)S(1)} %reshape.511, s32[2048]{0:T(1024)S(1)} %bitcast.89), kind=kCustom, calls=%fused_computation.9 | custom fusion | bytes 32768 | tf_op jit(solution)/shard_map/vmap()/gather | solution.py:82
  366.7 0.9 copy-done.6
  367.6 1.2 copy.126
  368.9 11.2 %gather_fusion.15 = bf16[2048,128]{1,0:T(8,128)(2,1)S(1)} fusion(bf16[8,384,128]{2,1,0:T(8,128)(2,1)S(1)} %copy.126, s32[2048]{0:T(1024)S(1)} %bitcast.90), kind=kCustom, calls=%fused_computation.15 | custom fusion | bytes 1064960 | tf_op jit(solution)/shard_map/vmap()/gather | solution.py:82
  380.8 16.4 %gather_fusion.10 = bf16[3072,128]{1,0:T(8,128)(2,1)S(1)} fusion(bf16[8,256,128]{2,1,0:T(8,128)(2,1)S(1)} %fusion.34, s32[3072]{0:T(1024)S(1)} %reshape.522), kind=kCustom, calls=%fused_computation.10 | custom fusion | bytes 1597440 | tf_op jit(solution)/shard_map/vmap()/gather | solution.py:76
  397.4 25.1 %gather_fusion.16 = bf16[3072]{0:T(1024)(128)(2,1)S(1)} fusion(bf16[8,256]{1,0:T(8,128)(2,1)S(1)} %get-tuple-element.13, s32[3072]{0:T(1024)S(1)} %reshape.522), kind=kCustom, calls=%fused_computation.16 | custom fusion | bytes 36864 | tf_op jit(solution)/shard_map/vmap()/gather | solution.py:76
  423.7 7.4 %all-to-all-start.7 = ((bf16[8,32,12]{2,0,1:T(8,128)(2,1)}), bf16[8,32,12]{2,0,1:T(8,128)(2,1)S(1)}, u32[]{:S(2)}, u32[]{:S(2)}) async-start(bf16[8,32,12]{2,0,1:T(8,128)(2,1)} %copy.128), calls=%async_computation.7 | async-start | bytes 131072 | tf_op jit(solution)/shard_map/all_to_all | solution.py:231
  431.8 1.9 copy.119
  433.6 4.9 all-to-all-done.7
  438.5 4.1 all-to-all-start.4
  443.1 25.3 %gather_fusion.17 = f32[4096]{0:T(1024)S(1)} fusion(f32[8,384]{1,0:T(8,128)S(1)} %reshape.514, s32[4096]{0:T(1024)S(1)} %bitcast.87), kind=kCustom, calls=%fused_computation.17 | custom fusion | bytes 65536 | tf_op jit(solution)/shard_map/vmap()/gather | solution.py:76
  468.5 40.2 %gather_fusion.11 = bf16[4096,128]{1,0:T(8,128)(2,1)} fusion(bf16[8,384,128]{2,1,0:T(8,128)(2,1)S(1)} %copy.120, s32[4096]{0:T(1024)S(1)} %bitcast.88), kind=kCustom, calls=%fused_computation.11 | custom fusion | bytes 2129920 | tf_op jit(solution)/shard_map/vmap()/gather | solution.py:76
  508.7 2.7 convolution_convert_fusion.1
  511.4 16.4 %gather_fusion.20 = bf16[3072,128]{1,0:T(8,128)(2,1)S(1)} fusion(bf16[8,512,128]{2,1,0:T(8,128)(2,1)S(1)} %bitcast.98, s32[3072]{0:T(1024)S(1)} %reshape.558), kind=kCustom, calls=%fused_computation.20 | custom fusion | bytes 1597440 | tf_op jit(solution)/shard_map/vmap()/gather | solution.py:82
  528.0 5.8 fusion.16
  534.0 5.0 fusion.19
  539.0 8.3 %fusion.21 = bf16[16,256,128]{2,1,0:T(8,128)(2,1)S(1)} fusion(bf16[16,256,128]{2,1,0:T(8,128)(2,1)S(1)} %get-tuple-element.31, f32[16,256]{1,0:T(8,128)S(1)} %multiply_multiply_fusion, f32[16,256]{1,0:T(8,128)S(1)} %rsqrt.11, bf16[16,256,128]{2,1,0:T(8,128)(2,1)} %bitcast.103, pred[16,256]{1,0:T(8,128)(4,1)S(1)} %iota_compare_fusion.5, ...), kind=kOutput, calls=%fused_computation.50 | convolution fusion | flops 289931264 | bytes 9605120 | tf_op jit(solution)/shard_map/transpose(jvp(vmap()))/dot_general | solution.py:22
  547.3 16.4 %gather_fusion.18 = bf16[3072,128]{1,0:T(8,128)(2,1)S(1)} fusion(bf16[8,512,128]{2,1,0:T(8,128)(2,1)S(1)} %bitcast.97, s32[3072]{0:T(1024)S(1)} %reshape.558), kind=kCustom, calls=%fused_computation.18 | custom fusion | bytes 1597440 | tf_op jit(solution)/shard_map/vmap()/gather | solution.py:82
  563.7 1.2 reshape.506
  564.9 1.8 broadcast_select_fusion.7
  566.6 1.8 copy.132
  568.4 7.5 %all-to-all-start.8 = ((bf16[8,32,12,128]{3,0,2,1:T(8,128)(2,1)}), bf16[8,32,12,128]{3,0,2,1:T(8,128)(2,1)S(1)}, u32[]{:S(2)}, u32[]{:S(2)}) async-start(bf16[8,32,12,128]{3,0,2,1:T(8,128)(2,1)} %copy.132), calls=%async_computation.8 | async-start | bytes 1572864 | tf_op jit(solution)/shard_map/all_to_all | solution.py:248
  575.9 1.8 copy.135
  577.7 12.8 %all-to-all-done.8 = bf16[8,32,12,128]{3,0,2,1:T(8,128)(2,1)S(1)} async-done(((bf16[8,32,12,128]{3,0,2,1:T(8,128)(2,1)}), bf16[8,32,12,128]{3,0,2,1:T(8,128)(2,1)S(1)}, u32[]{:S(2)}, u32[]{:S(2)}) %all-to-all-start.8) | async-done | bytes 786464 | tf_op jit(solution)/shard_map/all_to_all | solution.py:248
  590.5 3.9 all-to-all-start.9
  594.7 1.2 copy.133
  596.0 11.2 %gather_fusion.19 = bf16[2048,128]{1,0:T(8,128)(2,1)S(1)} fusion(bf16[8,384,128]{2,1,0:T(8,128)(2,1)S(1)} %copy.133, s32[2048]{0:T(1024)S(1)} %bitcast.91), kind=kCustom, calls=%fused_computation.19 | custom fusion | bytes 1064960 | tf_op jit(solution)/shard_map/vmap()/gather | solution.py:82
  607.6 1.3 all-to-all-done.9
  609.1 11.2 %gather_fusion.21 = bf16[2048,128]{1,0:T(8,128)(2,1)S(1)} fusion(bf16[8,384,128]{2,1,0:T(8,128)(2,1)S(1)} %copy.136, s32[2048]{0:T(1024)S(1)} %bitcast.92), kind=kCustom, calls=%fused_computation.21 | custom fusion | bytes 1064960 | tf_op jit(solution)/shard_map/vmap()/gather | solution.py:82
  620.8 7.3 %fusion.7 = bf16[256,4096]{1,0:T(8,128)(2,1)} fusion(bf16[4096,2,512]{2,1,0:T(2,128)(2,1)} %param.5, bf16[256,1,512]{2,0,1:T(8,128)(2,1)S(1)} %stack_reshape.7, bf16[256,1,512]{2,0,1:T(8,128)(2,1)S(1)} %stack_reshape.6), kind=kOutput, calls=%fused_computation.29 | convolution fusion | flops 2148794368 | bytes 11010048 | tf_op jit(solution)/shard_map/tcf,dcf->td/dot_general | solution.py:254
  628.0 30.1 %reduce-scatter.2.cloned.1.call-done = bf16[64,4096]{1,0:T(8,128)(2,1)} async-done(((bf16[256,4096]{1,0:T(8,128)(2,1)}), bf16[64,4096]{1,0:T(8,128)(2,1)}) %reduce-scatter.2.cloned.1.call-update) | async-done | bytes 524304 | tf_op jit(solution)/shard_map/reduce_scatter | solution.py:253
  (162 shorter events, 19.1 us)
Async XLA Ops:
  6.5 3.4 copy-start
  6.5 9.7 %sort.77.cloned.1.call-start = ((), (), s32[]{:S(2)}) async-start(), calls=%async_computation.12 | async-start | bytes 49184 | tf_op jit(solution)/shard_map/vmap(jit(argsort))/sort | solution.py:60
  36.4 0.7 copy-start.2
  57.7 48.7 %all-to-all-start = ((s32[8,32,12]{2,0,1:T(8,128)}), s32[8,32,12]{2,0,1:T(8,128)S(1)}, u32[]{:S(2)}, u32[]{:S(2)}) async-start(s32[8,32,12]{2,0,1:T(8,128)} %copy.96), calls=%async_computation | async-start | bytes 262144 | tf_op jit(solution)/shard_map/all_to_all | solution.py:228
  106.4 15.2 %all-to-all-start.1 = ((s32[8,32,12]{2,0,1:T(8,128)}), s32[8,32,12]{2,0,1:T(8,128)S(1)}, u32[]{:S(2)}, u32[]{:S(2)}) async-start(s32[8,32,12]{2,0,1:T(8,128)} %copy.103), calls=%async_computation.1 | async-start | bytes 262144 | tf_op jit(solution)/shard_map/all_to_all | solution.py:229
  113.8 26.2 %sort.79.cloned.1.call-start = ((), (), s32[]{:S(2)}) async-start(), calls=%async_computation.13 | async-start | bytes 73760 | tf_op jit(solution)/shard_map/vmap(jit(argsort))/sort | solution.py:60
  114.2 1.3 copy-start.9
  121.5 74.7 %all-to-all-start.2 = ((bf16[8,32,12,128]{3,0,2,1:T(8,128)(2,1)}), bf16[8,32,12,128]{3,0,2,1:T(8,128)(2,1)S(1)}, u32[]{:S(2)}, u32[]{:S(2)}) async-start(bf16[8,32,12,128]{3,0,2,1:T(8,128)(2,1)} %copy.110), calls=%async_computation.2 | async-start | bytes 1572864 | tf_op jit(solution)/shard_map/all_to_all | solution.py:226
  125.5 70.0 %sort.81.cloned.1.call-start = ((), (), s32[]{:S(2)}) async-start(), calls=%async_computation.14 | async-start | bytes 73760 | tf_op jit(solution)/shard_map/vmap(jit(argsort))/sort | solution.py:70
  166.1 29.4 %copy-start.10 = (s32[8,384]{1,0:T(8,128)S(1)}, s32[8,384]{1,0:T(8,128)}, u32[]{:S(2)}) copy-start(s32[8,384]{1,0:T(8,128)} %copy-done.9) | copy-start | bytes 36868
  196.2 67.2 %all-to-all-start.5 = ((bf16[8,32,12,128]{3,0,2,1:T(8,128)(2,1)}), bf16[8,32,12,128]{3,0,2,1:T(8,128)(2,1)}, u32[]{:S(2)}, u32[]{:S(2)}) async-start(bf16[8,32,12,128]{3,0,2,1:T(8,128)(2,1)} %copy.122), calls=%async_computation.5 | async-start | bytes 1572864 | tf_op jit(solution)/shard_map/all_to_all | solution.py:227
  225.6 308.3 %copy-start.5 = (bf16[4096,128]{1,0:T(8,128)(2,1)}, bf16[4096,128]{1,0:T(8,128)(2,1)S(1)}, u32[]{:S(2)}) copy-start(bf16[4096,128]{1,0:T(8,128)(2,1)S(1)} %gather_fusion.5) | copy-start | bytes 3145732
  229.9 2.0 copy-start.3
  263.5 71.4 %all-to-all-start.3 = ((bf16[8,32,12]{2,0,1:T(8,128)(2,1)}), bf16[8,32,12]{2,0,1:T(8,128)(2,1)S(1)}, u32[]{:S(2)}, u32[]{:S(2)}) async-start(bf16[8,32,12]{2,0,1:T(8,128)(2,1)} %copy.115), calls=%async_computation.3 | async-start | bytes 131072 | tf_op jit(solution)/shard_map/all_to_all | solution.py:217
  333.0 9.4 %copy-start.11 = (s32[2,4,256]{2,1,0:T(4,128)S(1)}, s32[2,4,256]{2,1,0:T(4,128)}, u32[]{:S(2)}) copy-start(s32[2,4,256]{2,1,0:T(4,128)} %param.7) | copy-start | bytes 24580
  334.8 31.8 %all-to-all-start.6 = ((bf16[8,32,12,128]{3,0,2,1:T(8,128)(2,1)}), bf16[8,32,12,128]{3,0,2,1:T(8,128)(2,1)S(1)}, u32[]{:S(2)}, u32[]{:S(2)}) async-start(bf16[8,32,12,128]{3,0,2,1:T(8,128)(2,1)} %copy.125), calls=%async_computation.6 | async-start | bytes 1572864 | tf_op jit(solution)/shard_map/all_to_all | solution.py:216
  342.3 10.2 %sort.83.cloned.1.call-start = ((), (), s32[]{:S(2)}) async-start(), calls=%async_computation.15 | async-start | bytes 49184 | tf_op jit(solution)/shard_map/vmap(jit(argsort))/sort | solution.py:70
  343.1 9.2 %copy-start.8 = (bf16[256,512]{1,0:T(8,128)(2,1)S(1)}, bf16[256,512]{1,0:T(8,128)(2,1)}, u32[]{:S(2)}) copy-start(bf16[256,512]{1,0:T(8,128)(2,1)} %param.6) | copy-start | bytes 786436
  366.7 0.9 copy-start.6
  423.7 14.9 %all-to-all-start.7 = ((bf16[8,32,12]{2,0,1:T(8,128)(2,1)}), bf16[8,32,12]{2,0,1:T(8,128)(2,1)S(1)}, u32[]{:S(2)}, u32[]{:S(2)}) async-start(bf16[8,32,12]{2,0,1:T(8,128)(2,1)} %copy.128), calls=%async_computation.7 | async-start | bytes 131072 | tf_op jit(solution)/shard_map/all_to_all | solution.py:231
  438.5 29.9 %all-to-all-start.4 = ((bf16[8,32,12,128]{3,0,2,1:T(8,128)(2,1)}), bf16[8,32,12,128]{3,0,2,1:T(8,128)(2,1)S(1)}, u32[]{:S(2)}, u32[]{:S(2)}) async-start(bf16[8,32,12,128]{3,0,2,1:T(8,128)(2,1)} %copy.119), calls=%async_computation.4 | async-start | bytes 1572864 | tf_op jit(solution)/shard_map/all_to_all | solution.py:230
  528.0 5.9 copy-start.4
  568.4 22.1 %all-to-all-start.8 = ((bf16[8,32,12,128]{3,0,2,1:T(8,128)(2,1)}), bf16[8,32,12,128]{3,0,2,1:T(8,128)(2,1)S(1)}, u32[]{:S(2)}, u32[]{:S(2)}) async-start(bf16[8,32,12,128]{3,0,2,1:T(8,128)(2,1)} %copy.132), calls=%async_computation.8 | async-start | bytes 1572864 | tf_op jit(solution)/shard_map/all_to_all | solution.py:248
  590.5 4.2 copy-start.7
  590.5 18.5 %all-to-all-start.9 = ((bf16[8,32,12,128]{3,0,2,1:T(8,128)(2,1)}), bf16[8,32,12,128]{3,0,2,1:T(8,128)(2,1)S(1)}, u32[]{:S(2)}, u32[]{:S(2)}) async-start(bf16[8,32,12,128]{3,0,2,1:T(8,128)(2,1)} %copy.135), calls=%async_computation.9 | async-start | bytes 1572864 | tf_op jit(solution)/shard_map/all_to_all | solution.py:249
  594.4 63.7 %reduce-scatter.2.cloned.1.call-start = ((), (), s32[]{:S(2)}) async-start(), calls=%async_computation.11 | async-start | bytes 2621440 | tf_op jit(solution)/shard_map/reduce_scatter | solution.py:253
  620.8 37.4 %copy-start.1 = (bf16[256,4096]{1,0:T(8,128)(2,1)S(1)}, bf16[256,4096]{1,0:T(8,128)(2,1)}, u32[]{:S(2)}) copy-start(bf16[256,4096]{1,0:T(8,128)(2,1)} %param.4) | copy-start | bytes 6291460
Sparse Core Ops, SparseCore 0:
  9.7 2.7 sort.85.cloned.1.call-done
  117.1 2.5 sort.87.cloned.1.call-done
  192.2 2.9 sort.89.cloned.1.call-done
  345.3 2.6 sort.91.cloned.1.call-done
  628.2 29.9 reduce-scatter.1
  (4 shorter events, 0.0 us)
where the time goes:
time: 676 us; the launch traced here: 665 us
  local copies, waits for them, and re-layouts  471 us (70%)
  starting transfers between devices  65.2 us (10%)
  waiting for transfers between devices  54.9 us (8%)
  matrix products  40.8 us (6%)
  other arithmetic  18.3 us (3%)
  between operations  14.7 us (2%)
    gather x20, local copies, waits for them, and re-layouts, pick_rows(): picked = source_rows[sources]  249 us
    gather x10, local copies, waits for them, and re-layouts, put_back(): return flattened[jnp.clip(positions, 0, flattened.shape[0] - 1)]  121 us
    gather x5, local copies, waits for them, and re-layouts, bucket_plan(): ordering[jnp.clip(starts[:, None] + slot_ids[None, :], 0, row_count - 1)]  46.5 us
    reduce_scatter x1, waiting for transfers between devices, per_device(): lax.psum_scatter(jnp.einsum('tcf,dcf->td', grads, weights, preferred_elem...  30.1 us
    gather x5, local copies, waits for them, and re-layouts, bucket_plan(): starts[jnp.clip(targets, 0, group_count - 1)]  22.6 us
    dot_general x3, matrix products, attend(): jnp.dot(query_half, unit_keys.T, preferred_element_type=jnp.float32)  16.2 us
  transfers between devices with their start and end apart: 11, of which 5 were waited for; matrix products, arithmetic and copies ran while one was open for 45% of the time, Pallas kernels for 0%

commit v1 on v0

v1 whole, which is shorter than its diff:
```python
import functools
import math

import jax
import jax.numpy as jnp
from jax import lax
from jax.experimental import pallas as pl
from jax.experimental.pallas import tpu as pltpu
from jax.sharding import PartitionSpec as P

HH = 4
RR = 2
TT = 256
HS = 128
NO = 32
CAP = 12
ROWS = NO * 24
SLOTS = NO * CAP
MAIN = NO * 8
ITEMS = HH * RR
SCALE = 1.0 / math.sqrt(HS)
SELF_SCORE = -100000.0
FAR = -(2.0**30)
F32 = jnp.float32
BF = jnp.bfloat16
VMEM = 40 * 1024 * 1024


def iota(shape, axis):
    return lax.broadcasted_iota(jnp.int32, shape, axis)


def dot(a, b, ca=1, cb=0, precision=None):
    return lax.dot_general(
        a, b, (((ca,), (cb,)), ((), ())), preferred_element_type=F32, precision=precision
    )


def halves(x):
    high = x.astype(BF)
    return high, (x - high.astype(F32)).astype(BF)


def slots_kernel(odd_ref, buckets_ref, rows_ref):
    odd = odd_ref[0]
    owners = lax.shift_right_logical(buckets_ref[...], 1)
    before = (iota((TT, TT), 0) < iota((TT, TT), 1)).astype(BF)
    for item in range(ITEMS):
        mine = owners[item : item + 1, :]
        hot = iota((NO, TT), 0) == mine
        counts = dot(hot.astype(BF), before)
        rank = jnp.sum(jnp.where(hot, counts, 0.0), axis=0, keepdims=True).astype(jnp.int32)
        first = item // HH
        late = 4 * odd if first == 0 else 4 - 4 * odd
        row = jnp.where(rank < 8, rank + 16 * first, rank + late)
        rows_ref[item : item + 1, :] = mine * 24 + row


def slot_rows(odd, buckets):
    return pl.pallas_call(
        slots_kernel,
        out_shape=jax.ShapeDtypeStruct((ITEMS, TT), jnp.int32),
        in_specs=[
            pl.BlockSpec(memory_space=pltpu.SMEM),
            pl.BlockSpec(memory_space=pltpu.VMEM),
        ],
        out_specs=pl.BlockSpec(memory_space=pltpu.VMEM),
        name="slots",
    )(odd, buckets)


WIRE = HH * 3 * HS + 128


def dispatch_kernel(rows_ref, buckets_ref, proj_ref, cot_ref, out_ref):
    row_ids = iota((ROWS, TT), 0)
    marks = jnp.zeros((ROWS, 128), F32)
    for h in range(HH):
        first = row_ids == rows_ref[h : h + 1, :]
        second = row_ids == rows_ref[HH + h : HH + h + 1, :]
        code0 = (1 + (buckets_ref[h : h + 1, :] & 1)).astype(F32)
        code1 = (1 + (buckets_ref[HH + h : HH + h + 1, :] & 1)).astype(F32)
        code = jnp.where(first, code0, jnp.where(second, code1, 0.0)).astype(BF)
        hot = (first | second).astype(BF)
        lanes = pl.ds(h * HS, HS)
        source = jnp.concatenate(
            [proj_ref[0, :, lanes], proj_ref[1, :, lanes], cot_ref[:, lanes]], axis=1
        )
        out_ref[:, pl.ds(h * 3 * HS, 3 * HS)] = dot(hot, source).astype(BF)
        marks += dot(code, (iota((TT, 128), 1) == h).astype(BF))
    out_ref[:, pl.ds(HH * 3 * HS, 128)] = marks.astype(BF)


def dispatch(rows, buckets, proj, cot):
    return pl.pallas_call(
        dispatch_kernel,
        out_shape=jax.ShapeDtypeStruct((ROWS, WIRE), BF),
        compiler_params=pltpu.CompilerParams(vmem_limit_bytes=VMEM),
        name="dispatch",
    )(rows, buckets, proj, cot)


def split_rounds(x):
    width = x.shape[1]
    x = x.reshape(NO, 3, 8, width)
    mixed = x[:, 1].reshape(NO // 2, 2, 8, width)
    even, odd = mixed[:, 0], mixed[:, 1]
    top = iota((NO // 2, 8, width), 1) < 4
    late0 = jnp.where(top, even, odd).reshape(SLOTS - MAIN, width)
    late1 = jnp.where(top, odd, even).reshape(SLOTS - MAIN, width)
    return (
        jnp.concatenate([x[:, 0].reshape(MAIN, width), late0], axis=0),
        jnp.concatenate([x[:, 2].reshape(MAIN, width), late1], axis=0),
    )


def join_rounds(x0, x1):
    width = x0.shape[1]
    late0 = x0[MAIN:].reshape(NO // 2, 8, width)
    late1 = x1[MAIN:].reshape(NO // 2, 8, width)
    top = iota((NO // 2, 8, width), 1) < 4
    even = jnp.where(top, late0, late1)
    odd = jnp.where(top, late1, late0)
    mixed = jnp.stack([even, odd], axis=1).reshape(NO, 1, 8, width)
    main0 = x0[:MAIN].reshape(NO, 1, 8, width)
    main1 = x1[:MAIN].reshape(NO, 1, 8, width)
    return jnp.concatenate([main0, mixed, main1], axis=1).reshape(ROWS, width)


def source_and_slot(shape, axis, which):
    row = iota(shape, axis)
    late = row - MAIN
    flip = ((late & 7) >= 4).astype(jnp.int32)
    source_late = 2 * lax.shift_right_arithmetic(late, 3) + (flip if which == 0 else 1 - flip)
    source = jnp.where(row < MAIN, lax.shift_right_logical(row, 3), source_late)
    slot = jnp.where(row < MAIN, row & 7, 8 + (late & 3))
    return source, slot


def forward_kernel(x_ref, marks_ref, probs_ref, rows_ref, self_ref, wire_ref, bias, spread):
    h = pl.program_id(0)

    @pl.when(h == 0)
    def _():
        for r in range(RR):
            source_i, slot_i = source_and_slot((SLOTS, SLOTS), 0, r)
            source_j, slot_j = source_and_slot((SLOTS, SLOTS), 1, r)
            earlier = source_j * CAP + slot_j < source_i * CAP + slot_i
            bias[r] = jnp.where(earlier, 0.0, FAR)
        spread[...] = jnp.zeros_like(spread)

    rounds = split_rounds(x_ref[...].astype(F32))
    marks = split_rounds(marks_ref[...].astype(F32))
    lane = iota((SLOTS, HS), 1)
    for r in range(RR):
        x = rounds[r].astype(BF)
        q = rounds[r][:, :HS]
        u = rounds[r][:, 2 * HS :]
        v_half = x[:, HS : 2 * HS]
        code = jnp.sum(jnp.where(lane == h, marks[r], 0.0), axis=1, keepdims=True)
        scale = lax.rsqrt(jnp.sum(q * q, axis=1, keepdims=True) + 1e-06)
        unit = (q * scale).astype(BF)
        in1 = (code == 1.0).astype(F32)
        in2 = (code == 2.0).astype(F32)
        far_q = jnp.where(lane == 0, FAR * in1, jnp.where(lane == 1, FAR * in2, 0.0))
        far_q = jnp.where(lane == 2, FAR * (1.0 - in1 - in2), far_q).astype(BF)
        far_k = jnp.where(lane == 0, 1.0 - in1, jnp.where(lane == 1, 1.0 - in2, 0.0))
        far_k = jnp.where(lane == 2, 1.0, far_k).astype(BF)
        scores = dot(
            jnp.concatenate([x[:, :HS], far_q], axis=1),
            jnp.concatenate([unit, far_k], axis=1),
            1,
            1,
        )
        scores = scores * SCALE + bias[r]
        top = jnp.maximum(jnp.max(scores, axis=1, keepdims=True), SELF_SCORE)
        shifted = jnp.exp(scores - top)
        own = jnp.exp(SELF_SCORE - top)
        totals = jnp.sum(shifted, axis=1, keepdims=True) + own
        inverse = 1.0 / totals
        probs = (shifted * inverse).astype(BF)
        own = (own * inverse).astype(BF).astype(F32)
        out = dot(probs, v_half) + own * rounds[r][:, HS : 2 * HS]
        out = out.astype(BF).astype(F32)
        inner = jnp.sum(u * out, axis=1, keepdims=True)
        lse = top + jnp.log(totals)
        probs_ref[0, r] = probs
        rows_ref[0, r] = x
        self_ref[0, r] = jnp.where(
            lane == 0, own, jnp.where(lane == 1, inner, jnp.where(lane == 2, scale, 0.0))
        )
        _, slot = source_and_slot((SLOTS, HS), 0, r)
        here = lane == slot + (r * HH + h) * CAP
        spread[r, :, :HS] += jnp.where(here, lse, 0.0)
        spread[r, :, HS:] += jnp.where(here, inner, 0.0)

    @pl.when(h == HH - 1)
    def _():
        total = jnp.zeros((NO, 2 * HS), F32)
        for r in range(RR):
            source, _ = source_and_slot((NO, SLOTS), 1, r)
            hot = (source == iota((NO, SLOTS), 0)).astype(F32)
            total += dot(hot, spread[r], precision=lax.Precision.HIGHEST)
        wire_ref[:, 0, :] = total[:, :HS]
        wire_ref[:, 1, :] = total[:, HS:]


def forward(received):
    return pl.pallas_call(
        forward_kernel,
        grid=(HH,),
        out_shape=(
            jax.ShapeDtypeStruct((HH, RR, SLOTS, SLOTS), BF),
            jax.ShapeDtypeStruct((HH, RR, SLOTS, 3 * HS), BF),
            jax.ShapeDtypeStruct((HH, RR, SLOTS, HS), F32),
            jax.ShapeDtypeStruct((NO, 2, HS), F32),
        ),
        in_specs=[
            pl.BlockSpec((ROWS, 3 * HS), lambda h: (0, h)),
            pl.BlockSpec((ROWS, 128), lambda h: (0, HH * 3)),
        ],
        out_specs=(
            pl.BlockSpec((1, RR, SLOTS, SLOTS), lambda h: (h, 0, 0, 0)),
            pl.BlockSpec((1, RR, SLOTS, 3 * HS), lambda h: (h, 0, 0, 0)),
            pl.BlockSpec((1, RR, SLOTS, HS), lambda h: (h, 0, 0, 0)),
            pl.BlockSpec((NO, 2, HS), lambda h: (0, 0, 0)),
        ),
        scratch_shapes=[
            pltpu.VMEM((RR, SLOTS, SLOTS), F32),
            pltpu.VMEM((RR, SLOTS, 2 * HS), F32),
        ],
        compiler_params=pltpu.CompilerParams(vmem_limit_bytes=VMEM),
        name="forward",
    )(received, received)


def between_kernel(probs_ref, rows_ref, self_ref, weighted_ref, first_ref, second_ref):
    for r in range(RR):
        probs = probs_ref[0, r]
        q = rows_ref[0, r, :, :HS]
        v = rows_ref[0, r, :, HS : 2 * HS]
        u = rows_ref[0, r, :, 2 * HS :]
        inner = self_ref[0, r, :, 1:2]
        scale = self_ref[0, r, :, 2:3]
        unit = (q.astype(F32) * scale).astype(BF)
        weighted = (probs.astype(F32) * (dot(u, v, 1, 1) - inner)).astype(BF)
        weighted_ref[0, r] = weighted
        first_ref[0, r] = dot(weighted, unit)
        second_ref[0, r] = dot(probs, unit)


def between(probs, rows, own):
    square = pl.BlockSpec((1, RR, SLOTS, SLOTS), lambda h: (h, 0, 0, 0))
    narrow = pl.BlockSpec((1, RR, SLOTS, HS), lambda h: (h, 0, 0, 0))
    wide = pl.BlockSpec((1, RR, SLOTS, 3 * HS), lambda h: (h, 0, 0, 0))
    flops = ITEMS * SLOTS * SLOTS * HS * 6
    return pl.pallas_call(
        between_kernel,
        grid=(HH,),
        out_shape=(
            jax.ShapeDtypeStruct((HH, RR, SLOTS, SLOTS), BF),
            jax.ShapeDtypeStruct((HH, RR, SLOTS, HS), F32),
            jax.ShapeDtypeStruct((HH, RR, SLOTS, HS), F32),
        ),
        in_specs=[square, wide, narrow],
        out_specs=(square, narrow, narrow),
        compiler_params=pltpu.CompilerParams(vmem_limit_bytes=VMEM),
        cost_estimate=pl.CostEstimate(flops=flops, bytes_accessed=12 << 20, transcendentals=0),
        name="between",
    )(probs, rows, own)


def shares_kernel(buckets_ref, got_ref, out_ref):
    got = jnp.concatenate([got_ref[:, 0, :], got_ref[:, 1, :]], axis=1)
    got_high, got_low = halves(got)
    got2 = jnp.concatenate([got_high, got_low], axis=0)
    owners = lax.shift_right_logical(buckets_ref[...], 1)
    before = (iota((TT, TT), 1) < iota((TT, TT), 0)).astype(BF)
    lane = iota((TT, HS), 1)
    total = jnp.zeros((NO, 2 * HS), F32)
    for h in range(HH):
        logs, inners, heres, hots = [], [], [], []
        for r in range(RR):
            item = r * HH + h
            hot = iota((TT, NO), 1) == owners[:, item : item + 1]
            counts = dot(before, hot.astype(BF))
            rank = jnp.sum(jnp.where(hot, counts, 0.0), axis=1, keepdims=True).astype(jnp.int32)
            hot = hot.astype(BF)
            seen = dot(jnp.concatenate([hot, hot], axis=1), got2)
            here = lane == rank + item * CAP
            logs.append(jnp.sum(jnp.where(here, seen[:, :HS], 0.0), axis=1, keepdims=True))
            inners.append(jnp.sum(jnp.where(here, seen[:, HS:], 0.0), axis=1, keepdims=True))
            heres.append(here)
            hots.append(hot)
        top = jnp.maximum(logs[0], logs[1])
        weights = [jnp.exp(logs[0] - top), jnp.exp(logs[1] - top)]
        inverse = 1.0 / (weights[0] + weights[1])
        share = [weights[0] * inverse, weights[1] * inverse]
        gap = inners[1] - inners[0]
        shift = [share[1] * gap, -share[0] * gap]
        for r in range(RR):
            back = jnp.concatenate(
                [jnp.where(heres[r], share[r], 0.0), jnp.where(heres[r], shift[r], 0.0)], axis=1
            )
            high, low = halves(back)
            total += dot(hots[r], high, 0, 0) + dot(hots[r], low, 0, 0)
    out_ref[:, 0, :] = total[:, :HS]
    out_ref[:, 1, :] = total[:, HS:]


def shares(buckets, got):
    return pl.pallas_call(
        shares_kernel,
        out_shape=jax.ShapeDtypeStruct((NO, 2, HS), F32),
        compiler_params=pltpu.CompilerParams(vmem_limit_bytes=VMEM),
        name="shares",
    )(buckets, got)


def backward_kernel(
    probs_ref, weighted_ref, rows_ref, self_ref, first_ref, second_ref, back_ref, out_ref
):
    h = pl.program_id(0)
    back = jnp.concatenate([back_ref[:, 0, :], back_ref[:, 1, :]], axis=1)
    high, low = halves(back)
    back2 = jnp.concatenate([high, low], axis=0)
    lane = iota((SLOTS, HS), 1)
    grads = []
    for r in range(RR):
        source, _ = source_and_slot((SLOTS, NO), 0, r)
        hot = (source == iota((SLOTS, NO), 1)).astype(BF)
        seen = dot(jnp.concatenate([hot, hot], axis=1), back2)
        _, slot = source_and_slot((SLOTS, HS), 0, r)
        here = lane == slot + (r * HH + h) * CAP
        share = jnp.sum(jnp.where(here, seen[:, :HS], 0.0), axis=1, keepdims=True)
        shift = jnp.sum(jnp.where(here, seen[:, HS:], 0.0), axis=1, keepdims=True)
        probs = probs_ref[0, r]
        weighted = weighted_ref[0, r]
        q = rows_ref[0, r, :, :HS].astype(F32)
        u = rows_ref[0, r, :, 2 * HS :].astype(F32)
        own = self_ref[0, r, :, 0:1]
        scale = self_ref[0, r, :, 2:3]
        q_share = share * q
        u_share = share * u
        right = jnp.concatenate([-shift * q_share, u_share], axis=1).astype(BF)
        both = dot(probs, right, 0, 0)
        unit_grad = (dot(weighted, q_share.astype(BF), 0, 0) + both[:, :HS]) * SCALE
        value_grad = both[:, HS:] + own * u_share
        along = jnp.sum(q * unit_grad, axis=1, keepdims=True)
        query_grad = share * (first_ref[0, r] - shift * second_ref[0, r]) * SCALE
        query_grad += scale * unit_grad - q * (scale * scale * scale * along)
        grads.append(jnp.concatenate([query_grad, value_grad], axis=1))
    out_ref[...] = join_rounds(grads[0], grads[1]).astype(BF)


def backward(probs, weighted, rows, own, first, second, back):
    square = pl.BlockSpec((1, RR, SLOTS, SLOTS), lambda h: (h, 0, 0, 0))
    narrow = pl.BlockSpec((1, RR, SLOTS, HS), lambda h: (h, 0, 0, 0))
    wide = pl.BlockSpec((1, RR, SLOTS, 3 * HS), lambda h: (h, 0, 0, 0))
    return pl.pallas_call(
        backward_kernel,
        grid=(HH,),
        out_shape=jax.ShapeDtypeStruct((ROWS, HH * 2 * HS), BF),
        in_specs=[
            square,
            square,
            wide,
            narrow,
            narrow,
            narrow,
            pl.BlockSpec((NO, 2, HS), lambda h: (0, 0, 0)),
        ],
        out_specs=pl.BlockSpec((ROWS, 2 * HS), lambda h: (0, h)),
        compiler_params=pltpu.CompilerParams(vmem_limit_bytes=VMEM),
        name="backward",
    )(probs, weighted, rows, own, first, second, back)


def collect_kernel(rows_ref, got_ref, out_ref):
    row_ids = iota((ROWS, TT), 0)
    for h in range(HH):
        first = row_ids == rows_ref[h : h + 1, :]
        second = row_ids == rows_ref[HH + h : HH + h + 1, :]
        hot = (first | second).astype(BF)
        sums = dot(hot, got_ref[:, pl.ds(h * 2 * HS, 2 * HS)], 0, 0).astype(BF)
        out_ref[0, :, pl.ds(h * HS, HS)] = sums[:, :HS]
        out_ref[1, :, pl.ds(h * HS, HS)] = sums[:, HS:]


def collect(rows, got):
    return pl.pallas_call(
        collect_kernel,
        out_shape=jax.ShapeDtypeStruct((2, TT, HH * HS), BF),
        compiler_params=pltpu.CompilerParams(vmem_limit_bytes=VMEM),
        name="collect",
    )(rows, got)


def exchange(x):
    return lax.all_to_all(x, "seq", split_axis=0, concat_axis=0, tiled=True)


def per_device(tokens, weights, cotangent, buckets):
    flat = buckets.reshape(ITEMS, TT)
    odd = (lax.axis_index("seq") % 2).astype(jnp.int32).reshape(1)
    rows = slot_rows(odd, flat)
    projected = jnp.einsum(
        "td,dcf->ctf", tokens, weights, preferred_element_type=jnp.float32
    ).astype(jnp.bfloat16)
    received = exchange(dispatch(rows, flat, projected, cotangent))
    probs, held, own, wire = forward(received)
    home = exchange(wire)
    weighted, first, second = between(probs, held, own)
    back = exchange(shares(flat.T, home))
    slot_grads = exchange(backward(probs, weighted, held, own, first, second, back))
    grads = collect(rows, slot_grads)
    return lax.psum_scatter(
        jnp.einsum("ctf,dcf->td", grads, weights, preferred_element_type=jnp.float32).astype(
            jnp.bfloat16
        ),
        "bkt",
        scatter_dimension=0,
        tiled=True,
    )


def solution(mesh):
    in_specs = (P("seq", None), P(None, None, "bkt"), P("seq", "bkt"), P(None, "bkt", "seq"))
    out_specs = P(("seq", "bkt"), None)
    return jax.shard_map(
        per_device, mesh=mesh, in_specs=in_specs, out_specs=out_specs, check_vma=False
    )
```

time: 676 us -> 194 us (0.29); the launches traced: 665 us -> 192 us
  local copies, waits for them, and re-layouts: 471 us -> 23.4 us
  blocking collectives: 0 us -> 71.7 us
  starting transfers between devices: 65.2 us -> 7.93 us
  matrix products: 40.8 us -> 12.8 us
  Pallas kernels: 0 us -> 27.8 us
  waiting for transfers between devices: 54.9 us -> 35 us
  other arithmetic: 18.3 us -> 0 us
    gather x40 -> x0, local copies, waits for them, and re-layouts: 439 us -> none  [the longest x20 249 us: pick_rows(): picked = source_rows[sources]]
    all_to_all x0 -> x2, blocking collectives: none -> 71.7 us  [exchange(): return lax.all_to_all(x, 'seq', split_axis=0, concat_axis=0, tiled=True)]
    all_to_all x10 -> x2, starting transfers between devices: 64.9 us -> 7.7 us  [exchange(): return lax.all_to_all(x, 'seq', split_axis=0, concat_axis=0, tiled=True)]
    dot_general x8 -> x2, matrix products: 40.8 us -> 12.8 us  [the longest x1 7.09 us: per_device(): jnp.einsum('ctf,dcf->td', grads, weights, preferred_element_type=jnp.floa...]
    pallas_call x0 -> x7, Pallas kernels: none -> 27.8 us  [the longest x1 9.2 us: backward(): pl.pallas_call(backward_kernel, grid=(HH,), out_shape=jax.ShapeDtypeStruc...]
    unnamed x33 -> x38, local copies, waits for them, and re-layouts: 1.46 us -> 21.8 us
    all_to_all x10 -> x2, waiting for transfers between devices: 24.8 us -> 7.28 us  [exchange(): return lax.all_to_all(x, 'seq', split_axis=0, concat_axis=0, tiled=True)]
    select_n x10 -> x0, local copies, waits for them, and re-layouts: 12.7 us -> none  [the longest x3 5.47 us: to_slots(): return jnp.where(keep_mask, picked, jnp.zeros((), picked.dtype))]
  transfers between devices with their start and end apart: 11 -> 3, of which waited for: 5 -> 2; matrix products, arithmetic and copies ran while one was open for 45% -> 0% of each run, Pallas kernels for 0% -> 2%
where the time goes in v1:
time: 194 us; the launch traced here: 192 us
  blocking collectives  71.7 us (37%)
  waiting for transfers between devices  35 us (18%)
  Pallas kernels  27.8 us (14%)
  local copies, waits for them, and re-layouts  23.4 us (12%)
  between operations  13.5 us (7%)
  matrix products  12.8 us (7%)
  starting transfers between devices  7.93 us (4%)
    all_to_all x2, blocking collectives, exchange(): return lax.all_to_all(x, 'seq', split_axis=0, concat_axis=0, tiled=True)  71.7 us
    reduce_scatter x1, waiting for transfers between devices, per_device(): lax.psum_scatter(jnp.einsum('ctf,dcf->td', grads, weights, preferred_elem...  27.7 us
    unnamed x38, local copies, waits for them, and re-layouts  21.8 us
    pallas_call x1, Pallas kernels, backward(): pl.pallas_call(backward_kernel, grid=(HH,), out_shape=jax.ShapeDtypeStruc...  9.2 us
    all_to_all x2, starting transfers between devices, exchange(): return lax.all_to_all(x, 'seq', split_axis=0, concat_axis=0, tiled=True)  7.7 us
    pallas_call x1, Pallas kernels, forward(): pl.pallas_call(forward_kernel, grid=(HH,), out_shape=(jax.ShapeDtypeStruc...  7.67 us
    all_to_all x2, waiting for transfers between devices, exchange(): return lax.all_to_all(x, 'seq', split_axis=0, concat_axis=0, tiled=True)  7.28 us
    dot_general x1, matrix products, per_device(): jnp.einsum('ctf,dcf->td', grads, weights, preferred_element_type=jnp.floa...  7.09 us
  transfers between devices with their start and end apart: 3, of which 2 were waited for; matrix products, arithmetic and copies ran while one was open for 0% of the time, Pallas kernels for 2%

profile of v1, /device:TPU:0, one launch (start us, length us, event | category | flops | bytes accessed | tf_op | source)
XLA Modules:
  0.0 192.1 jit_solution(15725281237681533386)
XLA Ops:
  6.5 0.0 copy-start
  6.5 1.5 reshape.11.buckets_ref
  8.0 1.6 slots.1.rows_ref
  9.6 0.0 copy-done
  9.6 0.0 copy-start.16
  9.6 0.0 copy-start.17
  9.6 0.0 copy-start.18
  9.6 5.8 %fusion.16.proj_ref = bf16[2,256,512]{2,1,0:T(8,128)(2,1)S(1)} fusion(bf16[4096,2,512]{2,1,0:T(2,128)(2,1)} %param.5, bf16[256,4096]{1,0:T(8,128)(2,1)S(1)} %copy-done), kind=kOutput, calls=%fused_computation.8 | convolution fusion | flops 2147745792 | bytes 11010048 | tf_op jit(solution)/shard_map/td,dcf->ctf/dot_general | solution.py:407
  15.4 0.0 copy-done.16
  15.4 0.0 copy-done.17
  15.4 0.0 copy-done.18
  15.4 1.8 dispatch.1
  17.2 41.5 %all_to_all.32 = bf16[32,24,1664]{2,1,0:T(8,128)(2,1)S(1)} all-to-all(bf16[32,24,1664]{2,1,0:T(8,128)(2,1)S(1)} %bitcast.22), channel_id=1, replica_groups=mesh['seq'=32,'bkt'=4] {'seq'}, dimensions={0} | all-to-all | bytes 5111808 | tf_op jit(solution)/shard_map/all_to_all | solution.py:400
  58.7 7.7 %forward.1 = (bf16[4,2,384,384]{3,2,1,0:T(8,128)(2,1)S(1)}, bf16[4,2,384,384]{3,2,1,0:T(8,128)(2,1)S(1)}, f32[4,2,384,128]{3,2,1,0:T(8,128)S(1)}, f32[32,2,128]{2,1,0:T(2,128)}) custom-call(bf16[768,1664]{1,0:T(8,128)(2,1)S(1)} %bitcast.20, bf16[768,1664]{1,0:T(8,128)(2,1)S(1)} %bitcast.21), custom_call_target="tpu_custom_call" | custom-call | tf_op jit(solution)/shard_map/forward/pallas_call | solution.py:209
  66.4 0.0 copy-start.1
  66.4 1.4 copy-done.1
  67.8 0.0 copy-start.4
  67.8 1.4 copy-done.4
  69.3 0.0 copy-start.7
  69.3 1.3 copy-done.7
  70.5 3.9 %all-to-all-start.1 = ((f32[32,2,128]{2,1,0:T(2,128)}), f32[32,2,128]{2,1,0:T(2,128)S(1)}, u32[]{:S(2)}, u32[]{:S(2)}) async-start(f32[32,2,128]{2,1,0:T(2,128)} %get-tuple-element.18), calls=%async_computation.1 | async-start | bytes 65536 | tf_op jit(solution)/shard_map/all_to_all | solution.py:400
  74.4 0.1 copy.13
  74.5 7.3 %all-to-all-done.1.got_ref = f32[32,2,128]{2,1,0:T(2,128)S(1)} async-done(((f32[32,2,128]{2,1,0:T(2,128)}), f32[32,2,128]{2,1,0:T(2,128)S(1)}, u32[]{:S(2)}, u32[]{:S(2)}) %all-to-all-start.1) | async-done | bytes 32800 | tf_op jit(solution)/shard_map/all_to_all | solution.py:400
  81.8 3.6 %shares.1 = f32[32,2,128]{2,1,0:T(2,128)} custom-call(s32[256,8]{1,0:T(8,128)S(1)} %bitcast.25, f32[32,2,128]{2,1,0:T(2,128)S(1)} %all-to-all-done.1.got_ref), custom_call_target="tpu_custom_call" | custom-call | tf_op jit(solution)/shard_map/shares/pallas_call | solution.py:312
  85.4 3.9 %all-to-all-start.2 = ((f32[32,2,128]{2,1,0:T(2,128)}), f32[32,2,128]{2,1,0:T(2,128)S(1)}, u32[]{:S(2)}, u32[]{:S(2)}) async-start(f32[32,2,128]{2,1,0:T(2,128)} %shares.1), calls=%async_computation.2 | async-start | bytes 65536 | tf_op jit(solution)/shard_map/all_to_all | solution.py:400
  89.2 0.2 reduce-scatter.2.cloned.1.call-start
  89.5 0.0 copy-start.2
  89.5 1.7 copy-done.2
  91.1 0.0 copy-start.5
  91.1 1.7 copy-done.5
  92.8 0.0 copy-start.8
  92.8 1.4 copy-done.8
  94.2 3.1 %between.1 = (bf16[4,2,384,384]{3,2,1,0:T(8,128)(2,1)S(1)}, f32[4,2,384,128]{3,2,1,0:T(8,128)S(1)}, f32[4,2,384,128]{3,2,1,0:T(8,128)S(1)}) custom-call(bf16[4,2,384,384]{3,2,1,0:T(8,128)(2,1)S(1)} %copy-done.2, bf16[4,2,384,384]{3,2,1,0:T(8,128)(2,1)S(1)} %copy-done.5, f32[4,2,384,128]{3,2,1,0:T(8,128)S(1)} %copy-done.8), custom_call_target="tpu_custom_call" | custom-call | flops 905969664 | bytes 12582912 | tf_op jit(solution)/shard_map/between/pallas_call | solution.py:257
  97.3 0.0 copy-start.10
  97.3 1.4 copy-done.10
  98.7 0.0 copy-start.12
  98.7 1.2 copy-done.12
  99.9 0.0 copy-start.14
  99.9 1.2 copy-done.14
  101.1 0.0 all-to-all-done.2.back_ref
  101.1 0.0 copy-start.3
  101.1 1.7 copy-done.3
  102.7 0.0 copy-start.6
  102.7 1.7 copy-done.6
  104.4 0.0 copy-start.9
  104.4 1.4 copy-done.9
  105.8 0.0 copy-start.11
  105.8 1.7 copy-done.11
  107.5 0.0 copy-start.13
  107.5 1.4 copy-done.13
  108.9 0.0 copy-start.15
  108.9 1.4 copy-done.15
  110.3 9.2 %backward.1 = bf16[768,1024]{1,0:T(8,128)(2,1)S(1)} custom-call(bf16[4,2,384,384]{3,2,1,0:T(8,128)(2,1)S(1)} %copy-done.3, bf16[4,2,384,384]{3,2,1,0:T(8,128)(2,1)S(1)} %copy-done.11, bf16[4,2,384,384]{3,2,1,0:T(8,128)(2,1)S(1)} %copy-done.6, f32[4,2,384,128]{3,2,1,0:T(8,128)S(1)} %copy-done.9, f32[4,2,384,128]{3,2,1,0:T(8,128)S(1)} %copy-done.13, ...), custom_call_target="tpu_custom_call" | custom-call | tf_op jit(solution)/shard_map/backward/pallas_call | solution.py:360
  119.5 30.2 %all_to_all.33 = bf16[32,24,1024]{2,1,0:T(8,128)(2,1)S(1)} all-to-all(bf16[32,24,1024]{2,1,0:T(8,128)(2,1)S(1)} %bitcast.23), channel_id=1, replica_groups=mesh['seq'=32,'bkt'=4] {'seq'}, dimensions={0} | all-to-all | bytes 3145728 | tf_op jit(solution)/shard_map/all_to_all | solution.py:400
  149.7 0.8 collect.1
  150.5 7.1 %fusion.7 = bf16[256,4096]{1,0:T(8,128)(2,1)} fusion(bf16[2,256,512]{2,1,0:T(8,128)(2,1)S(1)} %collect.1, bf16[4096,2,512]{2,1,0:T(2,128)(2,1)} %param.5), kind=kOutput, calls=%fused_computation.5 | convolution fusion | flops 2148532224 | bytes 11010048 | tf_op jit(solution)/shard_map/ctf,dcf->td/dot_general | solution.py:418
  157.6 0.0 reduce-scatter.2.cloned.1.call-update
  157.6 27.7 %reduce-scatter.2.cloned.1.call-done = bf16[64,4096]{1,0:T(8,128)(2,1)} async-done(((bf16[256,4096]{1,0:T(8,128)(2,1)}), bf16[64,4096]{1,0:T(8,128)(2,1)}) %reduce-scatter.2.cloned.1.call-update) | async-done | bytes 524304 | tf_op jit(solution)/shard_map/reduce_scatter | solution.py:417
Async XLA Ops:
  6.5 3.1 %copy-start = (bf16[256,4096]{1,0:T(8,128)(2,1)S(1)}, bf16[256,4096]{1,0:T(8,128)(2,1)}, u32[]{:S(2)}) copy-start(bf16[256,4096]{1,0:T(8,128)(2,1)} %param.4) | copy-start | bytes 6291460
  9.6 5.8 %copy-start.16 = (bf16[256,512]{1,0:T(8,128)(2,1)S(1)}, bf16[256,512]{1,0:T(8,128)(2,1)}, u32[]{:S(2)}) copy-start(bf16[256,512]{1,0:T(8,128)(2,1)} %cot_ref.1) | copy-start | bytes 786436
  9.6 5.8 %copy-start.17 = (s32[8,256]{1,0:T(8,128)S(1)}, s32[8,256]{1,0:T(8,128)}, u32[]{:S(2)}) copy-start(s32[8,256]{1,0:T(8,128)} %reshape.11.buckets_ref) | copy-start | bytes 24580
  9.6 5.8 %copy-start.18 = (s32[8,256]{1,0:T(8,128)S(1)}, s32[8,256]{1,0:T(8,128)}, u32[]{:S(2)}) copy-start(s32[8,256]{1,0:T(8,128)} %slots.1.rows_ref) | copy-start | bytes 24580
  66.4 1.4 copy-start.1
  67.8 1.4 copy-start.4
  69.3 1.3 copy-start.7
  70.5 11.3 %all-to-all-start.1 = ((f32[32,2,128]{2,1,0:T(2,128)}), f32[32,2,128]{2,1,0:T(2,128)S(1)}, u32[]{:S(2)}, u32[]{:S(2)}) async-start(f32[32,2,128]{2,1,0:T(2,128)} %get-tuple-element.18), calls=%async_computation.1 | async-start | bytes 65536 | tf_op jit(solution)/shard_map/all_to_all | solution.py:400
  85.4 15.7 %all-to-all-start.2 = ((f32[32,2,128]{2,1,0:T(2,128)}), f32[32,2,128]{2,1,0:T(2,128)S(1)}, u32[]{:S(2)}, u32[]{:S(2)}) async-start(f32[32,2,128]{2,1,0:T(2,128)} %shares.1), calls=%async_computation.2 | async-start | bytes 65536 | tf_op jit(solution)/shard_map/all_to_all | solution.py:400
  89.2 96.1 %reduce-scatter.2.cloned.1.call-start = ((), (), s32[]{:S(2)}) async-start(), calls=%async_computation.5 | async-start | bytes 2621440 | tf_op jit(solution)/shard_map/reduce_scatter | solution.py:417
  89.5 1.7 copy-start.2
  91.1 1.7 copy-start.5
  92.8 1.4 copy-start.8
  97.3 1.4 copy-start.10
  98.7 1.2 copy-start.12
  99.9 1.2 copy-start.14
  101.1 1.7 copy-start.3
  102.7 1.7 copy-start.6
  104.4 1.4 copy-start.9
  105.8 1.7 copy-start.11
  107.5 1.4 copy-start.13
  108.9 1.4 copy-start.15
Sparse Core Ops, SparseCore 0:
  157.8 27.4 reduce-scatter.1

commit v2 on v1

v2 whole, which is shorter than its diff:
```python
import functools
import math

import jax
import jax.numpy as jnp
from jax import lax
from jax.experimental import pallas as pl
from jax.experimental.pallas import tpu as pltpu
from jax.sharding import PartitionSpec as P

HH = 4
RR = 2
TT = 256
HS = 128
NO = 32
CAP = 12
ROWS = NO * 24
SLOTS = NO * CAP
MAIN = NO * 8
ITEMS = HH * RR
SCALE = 1.0 / math.sqrt(HS)
POWER = SCALE / math.log(2.0)
SELF_SCORE = -100000.0
FAR = -(2.0**30)
F32 = jnp.float32
BF = jnp.bfloat16
VMEM = 24 * 1024 * 1024


def iota(shape, axis):
    return lax.broadcasted_iota(jnp.int32, shape, axis)


def dot(a, b, ca=1, cb=0, precision=None):
    return lax.dot_general(
        a, b, (((ca,), (cb,)), ((), ())), preferred_element_type=F32, precision=precision
    )


def halves(x):
    high = x.astype(BF)
    return high, (x - high.astype(F32)).astype(BF)


WIRE = HH * 3 * HS + 128


def dispatch_kernel(odd_ref, buckets_ref, proj_ref, cot_ref, rows_ref, out_ref):
    odd = odd_ref[0]
    before = (iota((TT, TT), 0) < iota((TT, TT), 1)).astype(BF)
    owner_ids = iota((NO, TT), 0)
    row_ids = iota((ROWS, TT), 0)
    buckets = [buckets_ref[r, h : h + 1, :] for r in range(RR) for h in range(HH)]
    hots = [owner_ids == lax.shift_right_logical(mine, 1) for mine in buckets]
    counts = dot(jnp.concatenate([hot.astype(BF) for hot in hots], axis=0), before)
    rows = []
    for item in range(ITEMS):
        count = counts[item * NO : (item + 1) * NO]
        rank = jnp.sum(jnp.where(hots[item], count, 0.0), axis=0, keepdims=True)
        rank = rank.astype(jnp.int32)
        first = item // HH
        late = 4 * odd if first == 0 else 4 - 4 * odd
        row = jnp.where(rank < 8, rank + 16 * first, rank + late)
        rows.append(lax.shift_right_logical(buckets[item], 1) * 24 + row)
        rows_ref[item : item + 1, :] = rows[item]
    marks = jnp.zeros((ROWS, 128), F32)
    for h in range(HH):
        first = row_ids == rows[h]
        second = row_ids == rows[HH + h]
        code0 = (1 + (buckets[h] & 1)).astype(F32)
        code1 = (1 + (buckets[HH + h] & 1)).astype(F32)
        code = jnp.where(first, code0, jnp.where(second, code1, 0.0)).astype(BF)
        hot = (first | second).astype(BF)
        lanes = pl.ds(h * HS, HS)
        source = jnp.concatenate(
            [proj_ref[0, :, lanes], proj_ref[1, :, lanes], cot_ref[:, lanes]], axis=1
        )
        out_ref[:, pl.ds(h * 3 * HS, 3 * HS)] = dot(hot, source).astype(BF)
        marks += dot(code, (iota((TT, 128), 1) == h).astype(BF))
    out_ref[:, pl.ds(HH * 3 * HS, 128)] = marks.astype(BF)


def dispatch(odd, buckets, proj, cot):
    vmem = pl.BlockSpec(memory_space=pltpu.VMEM)
    return pl.pallas_call(
        dispatch_kernel,
        out_shape=(
            jax.ShapeDtypeStruct((ITEMS, TT), jnp.int32),
            jax.ShapeDtypeStruct((ROWS, WIRE), BF),
        ),
        in_specs=[pl.BlockSpec(memory_space=pltpu.SMEM), vmem, vmem, vmem],
        compiler_params=pltpu.CompilerParams(vmem_limit_bytes=VMEM),
        name="dispatch",
    )(odd, buckets, proj, cot)


def split_rounds(x):
    width = x.shape[1]
    x = x.reshape(NO, 3, 8, width)
    mixed = x[:, 1].reshape(NO // 2, 2, 8, width)
    even, odd = mixed[:, 0], mixed[:, 1]
    top = iota((NO // 2, 8, width), 1) < 4
    late0 = jnp.where(top, even, odd).reshape(SLOTS - MAIN, width)
    late1 = jnp.where(top, odd, even).reshape(SLOTS - MAIN, width)
    return (
        jnp.concatenate([x[:, 0].reshape(MAIN, width), late0], axis=0),
        jnp.concatenate([x[:, 2].reshape(MAIN, width), late1], axis=0),
    )


def join_rounds(x0, x1):
    width = x0.shape[1]
    late0 = x0[MAIN:].reshape(NO // 2, 8, width)
    late1 = x1[MAIN:].reshape(NO // 2, 8, width)
    top = iota((NO // 2, 8, width), 1) < 4
    even = jnp.where(top, late0, late1)
    odd = jnp.where(top, late1, late0)
    mixed = jnp.stack([even, odd], axis=1).reshape(NO, 1, 8, width)
    main0 = x0[:MAIN].reshape(NO, 1, 8, width)
    main1 = x1[:MAIN].reshape(NO, 1, 8, width)
    return jnp.concatenate([main0, mixed, main1], axis=1).reshape(ROWS, width)


def source_and_slot(shape, axis, which):
    row = iota(shape, axis)
    late = row - MAIN
    flip = ((late & 7) >= 4).astype(jnp.int32)
    source_late = 2 * lax.shift_right_arithmetic(late, 3) + (flip if which == 0 else 1 - flip)
    source = jnp.where(row < MAIN, lax.shift_right_logical(row, 3), source_late)
    slot = jnp.where(row < MAIN, row & 7, 8 + (late & 3))
    return source, slot


def forward_kernel(x_ref, marks_ref, probs_ref, rows_ref, self_ref, wire_ref, bias, spread):
    h = pl.program_id(0)

    @pl.when(h == 0)
    def _():
        for r in range(RR):
            source_i, slot_i = source_and_slot((SLOTS, 1), 0, r)
            source_j, slot_j = source_and_slot((1, SLOTS), 1, r)
            earlier = source_j * CAP + slot_j < source_i * CAP + slot_i
            bias[r] = jnp.where(earlier, 0.0, FAR)
        spread[...] = jnp.zeros_like(spread)

    rounds = split_rounds(x_ref[...].astype(F32))
    marks = split_rounds(marks_ref[...].astype(F32))
    lane = iota((SLOTS, HS), 1)
    for r in range(RR):
        x = rounds[r].astype(BF)
        q = rounds[r][:, :HS]
        u = rounds[r][:, 2 * HS :]
        v_half = x[:, HS : 2 * HS]
        code = jnp.sum(jnp.where(lane == h, marks[r], 0.0), axis=1, keepdims=True)
        scale = lax.rsqrt(jnp.sum(q * q, axis=1, keepdims=True) + 1e-06)
        unit = (q * scale).astype(BF)
        in1 = (code == 1.0).astype(F32)
        in2 = (code == 2.0).astype(F32)
        far_q = jnp.where(lane == 0, FAR * in1, jnp.where(lane == 1, FAR * in2, 0.0))
        far_q = jnp.where(lane == 2, FAR * (1.0 - in1 - in2), far_q).astype(BF)
        far_k = jnp.where(lane == 0, 1.0 - in1, jnp.where(lane == 1, 1.0 - in2, 0.0))
        far_k = jnp.where(lane == 2, 1.0, far_k).astype(BF)
        scores = dot(
            jnp.concatenate([x[:, :HS], far_q], axis=1),
            jnp.concatenate([unit, far_k], axis=1),
            1,
            1,
        )
        scores = scores + bias[r]
        top = jnp.maximum(jnp.max(scores, axis=1, keepdims=True), SELF_SCORE / SCALE)
        shifted = jnp.exp2(scores * POWER - top * POWER)
        own = jnp.exp2((SELF_SCORE / SCALE) * POWER - top * POWER)
        totals = jnp.sum(shifted, axis=1, keepdims=True) + own
        inverse = 1.0 / totals
        probs = (shifted * inverse).astype(BF)
        own = (own * inverse).astype(BF).astype(F32)
        out = dot(probs, v_half) + own * rounds[r][:, HS : 2 * HS]
        out = out.astype(BF).astype(F32)
        inner = jnp.sum(u * out, axis=1, keepdims=True)
        lse = top * SCALE + jnp.log(totals)
        probs_ref[0, r] = probs
        rows_ref[0, r] = x
        self_ref[0, r] = jnp.where(
            lane == 0, own, jnp.where(lane == 1, inner, jnp.where(lane == 2, scale, 0.0))
        )
        _, slot = source_and_slot((SLOTS, HS), 0, r)
        here = lane == slot + (r * HH + h) * CAP
        spread[r, :, :HS] += jnp.where(here, lse, 0.0)
        spread[r, :, HS:] += jnp.where(here, inner, 0.0)

    @pl.when(h == HH - 1)
    def _():
        total = jnp.zeros((NO, 2 * HS), F32)
        for r in range(RR):
            source, _ = source_and_slot((NO, SLOTS), 1, r)
            hot = (source == iota((NO, SLOTS), 0)).astype(BF)
            high, low = halves(spread[r])
            total += dot(hot, high) + dot(hot, low)
        wire_ref[:, 0, :] = total[:, :HS]
        wire_ref[:, 1, :] = total[:, HS:]


def forward(received):
    return pl.pallas_call(
        forward_kernel,
        grid=(HH,),
        out_shape=(
            pltpu.HBM((HH, RR, SLOTS, SLOTS), BF),
            pltpu.HBM((HH, RR, SLOTS, 3 * HS), BF),
            pltpu.HBM((HH, RR, SLOTS, HS), F32),
            jax.ShapeDtypeStruct((NO, 2, HS), F32),
        ),
        in_specs=[
            pl.BlockSpec((ROWS, 3 * HS), lambda h: (0, h)),
            pl.BlockSpec((ROWS, 128), lambda h: (0, 3 * HH)),
        ],
        out_specs=(
            pl.BlockSpec((1, RR, SLOTS, SLOTS), lambda h: (h, 0, 0, 0)),
            pl.BlockSpec((1, RR, SLOTS, 3 * HS), lambda h: (h, 0, 0, 0)),
            pl.BlockSpec((1, RR, SLOTS, HS), lambda h: (h, 0, 0, 0)),
            pl.BlockSpec((NO, 2, HS), lambda h: (0, 0, 0)),
        ),
        scratch_shapes=[
            pltpu.VMEM((RR, SLOTS, SLOTS), F32),
            pltpu.VMEM((RR, SLOTS, 2 * HS), F32),
        ],
        compiler_params=pltpu.CompilerParams(vmem_limit_bytes=VMEM),
        name="forward",
    )(received, received)


def between_kernel(probs_ref, rows_ref, self_ref, probs_t_ref, weighted_t_ref, sums_ref):
    for r in range(RR):
        probs = probs_ref[0, r]
        q = rows_ref[0, r, :, :HS]
        v = rows_ref[0, r, :, HS : 2 * HS]
        u = rows_ref[0, r, :, 2 * HS :]
        own = self_ref[0, r, :, 0:1]
        inner = self_ref[0, r, :, 1:2]
        scale = self_ref[0, r, :, 2:3]
        unit = (q.astype(F32) * scale).astype(BF)
        weighted = (probs.astype(F32) * (dot(u, v, 1, 1) - inner)).astype(BF)
        probs_t_ref[0, r] = probs.T
        weighted_t_ref[0, r] = weighted.T
        sums_ref[0, r, :, :HS] = dot(weighted, unit).astype(BF)
        sums_ref[0, r, :, HS : 2 * HS] = dot(probs, unit).astype(BF)
        sums_ref[0, r, :, 2 * HS :] = jnp.broadcast_to(own, (SLOTS, HS)).astype(BF)


SQUARE = pl.BlockSpec((1, RR, SLOTS, SLOTS), lambda h: (h, 0, 0, 0))
NARROW = pl.BlockSpec((1, RR, SLOTS, HS), lambda h: (h, 0, 0, 0))
WIDE = pl.BlockSpec((1, RR, SLOTS, 3 * HS), lambda h: (h, 0, 0, 0))


def between(probs, rows, own):
    flops = ITEMS * SLOTS * SLOTS * HS * 6
    return pl.pallas_call(
        between_kernel,
        grid=(HH,),
        out_shape=(
            pltpu.HBM((HH, RR, SLOTS, SLOTS), BF),
            pltpu.HBM((HH, RR, SLOTS, SLOTS), BF),
            pltpu.HBM((HH, RR, SLOTS, 3 * HS), BF),
        ),
        in_specs=[SQUARE, WIDE, NARROW],
        out_specs=(SQUARE, SQUARE, WIDE),
        compiler_params=pltpu.CompilerParams(vmem_limit_bytes=VMEM),
        cost_estimate=pl.CostEstimate(flops=flops, bytes_accessed=12 << 20, transcendentals=0),
        name="between",
    )(pinned(probs), pinned(rows), pinned(own))


def ranks_kernel(buckets_ref, out_ref):
    owners = lax.shift_right_logical(buckets_ref[...], 1)
    before = (iota((TT, TT), 1) < iota((TT, TT), 0)).astype(BF)
    hots = [iota((TT, NO), 1) == owners[:, item : item + 1] for item in range(ITEMS)]
    counts = dot(before, jnp.concatenate([hot.astype(BF) for hot in hots], axis=1))
    for item in range(ITEMS):
        count = counts[:, item * NO : (item + 1) * NO]
        rank = jnp.sum(jnp.where(hots[item], count, 0.0), axis=1, keepdims=True)
        out_ref[:, item : item + 1] = rank.astype(jnp.int32) + item * CAP


def ranks(buckets):
    return pl.pallas_call(
        ranks_kernel,
        out_shape=jax.ShapeDtypeStruct((TT, ITEMS), jnp.int32),
        compiler_params=pltpu.CompilerParams(vmem_limit_bytes=VMEM),
        name="ranks",
    )(buckets)


def shares_kernel(buckets_ref, columns_ref, ranks_ref, got_ref, out_ref):
    got = jnp.concatenate([got_ref[:, 0, :], got_ref[:, 1, :]], axis=1)
    got_high, got_low = halves(got)
    got2 = jnp.concatenate([got_high, got_low], axis=0)
    lane = iota((TT, HS), 1)
    lane2 = iota((TT, 2 * NO), 1) & (NO - 1)
    total = jnp.zeros((NO, 2 * HS), F32)
    for h in range(HH):
        logs, inners, heres = [], [], []
        for r in range(RR):
            item = r * HH + h
            owner = lax.shift_right_logical(columns_ref[:, item : item + 1], 1)
            seen = dot((lane2 == owner).astype(BF), got2)
            here = lane == ranks_ref[:, item : item + 1]
            logs.append(jnp.sum(jnp.where(here, seen[:, :HS], 0.0), axis=1, keepdims=True))
            inners.append(jnp.sum(jnp.where(here, seen[:, HS:], 0.0), axis=1, keepdims=True))
            heres.append(here)
        top = jnp.maximum(logs[0], logs[1])
        weights = [jnp.exp(logs[0] - top), jnp.exp(logs[1] - top)]
        inverse = 1.0 / (weights[0] + weights[1])
        share = [weights[0] * inverse, weights[1] * inverse]
        gap = inners[1] - inners[0]
        shift = [share[1] * gap, -share[0] * gap]
        for r in range(RR):
            owner = lax.shift_right_logical(buckets_ref[r, h : h + 1, :], 1)
            hot = (iota((NO, TT), 0) == owner).astype(BF)
            back = jnp.concatenate(
                [jnp.where(heres[r], share[r], 0.0), jnp.where(heres[r], shift[r], 0.0)], axis=1
            )
            high, low = halves(back)
            total += dot(
                jnp.concatenate([hot, hot], axis=1), jnp.concatenate([high, low], axis=0)
            )
    out_ref[:, 0, :] = total[:, :HS]
    out_ref[:, 1, :] = total[:, HS:]


def shares(buckets, columns, rank_columns, got):
    return pl.pallas_call(
        shares_kernel,
        out_shape=jax.ShapeDtypeStruct((NO, 2, HS), F32),
        compiler_params=pltpu.CompilerParams(vmem_limit_bytes=VMEM),
        name="shares",
    )(buckets, columns, rank_columns, got)


def backward_kernel(probs_ref, weighted_ref, q_ref, u_ref, sums_ref, back_ref, out_ref, seen):
    h = pl.program_id(0)

    @pl.when(h == 0)
    def _():
        back = jnp.concatenate([back_ref[:, 0, :], back_ref[:, 1, :]], axis=1)
        high, low = halves(back)
        back2 = jnp.concatenate([high, low], axis=0)
        lane2 = iota((SLOTS, 2 * NO), 1) & (NO - 1)
        for r in range(RR):
            source, _ = source_and_slot((SLOTS, 1), 0, r)
            seen[r] = dot((source == lane2).astype(BF), back2)

    lane = iota((SLOTS, HS), 1)
    grads = []
    for r in range(RR):
        _, slot = source_and_slot((SLOTS, 1), 0, r)
        here = lane == slot + (r * HH + h) * CAP
        share = jnp.sum(jnp.where(here, seen[r, :, :HS], 0.0), axis=1, keepdims=True)
        shift = jnp.sum(jnp.where(here, seen[r, :, HS:], 0.0), axis=1, keepdims=True)
        q = q_ref[0, r].astype(F32)
        u_share = share * u_ref[0, r].astype(F32)
        q_share = share * q
        right = jnp.concatenate([-shift * q_share, u_share], axis=1).astype(BF)
        both = dot(probs_ref[0, r], right)
        unit_grad = (dot(weighted_ref[0, r], q_share.astype(BF)) + both[:, :HS]) * SCALE
        value_grad = both[:, HS:] + sums_ref[0, r, :, 2 * HS :].astype(F32) * u_share
        scale = lax.rsqrt(jnp.sum(q * q, axis=1, keepdims=True) + 1e-06)
        along = jnp.sum(q * unit_grad, axis=1, keepdims=True)
        first = sums_ref[0, r, :, :HS].astype(F32)
        second = sums_ref[0, r, :, HS : 2 * HS].astype(F32)
        query_grad = (share * SCALE) * (first - shift * second)
        query_grad += scale * unit_grad - q * (scale * scale * scale * along)
        grads.append(jnp.concatenate([query_grad, value_grad], axis=1))
    out_ref[...] = join_rounds(grads[0], grads[1]).astype(BF)


def pinned(x):
    return pltpu.with_memory_space_constraint(x, pltpu.HBM)


def backward(probs, weighted, rows, sums, back):
    return pl.pallas_call(
        backward_kernel,
        grid=(HH,),
        out_shape=jax.ShapeDtypeStruct((ROWS, HH * 2 * HS), BF),
        in_specs=[
            SQUARE,
            SQUARE,
            pl.BlockSpec((1, RR, SLOTS, HS), lambda h: (h, 0, 0, 0)),
            pl.BlockSpec((1, RR, SLOTS, HS), lambda h: (h, 0, 0, 2)),
            WIDE,
            pl.BlockSpec((NO, 2, HS), lambda h: (0, 0, 0)),
        ],
        out_specs=pl.BlockSpec((ROWS, 2 * HS), lambda h: (0, h)),
        scratch_shapes=[pltpu.VMEM((RR, SLOTS, 2 * HS), F32)],
        compiler_params=pltpu.CompilerParams(vmem_limit_bytes=VMEM),
        name="backward",
    )(pinned(probs), pinned(weighted), pinned(rows), pinned(rows), pinned(sums), back)


def collect_kernel(rows_ref, got_ref, out_ref):
    row_ids = iota((ROWS, TT), 0)
    for h in range(HH):
        first = row_ids == rows_ref[h : h + 1, :]
        second = row_ids == rows_ref[HH + h : HH + h + 1, :]
        hot = (first | second).astype(BF)
        sums = dot(hot, got_ref[:, pl.ds(h * 2 * HS, 2 * HS)], 0, 0).astype(BF)
        out_ref[0, :, pl.ds(h * HS, HS)] = sums[:, :HS]
        out_ref[1, :, pl.ds(h * HS, HS)] = sums[:, HS:]


def collect(rows, got):
    return pl.pallas_call(
        collect_kernel,
        out_shape=jax.ShapeDtypeStruct((2, TT, HH * HS), BF),
        compiler_params=pltpu.CompilerParams(vmem_limit_bytes=VMEM),
        name="collect",
    )(rows, got)


def exchange(x):
    return lax.all_to_all(x, "seq", split_axis=0, concat_axis=0, tiled=True)


def block_order(me):
    return [me, me ^ 3, me ^ 1, me ^ 2]


def blocks_of(x, me):
    size = x.shape[1] // 4
    parts = [lax.dynamic_slice_in_dim(x, i * size, size, 1) for i in block_order(me)]
    return jnp.concatenate(parts, axis=1)


def swap(x, mask):
    return lax.ppermute(x, "bkt", [(i, i ^ mask) for i in range(4)])


def per_device(tokens, weights, cotangent, buckets):
    odd = (lax.axis_index("seq") & 1).astype(jnp.int32).reshape(1)
    me = lax.axis_index("bkt")
    projected = jnp.einsum(
        "td,dcf->ctf", tokens, weights, preferred_element_type=jnp.float32
    ).astype(jnp.bfloat16)
    rows, send = dispatch(odd, buckets, projected, cotangent)
    received = exchange(send)
    columns = buckets.reshape(ITEMS, TT).T
    rank_columns = ranks(columns)
    rows = blocks_of(rows, me)
    probs, held, own, wire = forward(received)
    home = exchange(wire)
    probs_t, weighted_t, sums = between(probs, held, own)
    back = exchange(shares(buckets, columns, rank_columns, home))
    slot_grads = exchange(backward(probs_t, weighted_t, held, sums, back))
    grads = collect(rows, slot_grads)
    half = weights.shape[0] // 2
    one, two = (
        jnp.einsum("ctf,dcf->td", grads, w, preferred_element_type=jnp.float32)
        .astype(jnp.bfloat16)
        .reshape(4, TT // 4, half)
        for w in (weights[:half], weights[half:])
    )
    got_one = swap(one[2:], 1)
    got_two = swap(jnp.stack([two[1], two[3]]), 3)
    sum_one = one[:2] + got_one
    sum_two = jnp.stack([two[0], two[2]]) + got_two
    out_one = sum_one[0] + swap(sum_one[1], 3)
    out_two = sum_two[0] + swap(sum_two[1], 1)
    return jnp.concatenate([out_one, out_two], axis=1)


def solution(mesh):
    in_specs = (P("seq", None), P(None, None, "bkt"), P("seq", "bkt"), P(None, "bkt", "seq"))
    out_specs = P(("seq", "bkt"), None)
    return jax.shard_map(
        per_device, mesh=mesh, in_specs=in_specs, out_specs=out_specs, check_vma=False
    )
```

time: 194 us -> 157 us (0.81)
  blocking collectives: 71.7 us -> 41.5 us
  between operations: 13.5 us -> 0.21 us
  local copies, waits for them, and re-layouts: 23.4 us -> 11.7 us
  starting transfers between devices: 7.93 us -> 19 us
  waiting for transfers between devices: 35 us -> 42.5 us
  Pallas kernels: 27.8 us -> 30.1 us
  matrix products: 12.8 us -> 10.7 us
    all_to_all x2 -> x1, blocking collectives: 71.7 us -> 41.5 us  [exchange(): return lax.all_to_all(x, 'seq', split_axis=0, concat_axis=0, tiled=True)]
    reduce_scatter x1 -> x0, waiting for transfers between devices: 27.7 us -> none  [per_device(): lax.psum_scatter(jnp.einsum('ctf,dcf->td', grads, weights, preferred_elem...]
    ppermute x0 -> x4, waiting for transfers between devices: none -> 21.4 us  [swap(): return lax.ppermute(x, 'bkt', [(i, i ^ mask) for i in range(4)])]
    unnamed x38 -> x10, local copies, waits for them, and re-layouts: 21.8 us -> 2.74 us
    all_to_all x2 -> x3, waiting for transfers between devices: 7.28 us -> 21.1 us  [exchange(): return lax.all_to_all(x, 'seq', split_axis=0, concat_axis=0, tiled=True)]
    slice x0 -> x3, local copies, waits for them, and re-layouts: none -> 8.68 us  [the longest x1 8.49 us: per_device(): weights[:half]]
    all_to_all x2 -> x3, starting transfers between devices: 7.7 us -> 15.2 us  [exchange(): return lax.all_to_all(x, 'seq', split_axis=0, concat_axis=0, tiled=True)]
    pallas_call x4, Pallas kernels: 14.2 us -> 18.9 us  [the longest x1 8.07 us: forward(): pl.pallas_call(forward_kernel, grid=(HH,), out_shape=(pltpu.HBM((HH, RR,...]
  transfers between devices with their start and end apart: 3 -> 7, of which waited for: 2 -> 6; matrix products, arithmetic and copies ran while one was open for 0% -> 7% of each run, Pallas kernels for 2% -> 6%
where the time goes in v2:
time: 157 us
  waiting for transfers between devices  42.5 us (27%)
  blocking collectives  41.5 us (26%)
  Pallas kernels  30.1 us (19%)
  starting transfers between devices  19 us (12%)
  local copies, waits for them, and re-layouts  11.7 us (7%)
  matrix products  10.7 us (7%)
    all_to_all x1, blocking collectives, exchange(): return lax.all_to_all(x, 'seq', split_axis=0, concat_axis=0, tiled=True)  41.5 us
    ppermute x4, waiting for transfers between devices, swap(): return lax.ppermute(x, 'bkt', [(i, i ^ mask) for i in range(4)])  21.4 us
    all_to_all x3, waiting for transfers between devices, exchange(): return lax.all_to_all(x, 'seq', split_axis=0, concat_axis=0, tiled=True)  21.1 us
    all_to_all x3, starting transfers between devices, exchange(): return lax.all_to_all(x, 'seq', split_axis=0, concat_axis=0, tiled=True)  15.2 us
    slice x1, local copies, waits for them, and re-layouts, per_device(): weights[:half]  8.49 us
    pallas_call x1, Pallas kernels, forward(): pl.pallas_call(forward_kernel, grid=(HH,), out_shape=(pltpu.HBM((HH, RR,...  8.07 us
    pallas_call x1, Pallas kernels, between(): pl.pallas_call(between_kernel, grid=(HH,), out_shape=(pltpu.HBM((HH, RR,...  7.27 us
    pallas_call x1, Pallas kernels, backward(): pl.pallas_call(backward_kernel, grid=(HH,), out_shape=jax.ShapeDtypeStruc...  6.01 us
  transfers between devices with their start and end apart: 7, of which 6 were waited for; matrix products, arithmetic and copies ran while one was open for 7% of the time, Pallas kernels for 6%

profile of v2, /device:TPU:0, one launch (start us, length us, event | category | flops | bytes accessed | tf_op | source)
XLA Modules:
  0.0 156.9 jit_solution(10952786210557918023)
XLA Ops:
  0.0 0.0 copy-start
  0.0 1.6 %copy-done = bf16[256,4096]{1,0:T(8,128)(2,1)S(1)} copy-done((bf16[256,4096]{1,0:T(8,128)(2,1)S(1)}, bf16[256,4096]{1,0:T(8,128)(2,1)}, u32[]{:S(2)}) %copy-start) | copy-done | bytes 2097176
  1.6 0.0 copy-start.2
  1.6 0.0 copy-start.3
  1.6 5.7 %fusion.24.proj_ref = bf16[2,256,512]{2,1,0:T(8,128)(2,1)S(1)} fusion(bf16[4096,2,512]{2,1,0:T(2,128)(2,1)} %param.5, bf16[256,4096]{1,0:T(8,128)(2,1)S(1)} %copy-done), kind=kOutput, calls=%fused_computation.12 | convolution fusion | flops 2147745792 | bytes 11010048 | tf_op jit(solution)/shard_map/td,dcf->ctf/dot_general | solution.py:441
  7.4 0.0 copy-done.2
  7.4 0.0 copy-done.3
  7.4 2.1 %dispatch.1 = (s32[8,256]{1,0:T(8,128)S(1)}, bf16[768,1664]{1,0:T(8,128)(2,1)S(1)}) custom-call(s32[1]{0:T(128)} %bitcast.odd_ref, s32[2,4,256]{2,1,0:T(4,128)S(1)} %copy-done.3, bf16[2,256,512]{2,1,0:T(8,128)(2,1)S(1)} %fusion.24.proj_ref, bf16[256,512]{1,0:T(8,128)(2,1)S(1)} %copy-done.2), custom_call_target="tpu_custom_call" | custom-call | tf_op jit(solution)/shard_map/dispatch/pallas_call | solution.py:85
  9.5 41.5 %all_to_all.32 = bf16[32,24,1664]{2,1,0:T(8,128)(2,1)S(1)} all-to-all(bf16[32,24,1664]{2,1,0:T(8,128)(2,1)S(1)} %bitcast.50), channel_id=1, replica_groups=mesh['seq'=32,'bkt'=4] {'seq'}, dimensions={0} | all-to-all | bytes 5111808 | tf_op jit(solution)/shard_map/all_to_all | solution.py:421
  51.0 8.1 %forward.1 = (bf16[4,2,384,384]{3,2,1,0:T(8,128)(2,1)}, bf16[4,2,384,384]{3,2,1,0:T(8,128)(2,1)}, f32[4,2,384,128]{3,2,1,0:T(8,128)}, f32[32,2,128]{2,1,0:T(2,128)}) custom-call(bf16[768,1664]{1,0:T(8,128)(2,1)S(1)} %bitcast.47, bf16[768,1664]{1,0:T(8,128)(2,1)S(1)} %bitcast.48), custom_call_target="tpu_custom_call" | custom-call | tf_op jit(solution)/shard_map/forward/pallas_call | solution.py:204
  59.1 3.9 %all-to-all-start.1 = ((f32[32,2,128]{2,1,0:T(2,128)}), f32[32,2,128]{2,1,0:T(2,128)S(1)}, u32[]{:S(2)}, u32[]{:S(2)}) async-start(f32[32,2,128]{2,1,0:T(2,128)} %get-tuple-element.22), calls=%async_computation.1 | async-start | bytes 65536 | tf_op jit(solution)/shard_map/all_to_all | solution.py:421
  63.0 0.1 copy.12
  63.1 1.4 ranks.1.ranks_ref
  64.5 5.8 %all-to-all-done.1.got_ref = f32[32,2,128]{2,1,0:T(2,128)S(1)} async-done(((f32[32,2,128]{2,1,0:T(2,128)}), f32[32,2,128]{2,1,0:T(2,128)S(1)}, u32[]{:S(2)}, u32[]{:S(2)}) %all-to-all-start.1) | async-done | bytes 32800 | tf_op jit(solution)/shard_map/all_to_all | solution.py:421
  70.4 2.9 %shares.1 = f32[32,2,128]{2,1,0:T(2,128)} custom-call(s32[2,4,256]{2,1,0:T(4,128)S(1)} %copy-done.3, s32[256,8]{1,0:T(8,128)S(1)} %bitcast.52, s32[256,8]{1,0:T(8,128)S(1)} %ranks.1.ranks_ref, f32[32,2,128]{2,1,0:T(2,128)S(1)} %all-to-all-done.1.got_ref), custom_call_target="tpu_custom_call" | custom-call | tf_op jit(solution)/shard_map/shares/pallas_call | solution.py:331
  73.3 4.0 %all-to-all-start.2 = ((f32[32,2,128]{2,1,0:T(2,128)}), f32[32,2,128]{2,1,0:T(2,128)S(1)}, u32[]{:S(2)}, u32[]{:S(2)}) async-start(f32[32,2,128]{2,1,0:T(2,128)} %shares.1), calls=%async_computation.2 | async-start | bytes 65536 | tf_op jit(solution)/shard_map/all_to_all | solution.py:421
  77.4 7.3 %between.1 = (bf16[4,2,384,384]{3,2,1,0:T(8,128)(2,1)}, bf16[4,2,384,384]{3,2,1,0:T(8,128)(2,1)}, bf16[4,2,384,384]{3,2,1,0:T(8,128)(2,1)}) custom-call(bf16[4,2,384,384]{3,2,1,0:T(8,128)(2,1)} %get-tuple-element.16.probs_ref, bf16[4,2,384,384]{3,2,1,0:T(8,128)(2,1)} %get-tuple-element.17.rows_ref.q_ref.u_ref, f32[4,2,384,128]{3,2,1,0:T(8,128)} %get-tuple-element.18.self_ref), custom_call_target="tpu_custom_call" | custom-call | flops 905969664 | bytes 12582912 | tf_op jit(solution)/shard_map/between/pallas_call | solution.py:257
  84.6 0.0 all-to-all-done.2.back_ref
  84.6 6.0 %backward.1 = bf16[768,1024]{1,0:T(8,128)(2,1)S(1)} custom-call(bf16[4,2,384,384]{3,2,1,0:T(8,128)(2,1)} %get-tuple-element.19.probs_ref, bf16[4,2,384,384]{3,2,1,0:T(8,128)(2,1)} %get-tuple-element.20.weighted_ref, bf16[4,2,384,384]{3,2,1,0:T(8,128)(2,1)} %get-tuple-element.17.rows_ref.q_ref.u_ref, ...), custom_call_target="tpu_custom_call" | custom-call | tf_op jit(solution)/shard_map/backward/pallas_call | solution.py:381
  90.7 0.0 copy-start.1
  90.7 1.1 copy-done.1
  91.8 7.3 %all-to-all-start.3 = ((bf16[32,24,1024]{2,1,0:T(8,128)(2,1)}), bf16[32,24,1024]{2,1,0:T(8,128)(2,1)}, u32[]{:S(2)}, u32[]{:S(2)}) async-start(bf16[32,24,1024]{2,1,0:T(8,128)(2,1)} %bitcast.49), calls=%async_computation.3 | async-start | bytes 3145728 | tf_op jit(solution)/shard_map/all_to_all | solution.py:421
  99.2 0.1 constant_dynamic-slice_fusion.3
  99.2 0.1 pad_add_fusion.rows_ref
  99.3 8.5 %fusion.31 = (bf16[2048,2,512]{2,1,0:T(2,128)(2,1)}, bf16[2048,2,512]{2,1,0:T(2,128)(2,1)}) fusion(bf16[4096,2,512]{2,1,0:T(2,128)(2,1)} %param.5), kind=kLoop, calls=%fused_computation.31 | loop fusion | bytes 16777216 | tf_op jit(solution)/shard_map/slice | solution.py:460
  107.8 15.2 %all-to-all-done.3 = bf16[32,24,1024]{2,1,0:T(8,128)(2,1)} async-done(((bf16[32,24,1024]{2,1,0:T(8,128)(2,1)}), bf16[32,24,1024]{2,1,0:T(8,128)(2,1)}, u32[]{:S(2)}, u32[]{:S(2)}) %all-to-all-start.3) | async-done | bytes 1572896 | tf_op jit(solution)/shard_map/all_to_all | solution.py:421
  123.1 2.2 %collect.1 = bf16[2,256,512]{2,1,0:T(8,128)(2,1)S(1)} custom-call(s32[8,256]{1,0:T(8,128)S(1)} %pad_add_fusion.rows_ref, bf16[768,1024]{1,0:T(8,128)(2,1)} %bitcast.7.got_ref), custom_call_target="tpu_custom_call" | custom-call | tf_op jit(solution)/shard_map/collect/pallas_call | solution.py:412
  125.3 0.0 copy-start.4
  125.3 3.6 %fusion.12 = bf16[256,2048]{1,0:T(8,128)(2,1)S(1)} fusion(bf16[2,256,512]{2,1,0:T(8,128)(2,1)S(1)} %collect.1, bf16[2048,2,512]{2,1,0:T(2,128)(2,1)} %get-tuple-element.24), kind=kOutput, calls=%fused_computation.8 | convolution fusion | flops 1074266112 | bytes 5767168 | tf_op jit(solution)/shard_map/ctf,dcf->td/dot_general | solution.py:457
  128.9 0.1 slice_bitcast_fusion.5
  129.0 0.1 pad_maximum_fusion
  129.1 3.1 %collective-permute-start.2 = (bf16[2,64,2048]{2,1,0:T(8,128)(2,1)S(1)}, bf16[2,64,2048]{2,1,0:T(8,128)(2,1)S(1)}, u32[]{:S(2)}, u32[]{:S(2)}) collective-permute-start(bf16[2,64,2048]{2,1,0:T(8,128)(2,1)S(1)} %pad_maximum_fusion), channel_id=1, source_target_pairs={{0,3},{1,2},{2,1},{3,0},{4,7},{5,6},{6,5},{7,4},{8,11},{9,10},{10,... | collective-permute-start | bytes 1572872 | tf_op jit(solution)/shard_map/ppermute | solution.py:435
  132.2 0.0 copy-done.4
  132.2 1.3 fusion.15
  133.5 0.1 fusion.32
  133.6 0.2 collective-permute-start
  133.8 9.0 %collective-permute-done.2 = bf16[2,64,2048]{2,1,0:T(8,128)(2,1)S(1)} collective-permute-done((bf16[2,64,2048]{2,1,0:T(8,128)(2,1)S(1)}, bf16[2,64,2048]{2,1,0:T(8,128)(2,1)S(1)}, u32[]{:S(2)}, u32[]{:S(2)}) %collective-permute-start.2) | collective-permute-done | bytes 524320 | tf_op jit(solution)/shard_map/ppermute | solution.py:435
  142.8 0.1 maximum_add_fusion
  142.9 0.4 collective-permute-start.3
  143.3 4.9 %collective-permute-done = bf16[2,64,2048]{2,1,0:T(8,128)(2,1)S(1)} collective-permute-done((bf16[2,64,2048]{2,1,0:T(8,128)(2,1)S(1)}, bf16[2,64,2048]{2,1,0:T(8,128)(2,1)S(1)}, u32[]{:S(2)}, u32[]{:S(2)}) %collective-permute-start) | collective-permute-done | bytes 524320 | tf_op jit(solution)/shard_map/ppermute | solution.py:435
  148.2 0.1 add.28
  148.3 0.1 collective-permute-start.1
  148.4 2.9 %collective-permute-done.3 = bf16[64,2048]{1,0:T(8,128)(2,1)S(1)} collective-permute-done((bf16[64,2048]{1,0:T(8,128)(2,1)S(1)}, bf16[64,2048]{1,0:T(8,128)(2,1)S(1)}, u32[]{:S(2)}, u32[]{:S(2)}) %collective-permute-start.3) | collective-permute-done | bytes 262176 | tf_op jit(solution)/shard_map/ppermute | solution.py:435
  151.4 4.6 %collective-permute-done.1 = bf16[64,2048]{1,0:T(8,128)(2,1)S(1)} collective-permute-done((bf16[64,2048]{1,0:T(8,128)(2,1)S(1)}, bf16[64,2048]{1,0:T(8,128)(2,1)S(1)}, u32[]{:S(2)}, u32[]{:S(2)}) %collective-permute-start.1) | collective-permute-done | bytes 262176 | tf_op jit(solution)/shard_map/ppermute | solution.py:435
  156.0 0.8 pad_maximum_fusion.1
  (5 shorter events, 0.1 us)
Async XLA Ops:
  0.0 1.6 %copy-start = (bf16[256,4096]{1,0:T(8,128)(2,1)S(1)}, bf16[256,4096]{1,0:T(8,128)(2,1)}, u32[]{:S(2)}) copy-start(bf16[256,4096]{1,0:T(8,128)(2,1)} %param.4) | copy-start | bytes 6291460
  1.6 5.8 %copy-start.2 = (bf16[256,512]{1,0:T(8,128)(2,1)S(1)}, bf16[256,512]{1,0:T(8,128)(2,1)}, u32[]{:S(2)}) copy-start(bf16[256,512]{1,0:T(8,128)(2,1)} %cot_ref.1) | copy-start | bytes 786436
  1.6 5.8 %copy-start.3 = (s32[2,4,256]{2,1,0:T(4,128)S(1)}, s32[2,4,256]{2,1,0:T(4,128)}, u32[]{:S(2)}) copy-start(s32[2,4,256]{2,1,0:T(4,128)} %buckets_ref.3) | copy-start | bytes 24580
  59.1 11.3 %all-to-all-start.1 = ((f32[32,2,128]{2,1,0:T(2,128)}), f32[32,2,128]{2,1,0:T(2,128)S(1)}, u32[]{:S(2)}, u32[]{:S(2)}) async-start(f32[32,2,128]{2,1,0:T(2,128)} %get-tuple-element.22), calls=%async_computation.1 | async-start | bytes 65536 | tf_op jit(solution)/shard_map/all_to_all | solution.py:421
  73.3 11.3 %all-to-all-start.2 = ((f32[32,2,128]{2,1,0:T(2,128)}), f32[32,2,128]{2,1,0:T(2,128)S(1)}, u32[]{:S(2)}, u32[]{:S(2)}) async-start(f32[32,2,128]{2,1,0:T(2,128)} %shares.1), calls=%async_computation.2 | async-start | bytes 65536 | tf_op jit(solution)/shard_map/all_to_all | solution.py:421
  90.7 1.1 copy-start.1
  91.8 31.3 %all-to-all-start.3 = ((bf16[32,24,1024]{2,1,0:T(8,128)(2,1)}), bf16[32,24,1024]{2,1,0:T(8,128)(2,1)}, u32[]{:S(2)}, u32[]{:S(2)}) async-start(bf16[32,24,1024]{2,1,0:T(8,128)(2,1)} %bitcast.49), calls=%async_computation.3 | async-start | bytes 3145728 | tf_op jit(solution)/shard_map/all_to_all | solution.py:421
  125.3 6.9 %copy-start.4 = (bf16[2048,2,512]{2,1,0:T(2,128)(2,1)S(1)}, bf16[2048,2,512]{2,1,0:T(2,128)(2,1)}, u32[]{:S(2)}) copy-start(bf16[2048,2,512]{2,1,0:T(2,128)(2,1)} %get-tuple-element.23) | copy-start | bytes 12582916
  129.1 13.7 %collective-permute-start.2 = (bf16[2,64,2048]{2,1,0:T(8,128)(2,1)S(1)}, bf16[2,64,2048]{2,1,0:T(8,128)(2,1)S(1)}, u32[]{:S(2)}, u32[]{:S(2)}) collective-permute-start(bf16[2,64,2048]{2,1,0:T(8,128)(2,1)S(1)} %pad_maximum_fusion), channel_id=1, source_target_pairs={{0,3},{1,2},{2,1},{3,0},{4,7},{5,6},{6,5},{7,4},{8,11},{9,10},{10,... | collective-permute-start | bytes 1572872 | tf_op jit(solution)/shard_map/ppermute | solution.py:435
  133.6 14.6 %collective-permute-start = (bf16[2,64,2048]{2,1,0:T(8,128)(2,1)S(1)}, bf16[2,64,2048]{2,1,0:T(8,128)(2,1)S(1)}, u32[]{:S(2)}, u32[]{:S(2)}) collective-permute-start(bf16[2,64,2048]{2,1,0:T(8,128)(2,1)S(1)} %bitcast.54), channel_id=1, source_target_pairs={{0,1},{1,0},{2,3},{3,2},{4,5},{5,4},{6,7},{7,6},{8,9},{9,8},{10,11... | collective-permute-start | bytes 1572872 | tf_op jit(solution)/shard_map/ppermute | solution.py:435
  142.9 8.5 %collective-permute-start.3 = (bf16[64,2048]{1,0:T(8,128)(2,1)S(1)}, bf16[64,2048]{1,0:T(8,128)(2,1)S(1)}, u32[]{:S(2)}, u32[]{:S(2)}) collective-permute-start(bf16[64,2048]{1,0:T(8,128)(2,1)S(1)} %slice_bitcast_fusion), channel_id=1, source_target_pairs={{0,1},{1,0},{2,3},{3,2},{4,5},{5,4},{6,7},{7,6},{8,9},{9,8},{10,11... | collective-permute-start | bytes 786440 | tf_op jit(solution)/shard_map/ppermute | solution.py:435
  148.3 7.7 %collective-permute-start.1 = (bf16[64,2048]{1,0:T(8,128)(2,1)S(1)}, bf16[64,2048]{1,0:T(8,128)(2,1)S(1)}, u32[]{:S(2)}, u32[]{:S(2)}) collective-permute-start(bf16[64,2048]{1,0:T(8,128)(2,1)S(1)} %slice_bitcast_fusion.6), channel_id=1, source_target_pairs={{0,3},{1,2},{2,1},{3,0},{4,7},{5,6},{6,5},{7,4},{8,11},{9,10},{10,... | collective-permute-start | bytes 786440 | tf_op jit(solution)/shard_map/ppermute | solution.py:435

commit v3 on v2

v3 whole, which is shorter than its diff:
```python
import functools
import math

import jax
import jax.numpy as jnp
from jax import lax
from jax.experimental import pallas as pl
from jax.experimental.pallas import tpu as pltpu
from jax.sharding import PartitionSpec as P

HH = 4
RR = 2
TT = 256
HS = 128
NO = 32
CAP = 12
ROWS = NO * 24
SLOTS = NO * CAP
MAIN = NO * 8
ITEMS = HH * RR
SCALE = 1.0 / math.sqrt(HS)
POWER = SCALE / math.log(2.0)
SELF_SCORE = -100000.0
FAR = -(2.0**30)
F32 = jnp.float32
BF = jnp.bfloat16
VMEM = 24 * 1024 * 1024


def iota(shape, axis):
    return lax.broadcasted_iota(jnp.int32, shape, axis)


def dot(a, b, ca=1, cb=0, precision=None):
    return lax.dot_general(
        a, b, (((ca,), (cb,)), ((), ())), preferred_element_type=F32, precision=precision
    )


def halves(x):
    high = x.astype(BF)
    return high, (x - high.astype(F32)).astype(BF)


WIRE = HH * 3 * HS + 128
OWNERS = 32
PLACES = 40
CODES = 64


def dispatch_kernel(odd_ref, buckets_ref, proj_ref, cot_ref, rows_ref, out_ref):
    odd = odd_ref[0]
    before = (iota((TT, TT), 0) < iota((TT, TT), 1)).astype(BF)
    owner_ids = iota((NO, TT), 0)
    row_ids = iota((ROWS, TT), 0)
    buckets = [buckets_ref[r, h : h + 1, :] for r in range(RR) for h in range(HH)]
    hots = [owner_ids == lax.shift_right_logical(mine, 1) for mine in buckets]
    counts = dot(jnp.concatenate([hot.astype(BF) for hot in hots], axis=0), before)
    rows, ranks = [], []
    for item in range(ITEMS):
        count = counts[item * NO : (item + 1) * NO]
        rank = jnp.sum(jnp.where(hots[item], count, 0.0), axis=0, keepdims=True)
        rank = rank.astype(jnp.int32)
        first = item // HH
        late = 4 * odd if first == 0 else 4 - 4 * odd
        row = jnp.where(rank < 8, rank + 16 * first, rank + late)
        rows.append(lax.shift_right_logical(buckets[item], 1) * 24 + row)
        ranks.append(rank)
        rows_ref[item : item + 1, :] = rows[item]
    code_ids = iota((128, TT), 0)
    marks = jnp.zeros((ROWS, 128), F32)
    for h in range(HH):
        first = (row_ids == rows[h]).astype(BF)
        second = (row_ids == rows[HH + h]).astype(BF)
        hot = first + second
        codes = []
        for item, other in ((h, HH + h), (HH + h, h)):
            code = jnp.where((code_ids >= CODES) & (code_ids & 7 == h), 1 + (buckets[item] & 1), 0)
            owner = lax.shift_right_logical(buckets[other], 1)
            code = jnp.where(code_ids == OWNERS + item, owner, code)
            codes.append(jnp.where(code_ids == PLACES + item, ranks[other], code))
        codes = jnp.concatenate(codes, axis=1).astype(F32).astype(BF)
        lanes = pl.ds(h * HS, HS)
        source = jnp.concatenate(
            [proj_ref[0, :, lanes], proj_ref[1, :, lanes], cot_ref[:, lanes]], axis=1
        )
        out_ref[:, pl.ds(h * 3 * HS, 3 * HS)] = dot(hot, source).astype(BF)
        marks += dot(jnp.concatenate([first, second], axis=1), codes, 1, 1)
    out_ref[:, pl.ds(HH * 3 * HS, 128)] = marks.astype(BF)


def dispatch(odd, buckets, proj, cot):
    vmem = pl.BlockSpec(memory_space=pltpu.VMEM)
    return pl.pallas_call(
        dispatch_kernel,
        out_shape=(
            jax.ShapeDtypeStruct((ITEMS, TT), jnp.int32),
            jax.ShapeDtypeStruct((ROWS, WIRE), BF),
        ),
        in_specs=[pl.BlockSpec(memory_space=pltpu.SMEM), vmem, vmem, vmem],
        compiler_params=pltpu.CompilerParams(vmem_limit_bytes=VMEM),
        name="dispatch",
    )(odd, buckets, proj, cot)


def split_rounds(x):
    width = x.shape[1]
    x = x.reshape(NO, 3, 8, width)
    mixed = x[:, 1].reshape(NO // 2, 2, 8, width)
    even, odd = mixed[:, 0], mixed[:, 1]
    top = iota((NO // 2, 8, width), 1) < 4
    late0 = jnp.where(top, even, odd).reshape(SLOTS - MAIN, width)
    late1 = jnp.where(top, odd, even).reshape(SLOTS - MAIN, width)
    return (
        jnp.concatenate([x[:, 0].reshape(MAIN, width), late0], axis=0),
        jnp.concatenate([x[:, 2].reshape(MAIN, width), late1], axis=0),
    )


def join_rounds(x0, x1):
    width = x0.shape[1]
    late0 = x0[MAIN:].reshape(NO // 2, 8, width)
    late1 = x1[MAIN:].reshape(NO // 2, 8, width)
    top = iota((NO // 2, 8, width), 1) < 4
    even = jnp.where(top, late0, late1)
    odd = jnp.where(top, late1, late0)
    mixed = jnp.stack([even, odd], axis=1).reshape(NO, 1, 8, width)
    main0 = x0[:MAIN].reshape(NO, 1, 8, width)
    main1 = x1[:MAIN].reshape(NO, 1, 8, width)
    return jnp.concatenate([main0, mixed, main1], axis=1).reshape(ROWS, width)


def source_and_slot(shape, axis, which):
    row = iota(shape, axis)
    late = row - MAIN
    flip = ((late & 7) >= 4).astype(jnp.int32)
    source_late = 2 * lax.shift_right_arithmetic(late, 3) + (flip if which == 0 else 1 - flip)
    source = jnp.where(row < MAIN, lax.shift_right_logical(row, 3), source_late)
    slot = jnp.where(row < MAIN, row & 7, 8 + (late & 3))
    return source, slot


def forward_kernel(
    x_ref, marks_ref, probs_ref, rows_ref, self_ref, wire_ref, mine_ref, bias, spread, far
):
    h = pl.program_id(0)
    lane = iota((SLOTS, HS), 1)

    @pl.when(h == 0)
    def _():
        for r in range(RR):
            source_i, slot_i = source_and_slot((SLOTS, 1), 0, r)
            source_j, slot_j = source_and_slot((1, SLOTS), 1, r)
            earlier = source_j * CAP + slot_j < source_i * CAP + slot_i
            bias[r] = jnp.where(earlier, 0.0, FAR)
        for r, marks in enumerate(split_rounds(marks_ref[...].astype(F32))):
            spread[r] = jnp.where((lane >= OWNERS) & (lane < CODES), marks, 0.0)
            group = lane & (HS - 8)
            wanted = jnp.where(group == CODES, 1.0, jnp.where(group == CODES + 8, 2.0, 0.0))
            coded = (group >= CODES) & (group < CODES + 24)
            far[r, :, :HS] = jnp.where(coded & (marks == wanted), FAR, 0.0).astype(BF)
            other = coded & ((marks != wanted) | (group == CODES + 16))
            far[r, :, HS:] = jnp.where(other, 1.0, 0.0).astype(BF)

    rounds = split_rounds(x_ref[...].astype(F32))
    head = ((lane & 7) == h).astype(BF)
    for r in range(RR):
        x = rounds[r].astype(BF)
        q = rounds[r][:, :HS]
        u = rounds[r][:, 2 * HS :]
        v_half = x[:, HS : 2 * HS]
        scale = lax.rsqrt(jnp.sum(q * q, axis=1, keepdims=True) + 1e-06)
        unit = (q * scale).astype(BF)
        far_q = far[r, :, :HS] * head
        far_k = far[r, :, HS:]
        scores = dot(
            jnp.concatenate([x[:, :HS], far_q], axis=1),
            jnp.concatenate([unit, far_k], axis=1),
            1,
            1,
        )
        scores = scores + bias[r]
        top = jnp.maximum(jnp.max(scores, axis=1, keepdims=True), SELF_SCORE / SCALE)
        shifted = jnp.exp2(scores * POWER - top * POWER)
        own = jnp.exp2((SELF_SCORE / SCALE) * POWER - top * POWER)
        totals = jnp.sum(shifted, axis=1, keepdims=True) + own
        inverse = 1.0 / totals
        probs = (shifted * inverse).astype(BF)
        own = (own * inverse).astype(BF).astype(F32)
        out = dot(probs, v_half) + own * rounds[r][:, HS : 2 * HS]
        out = out.astype(BF).astype(F32)
        inner = jnp.sum(u * out, axis=1, keepdims=True)
        lse = top * SCALE + jnp.log(totals)
        probs_ref[0, r] = probs
        rows_ref[0, r] = x
        kept = 0.0
        for at, column in enumerate((own, inner, scale)):
            kept = jnp.where(lane == at, column.astype(F32), kept)
        self_ref[0, r] = kept
        high, low = halves(lse)
        sent = 0.0
        for at, column in enumerate((high, low, inner.astype(BF))):
            sent = jnp.where(lane == (r * HH + h) * 3 + at, column.astype(F32), sent)
        spread[r] += sent

    @pl.when(h == HH - 1)
    def _():
        total = jnp.zeros((HS, SLOTS), F32)
        for r in range(RR):
            source, slot = source_and_slot((SLOTS, 1), 0, r)
            hot = (iota((SLOTS, SLOTS), 1) == slot * NO + source).astype(BF)
            total += dot(spread[r].astype(BF), hot, 0, 0)
        total = total.astype(BF)
        mine_ref[...] = total
        total = total[: 3 * ITEMS]
        for k in range(NO):
            wire_ref[pl.ds(k * 3 * ITEMS, 3 * ITEMS), :] = total


def forward(received):
    return pl.pallas_call(
        forward_kernel,
        grid=(HH,),
        out_shape=(
            pltpu.HBM((HH, RR, SLOTS, SLOTS), BF),
            pltpu.HBM((HH, RR, SLOTS, 3 * HS), BF),
            pltpu.HBM((HH, RR, SLOTS, HS), F32),
            jax.ShapeDtypeStruct((NO * 3 * ITEMS, SLOTS), BF),
            pltpu.HBM((HS, SLOTS), BF),
        ),
        in_specs=[
            pl.BlockSpec((ROWS, 3 * HS), lambda h: (0, h)),
            pl.BlockSpec((ROWS, 128), lambda h: (0, 3 * HH)),
        ],
        out_specs=(
            pl.BlockSpec((1, RR, SLOTS, SLOTS), lambda h: (h, 0, 0, 0)),
            pl.BlockSpec((1, RR, SLOTS, 3 * HS), lambda h: (h, 0, 0, 0)),
            pl.BlockSpec((1, RR, SLOTS, HS), lambda h: (h, 0, 0, 0)),
            pl.BlockSpec((NO * 3 * ITEMS, SLOTS), lambda h: (0, 0)),
            pl.BlockSpec((HS, SLOTS), lambda h: (0, 0)),
        ),
        scratch_shapes=[
            pltpu.VMEM((RR, SLOTS, SLOTS), F32),
            pltpu.VMEM((RR, SLOTS, HS), F32),
            pltpu.VMEM((RR, SLOTS, 2 * HS), BF),
        ],
        compiler_params=pltpu.CompilerParams(vmem_limit_bytes=VMEM),
        name="forward",
    )(received, received)


def between_kernel(probs_ref, rows_ref, self_ref, probs_t_ref, weighted_t_ref, sums_ref):
    for r in range(RR):
        probs = probs_ref[0, r]
        q = rows_ref[0, r, :, :HS]
        v = rows_ref[0, r, :, HS : 2 * HS]
        u = rows_ref[0, r, :, 2 * HS :]
        inner = self_ref[0, r, :, 1:2]
        scale = self_ref[0, r, :, 2:3]
        unit = (q.astype(F32) * scale).astype(BF)
        weighted = (probs.astype(F32) * (dot(u, v, 1, 1) - inner)).astype(BF)
        probs_t_ref[0, r] = probs.T
        weighted_t_ref[0, r] = weighted.T
        sums_ref[0, r, :, :HS] = dot(weighted, unit).astype(BF)
        sums_ref[0, r, :, HS : 2 * HS] = dot(probs, unit).astype(BF)
        own = self_ref[0, r, :, 0:1]
        sums_ref[0, r, :, 2 * HS :] = jnp.broadcast_to(own, (SLOTS, HS)).astype(BF)


SQUARE = pl.BlockSpec((1, RR, SLOTS, SLOTS), lambda h: (h, 0, 0, 0))
NARROW = pl.BlockSpec((1, RR, SLOTS, HS), lambda h: (h, 0, 0, 0))
WIDE = pl.BlockSpec((1, RR, SLOTS, 3 * HS), lambda h: (h, 0, 0, 0))


def between(probs, rows, own):
    flops = ITEMS * SLOTS * SLOTS * HS * 6
    return pl.pallas_call(
        between_kernel,
        grid=(HH,),
        out_shape=(
            pltpu.HBM((HH, RR, SLOTS, SLOTS), BF),
            pltpu.HBM((HH, RR, SLOTS, SLOTS), BF),
            pltpu.HBM((HH, RR, SLOTS, 3 * HS), BF),
        ),
        in_specs=[SQUARE, WIDE, NARROW],
        out_specs=(SQUARE, SQUARE, WIDE),
        compiler_params=pltpu.CompilerParams(vmem_limit_bytes=VMEM),
        cost_estimate=pl.CostEstimate(flops=flops, bytes_accessed=12 << 20, transcendentals=0),
        name="between",
    )(pinned(probs), pinned(rows), pinned(own))


def round_shares(mine_ref, got_ref, got, put):
    for at in range(SLOTS // HS):
        got[at] = got_ref[:, pl.ds(at * HS, HS)].astype(F32)
    mine = mine_ref[...].astype(F32)
    owner_ids = iota((NO, SLOTS), 0).astype(F32)
    slot_ids = iota((SLOTS, SLOTS), 0)
    source = iota((1, SLOTS), 1) & (NO - 1)
    mine_lse, mine_inner, other_lse, other_inner = [], [], [], []
    for item in range(ITEMS):
        first_row = (item ^ HH) * 3
        high, low, inners = (
            jnp.concatenate(
                [
                    got[i, pl.ds(first_row + at, NO, stride=3 * ITEMS), :]
                    for i in range(SLOTS // HS)
                ],
                axis=1,
            ).astype(BF)
            for at in range(3)
        )
        hot = (owner_ids == mine[OWNERS + item : OWNERS + item + 1]).astype(BF)
        place = mine[PLACES + item : PLACES + item + 1].astype(jnp.int32) * NO + source
        here = slot_ids == place
        table = jnp.concatenate([high, low], axis=0)
        logs = dot(table, jnp.concatenate([hot, hot], axis=0), 0, 0)
        inners = dot(inners, hot, 0, 0)
        other_lse.append(jnp.sum(jnp.where(here, logs, 0.0), axis=0, keepdims=True))
        other_inner.append(jnp.sum(jnp.where(here, inners, 0.0), axis=0, keepdims=True))
        mine_lse.append(mine[item * 3 : item * 3 + 1] + mine[item * 3 + 1 : item * 3 + 2])
        mine_inner.append(mine[item * 3 + 2 : item * 3 + 3])
    mine_lse, mine_inner, other_lse, other_inner = (
        jnp.concatenate(x, axis=0) for x in (mine_lse, mine_inner, other_lse, other_inner)
    )
    top = jnp.maximum(mine_lse, other_lse)
    share = jnp.exp(mine_lse - top)
    other_share = jnp.exp(other_lse - top)
    inverse = 1.0 / (share + other_share)
    share = share * inverse
    shift = other_share * inverse * (other_inner - mine_inner)
    high, low = halves(jnp.concatenate([share, shift], axis=0))
    both = jnp.concatenate([high, low], axis=1)
    for r in range(RR):
        source, slot = source_and_slot((SLOTS, 1), 0, r)
        hot = (iota((SLOTS, SLOTS), 1) == slot * NO + source).astype(BF)
        columns = dot(jnp.concatenate([hot, hot], axis=1), both, 1, 1)
        for h in range(HH):
            item = r * HH + h
            put[h, r, :, :HS] = jnp.broadcast_to(columns[:, item : item + 1], (SLOTS, HS))
            item += ITEMS
            put[h, r, :, HS:] = jnp.broadcast_to(columns[:, item : item + 1], (SLOTS, HS))


def backward_kernel(
    probs_ref, weighted_ref, q_ref, u_ref, sums_ref, mine_ref, got_ref, out_ref, got, put
):
    h = pl.program_id(0)

    @pl.when(h == 0)
    def _():
        round_shares(mine_ref, got_ref, got, put)

    grads = []
    for r in range(RR):
        share = put[h, r, :, :HS]
        shift = put[h, r, :, HS:]
        q = q_ref[0, r].astype(F32)
        u_share = share * u_ref[0, r].astype(F32)
        q_share = share * q
        right = jnp.concatenate([-shift * q_share, u_share], axis=1).astype(BF)
        both = dot(probs_ref[0, r], right)
        unit_grad = (dot(weighted_ref[0, r], q_share.astype(BF)) + both[:, :HS]) * SCALE
        value_grad = both[:, HS:] + sums_ref[0, r, :, 2 * HS :].astype(F32) * u_share
        scale = lax.rsqrt(jnp.sum(q * q, axis=1, keepdims=True) + 1e-06)
        along = jnp.sum(q * unit_grad, axis=1, keepdims=True)
        first = sums_ref[0, r, :, :HS].astype(F32)
        second = sums_ref[0, r, :, HS : 2 * HS].astype(F32)
        query_grad = (share * SCALE) * (first - shift * second)
        query_grad += scale * unit_grad - q * (scale * scale * scale * along)
        grads.append(jnp.concatenate([query_grad, value_grad], axis=1))
    out_ref[...] = join_rounds(grads[0], grads[1]).astype(BF)


def pinned(x):
    return pltpu.with_memory_space_constraint(x, pltpu.HBM)


def backward(probs, weighted, rows, sums, mine, got):
    return pl.pallas_call(
        backward_kernel,
        grid=(HH,),
        out_shape=pltpu.HBM((ROWS, HH * 2 * HS), BF),
        in_specs=[
            SQUARE,
            SQUARE,
            pl.BlockSpec((1, RR, SLOTS, HS), lambda h: (h, 0, 0, 0)),
            pl.BlockSpec((1, RR, SLOTS, HS), lambda h: (h, 0, 0, 2)),
            WIDE,
            pl.BlockSpec((HS, SLOTS), lambda h: (0, 0)),
            pl.BlockSpec((NO * 3 * ITEMS, SLOTS), lambda h: (0, 0)),
        ],
        out_specs=pl.BlockSpec((ROWS, 2 * HS), lambda h: (0, h)),
        scratch_shapes=[
            pltpu.VMEM((SLOTS // HS, NO * 3 * ITEMS, HS), F32),
            pltpu.VMEM((HH, RR, SLOTS, 2 * HS), F32),
        ],
        compiler_params=pltpu.CompilerParams(vmem_limit_bytes=VMEM),
        name="backward",
    )(pinned(probs), pinned(weighted), pinned(rows), pinned(rows), pinned(sums), pinned(mine), got)


def collect_kernel(rows_ref, got_ref, out_ref):
    row_ids = iota((ROWS, TT), 0)
    for h in range(HH):
        first = row_ids == rows_ref[h : h + 1, :]
        second = row_ids == rows_ref[HH + h : HH + h + 1, :]
        hot = (first | second).astype(BF)
        sums = dot(hot, got_ref[:, pl.ds(h * 2 * HS, 2 * HS)], 0, 0).astype(BF)
        out_ref[0, :, pl.ds(h * HS, HS)] = sums[:, :HS]
        out_ref[1, :, pl.ds(h * HS, HS)] = sums[:, HS:]


def collect(rows, got):
    return pl.pallas_call(
        collect_kernel,
        out_shape=jax.ShapeDtypeStruct((2, TT, HH * HS), BF),
        compiler_params=pltpu.CompilerParams(vmem_limit_bytes=VMEM),
        name="collect",
    )(rows, got)


def exchange(x):
    return lax.all_to_all(x, "seq", split_axis=0, concat_axis=0, tiled=True)


def block_order(me):
    return [me, me ^ 3, me ^ 1, me ^ 2]


def blocks_of(x, me):
    size = x.shape[1] // 4
    parts = [lax.dynamic_slice_in_dim(x, i * size, size, 1) for i in block_order(me)]
    return jnp.concatenate(parts, axis=1)


def swap(x, mask):
    return lax.ppermute(x, "bkt", [(i, i ^ mask) for i in range(4)])


PARTS = 4


def per_device(tokens, weights, cotangent, buckets):
    odd = (lax.axis_index("seq") & 1).astype(jnp.int32).reshape(1)
    me = lax.axis_index("bkt")
    projected = jnp.einsum(
        "td,dcf->ctf", tokens, weights, preferred_element_type=jnp.float32
    ).astype(jnp.bfloat16)
    rows, send = dispatch(odd, buckets, projected, cotangent)
    received = exchange(send)
    rows = blocks_of(rows, me)
    probs, held, own, wire, mine = forward(received)
    everyones = exchange(wire)
    probs_t, weighted_t, sums = between(probs, held, own)
    slot_grads = exchange(backward(probs_t, weighted_t, held, sums, mine, everyones))
    grads = collect(rows, slot_grads)
    width = weights.shape[0] // PARTS
    slabs = lax.optimization_barrier(
        [weights[i * width : (i + 1) * width].transpose(1, 0, 2) for i in range(PARTS)]
    )
    sums = []
    for i, slab in enumerate(slabs):
        part = jnp.einsum("ctf,cdf->td", grads, slab, preferred_element_type=jnp.float32)
        part = part.astype(jnp.bfloat16).reshape(4, TT // 4, width)
        if i % 2 == 0:
            sums.append(part[:2] + swap(part[2:], 1))
        else:
            sums.append(
                jnp.stack([part[0], part[2]]) + swap(jnp.stack([part[1], part[3]]), 3)
            )
    outs = [x[0] + swap(x[1], 3 if i % 2 == 0 else 1) for i, x in enumerate(sums)]
    return jnp.concatenate(outs, axis=1)


def solution(mesh):
    in_specs = (P("seq", None), P(None, None, "bkt"), P("seq", "bkt"), P(None, "bkt", "seq"))
    out_specs = P(("seq", "bkt"), None)
    return jax.shard_map(
        per_device, mesh=mesh, in_specs=in_specs, out_specs=out_specs, check_vma=False
    )
```

time: 157 us -> 143 us (0.911)
  waiting for transfers between devices: 42.5 us -> 29.8 us
  matrix products: 10.7 us -> 8.73 us
    ppermute x4 -> x8, waiting for transfers between devices: 21.4 us -> 10.2 us  [swap(): return lax.ppermute(x, 'bkt', [(i, i ^ mask) for i in range(4)])]
    transpose x0 -> x1, local copies, waits for them, and re-layouts: none -> 9.37 us  [per_device(): weights[i * width:(i + 1) * width].transpose(1, 0, 2)]
    slice x3 -> x4, local copies, waits for them, and re-layouts: 8.68 us -> 0.15 us  [the longest x2 0.07 us: per_device(): part[0]]
    ppermute x4 -> x8, starting transfers between devices: 3.77 us -> 10.6 us  [swap(): return lax.ppermute(x, 'bkt', [(i, i ^ mask) for i in range(4)])]
    all_to_all x3 -> x2, starting transfers between devices: 15.2 us -> 8.78 us  [exchange(): return lax.all_to_all(x, 'seq', split_axis=0, concat_axis=0, tiled=True)]
    dot_general x2 -> x4, matrix products: 4.91 us -> 2.98 us  [per_device(): jnp.einsum('ctf,cdf->td', grads, slab, preferred_element_type=jnp.float32)]
    all_to_all x3 -> x2, waiting for transfers between devices: 21.1 us -> 19.6 us  [exchange(): return lax.all_to_all(x, 'seq', split_axis=0, concat_axis=0, tiled=True)]
    pallas_call x3 -> x1, Pallas kernels: 10.4 us -> 9.94 us  [backward(): pl.pallas_call(backward_kernel, grid=(HH,), out_shape=pltpu.HBM((ROWS, HH...]
  transfers between devices with their start and end apart: 7 -> 10, of which waited for: 6 -> 6; matrix products, arithmetic and copies ran while one was open for 7% -> 9% of each run, Pallas kernels for 6% -> 5%
where the time goes in v3:
time: 143 us; the launch traced here: 142 us
  blocking collectives  41.5 us (29%)
  Pallas kernels  30.2 us (21%)
  waiting for transfers between devices  29.8 us (21%)
  starting transfers between devices  19.4 us (14%)
  local copies, waits for them, and re-layouts  11.2 us (8%)
  matrix products  8.73 us (6%)
    all_to_all x1, blocking collectives, exchange(): return lax.all_to_all(x, 'seq', split_axis=0, concat_axis=0, tiled=True)  41.5 us
    all_to_all x2, waiting for transfers between devices, exchange(): return lax.all_to_all(x, 'seq', split_axis=0, concat_axis=0, tiled=True)  19.6 us
    ppermute x8, starting transfers between devices, swap(): return lax.ppermute(x, 'bkt', [(i, i ^ mask) for i in range(4)])  10.6 us
    ppermute x8, waiting for transfers between devices, swap(): return lax.ppermute(x, 'bkt', [(i, i ^ mask) for i in range(4)])  10.2 us
    pallas_call x1, Pallas kernels, backward(): pl.pallas_call(backward_kernel, grid=(HH,), out_shape=pltpu.HBM((ROWS, HH...  9.94 us
    transpose x1, local copies, waits for them, and re-layouts, per_device(): weights[i * width:(i + 1) * width].transpose(1, 0, 2)  9.37 us
    all_to_all x2, starting transfers between devices, exchange(): return lax.all_to_all(x, 'seq', split_axis=0, concat_axis=0, tiled=True)  8.78 us
    pallas_call x1, Pallas kernels, forward(): pl.pallas_call(forward_kernel, grid=(HH,), out_shape=(pltpu.HBM((HH, RR,...  8.1 us
  transfers between devices with their start and end apart: 10, of which 6 were waited for; matrix products, arithmetic and copies ran while one was open for 9% of the time, Pallas kernels for 5%

profile of v3, /device:TPU:0, one launch (start us, length us, event | category | flops | bytes accessed | tf_op | source)
XLA Modules:
  0.0 142.4 jit_solution(17019038739490891010)
XLA Ops:
  0.0 0.0 copy-start
  0.0 1.6 %copy-done = bf16[256,4096]{1,0:T(8,128)(2,1)S(1)} copy-done((bf16[256,4096]{1,0:T(8,128)(2,1)S(1)}, bf16[256,4096]{1,0:T(8,128)(2,1)}, u32[]{:S(2)}) %copy-start) | copy-done | bytes 2097176
  1.6 0.0 copy-start.1
  1.6 0.0 copy-start.2
  1.6 5.7 %fusion.40.proj_ref = bf16[2,256,512]{2,1,0:T(8,128)(2,1)S(1)} fusion(bf16[4096,2,512]{2,1,0:T(2,128)(2,1)} %param.5, bf16[256,4096]{1,0:T(8,128)(2,1)S(1)} %copy-done), kind=kOutput, calls=%fused_computation.24 | convolution fusion | flops 2147745792 | bytes 11010048 | tf_op jit(solution)/shard_map/td,dcf->ctf/dot_general | solution.py:447
  7.4 0.0 copy-done.1
  7.4 0.0 copy-done.2
  7.4 2.5 %dispatch.1 = (s32[8,256]{1,0:T(8,128)S(1)}, bf16[768,1664]{1,0:T(8,128)(2,1)S(1)}) custom-call(s32[1]{0:T(128)} %bitcast.odd_ref, s32[2,4,256]{2,1,0:T(4,128)S(1)} %copy-done.2, bf16[2,256,512]{2,1,0:T(8,128)(2,1)S(1)} %fusion.40.proj_ref, bf16[256,512]{1,0:T(8,128)(2,1)S(1)} %copy-done.1), custom_call_target="tpu_custom_call" | custom-call | tf_op jit(solution)/shard_map/dispatch/pallas_call | solution.py:94
  9.8 41.5 %all_to_all.33 = bf16[32,24,1664]{2,1,0:T(8,128)(2,1)S(1)} all-to-all(bf16[32,24,1664]{2,1,0:T(8,128)(2,1)S(1)} %bitcast.90), channel_id=1, replica_groups=mesh['seq'=32,'bkt'=4] {'seq'}, dimensions={0} | all-to-all | bytes 5111808 | tf_op jit(solution)/shard_map/all_to_all | solution.py:424
  51.4 8.1 %forward.1 = (bf16[4,2,384,384]{3,2,1,0:T(8,128)(2,1)}, bf16[4,2,384,384]{3,2,1,0:T(8,128)(2,1)}, f32[4,2,384,128]{3,2,1,0:T(8,128)}, bf16[768,384]{1,0:T(8,128)(2,1)}, bf16[128,384]{1,0:T(8,128)(2,1)}) custom-call(bf16[768,1664]{1,0:T(8,128)(2,1)S(1)} %bitcast.88, bf16[768,1664]{1,0:T(8,128)(2,1)S(1)} %bitcast.89), custom_call_target="tpu_custom_call" | custom-call | tf_op jit(solution)/shard_map/forward/pallas_call | solution.py:221
  59.5 3.9 %all-to-all-start.1 = ((bf16[32,24,384]{2,1,0:T(8,128)(2,1)}), bf16[32,24,384]{2,1,0:T(8,128)(2,1)S(1)}, u32[]{:S(2)}, u32[]{:S(2)}) async-start(bf16[32,24,384]{2,1,0:T(8,128)(2,1)} %bitcast.5), calls=%async_computation.1 | async-start | bytes 1179648 | tf_op jit(solution)/shard_map/all_to_all | solution.py:424
  63.4 7.3 %between.1 = (bf16[4,2,384,384]{3,2,1,0:T(8,128)(2,1)}, bf16[4,2,384,384]{3,2,1,0:T(8,128)(2,1)}, bf16[4,2,384,384]{3,2,1,0:T(8,128)(2,1)}) custom-call(bf16[4,2,384,384]{3,2,1,0:T(8,128)(2,1)} %get-tuple-element.21.probs_ref, bf16[4,2,384,384]{3,2,1,0:T(8,128)(2,1)} %get-tuple-element.22.rows_ref.q_ref.u_ref, f32[4,2,384,128]{3,2,1,0:T(8,128)} %get-tuple-element.23.self_ref), custom_call_target="tpu_custom_call" | custom-call | flops 905969664 | bytes 12582912 | tf_op jit(solution)/shard_map/between/pallas_call | solution.py:277
  70.7 5.2 %all-to-all-done.1 = bf16[32,24,384]{2,1,0:T(8,128)(2,1)S(1)} async-done(((bf16[32,24,384]{2,1,0:T(8,128)(2,1)}), bf16[32,24,384]{2,1,0:T(8,128)(2,1)S(1)}, u32[]{:S(2)}, u32[]{:S(2)}) %all-to-all-start.1) | async-done | bytes 589856 | tf_op jit(solution)/shard_map/all_to_all | solution.py:424
  75.9 9.9 %backward.1 = bf16[768,1024]{1,0:T(8,128)(2,1)} custom-call(bf16[4,2,384,384]{3,2,1,0:T(8,128)(2,1)} %get-tuple-element.24.probs_ref, bf16[4,2,384,384]{3,2,1,0:T(8,128)(2,1)} %get-tuple-element.25.weighted_ref, bf16[4,2,384,384]{3,2,1,0:T(8,128)(2,1)} %get-tuple-element.22.rows_ref.q_ref.u_ref, ...), custom_call_target="tpu_custom_call" | custom-call | tf_op jit(solution)/shard_map/backward/pallas_call | solution.py:380
  85.8 4.9 %all-to-all-start.2 = ((bf16[32,24,1024]{2,1,0:T(8,128)(2,1)}), bf16[32,24,1024]{2,1,0:T(8,128)(2,1)}, u32[]{:S(2)}, u32[]{:S(2)}) async-start(bf16[32,24,1024]{2,1,0:T(8,128)(2,1)} %bitcast.92), calls=%async_computation.2 | async-start | bytes 3145728 | tf_op jit(solution)/shard_map/all_to_all | solution.py:424
  90.8 9.4 %slice_bitcast_fusion = (bf16[2,1024,512]{2,0,1:T(2,128)(2,1)}, bf16[2,1024,512]{2,0,1:T(2,128)(2,1)}, bf16[2,1024,512]{2,0,1:T(2,128)(2,1)}, bf16[2,1024,512]{2,0,1:T(2,128)(2,1)}) fusion(bf16[4096,2,512]{2,1,0:T(2,128)(2,1)} %param.5), kind=kLoop, calls=%fused_computation.11 | loop fusion | bytes 16777216 | tf_op jit(solution)/shard_map/transpose | solution.py:460
  100.1 0.1 constant_dynamic-slice_fusion.3
  100.2 0.1 pad_add_fusion.rows_ref
  100.3 14.4 %all-to-all-done.2 = bf16[32,24,1024]{2,1,0:T(8,128)(2,1)} async-done(((bf16[32,24,1024]{2,1,0:T(8,128)(2,1)}), bf16[32,24,1024]{2,1,0:T(8,128)(2,1)}, u32[]{:S(2)}, u32[]{:S(2)}) %all-to-all-start.2) | async-done | bytes 1572896 | tf_op jit(solution)/shard_map/all_to_all | solution.py:424
  114.7 0.0 copy-start.6
  114.7 2.4 %collect.1 = bf16[2,256,512]{2,1,0:T(8,128)(2,1)S(1)} custom-call(s32[8,256]{1,0:T(8,128)S(1)} %pad_add_fusion.rows_ref, bf16[768,1024]{1,0:T(8,128)(2,1)} %bitcast.8.got_ref), custom_call_target="tpu_custom_call" | custom-call | tf_op jit(solution)/shard_map/collect/pallas_call | solution.py:415
  117.0 0.0 copy-done.6
  117.0 0.0 copy-start.5
  117.1 0.7 fusion.37
  117.9 0.0 copy-start.4
  117.9 1.7 %collective-permute-start = (bf16[2,64,1024]{2,1,0:T(8,128)(2,1)S(1)}, bf16[2,64,1024]{2,1,0:T(8,128)(2,1)S(1)}, u32[]{:S(2)}, u32[]{:S(2)}) collective-permute-start(bf16[2,64,1024]{2,1,0:T(8,128)(2,1)S(1)} %bitcast.96), channel_id=1, source_target_pairs={{0,1},{1,0},{2,3},{3,2},{4,5},{5,4},{6,7},{7,6},{8,9},{9,8},{10,11... | collective-permute-start | bytes 786440 | tf_op jit(solution)/shard_map/ppermute | solution.py:438
  119.5 0.0 copy-done.5
  119.5 0.7 fusion.34
  120.4 0.0 copy-start.3
  120.4 2.2 %collective-permute-start.2 = (bf16[2,64,1024]{2,1,0:T(8,128)(2,1)S(1)}, bf16[2,64,1024]{2,1,0:T(8,128)(2,1)S(1)}, u32[]{:S(2)}, u32[]{:S(2)}) collective-permute-start(bf16[2,64,1024]{2,1,0:T(8,128)(2,1)S(1)} %pad_maximum_fusion.1), channel_id=1, source_target_pairs={{0,3},{1,2},{2,1},{3,0},{4,7},{5,6},{6,5},{7,4},{8,11},{9,10},{10,... | collective-permute-start | bytes 786440 | tf_op jit(solution)/shard_map/ppermute | solution.py:438
  122.6 0.0 copy-done.4
  122.6 0.7 fusion.31
  123.4 0.0 copy-done.3
  123.4 0.7 fusion.28
  124.3 1.1 collective-permute-start.6
  125.4 0.3 collective-permute-start.4
  125.8 0.0 collective-permute-done
  125.8 0.1 add.40
  125.8 2.0 %collective-permute-start.1 = (bf16[64,1024]{1,0:T(8,128)(2,1)S(1)}, bf16[64,1024]{1,0:T(8,128)(2,1)S(1)}, u32[]{:S(2)}, u32[]{:S(2)}) collective-permute-start(bf16[64,1024]{1,0:T(8,128)(2,1)S(1)} %slice_bitcast_fusion.18), channel_id=1, source_target_pairs={{0,3},{1,2},{2,1},{3,0},{4,7},{5,6},{6,5},{7,4},{8,11},{9,10},{10,... | collective-permute-start | bytes 393224 | tf_op jit(solution)/shard_map/ppermute | solution.py:438
  127.8 2.0 %collective-permute-done.2 = bf16[2,64,1024]{2,1,0:T(8,128)(2,1)S(1)} collective-permute-done((bf16[2,64,1024]{2,1,0:T(8,128)(2,1)S(1)}, bf16[2,64,1024]{2,1,0:T(8,128)(2,1)S(1)}, u32[]{:S(2)}, u32[]{:S(2)}) %collective-permute-start.2) | collective-permute-done | bytes 262176 | tf_op jit(solution)/shard_map/ppermute | solution.py:438
  129.9 0.7 collective-permute-start.3
  130.6 4.5 %collective-permute-done.6 = bf16[2,64,1024]{2,1,0:T(8,128)(2,1)S(1)} collective-permute-done((bf16[2,64,1024]{2,1,0:T(8,128)(2,1)S(1)}, bf16[2,64,1024]{2,1,0:T(8,128)(2,1)S(1)}, u32[]{:S(2)}, u32[]{:S(2)}) %collective-permute-start.6) | collective-permute-done | bytes 262176 | tf_op jit(solution)/shard_map/ppermute | solution.py:438
  135.1 0.1 collective-permute-start.7
  135.2 0.0 collective-permute-done.4
  135.2 0.1 add.44
  135.3 2.5 %collective-permute-start.5 = (bf16[64,1024]{1,0:T(8,128)(2,1)S(1)}, bf16[64,1024]{1,0:T(8,128)(2,1)S(1)}, u32[]{:S(2)}, u32[]{:S(2)}) collective-permute-start(bf16[64,1024]{1,0:T(8,128)(2,1)S(1)} %slice_bitcast_fusion.10), channel_id=1, source_target_pairs={{0,3},{1,2},{2,1},{3,0},{4,7},{5,6},{6,5},{7,4},{8,11},{9,10},{10,... | collective-permute-start | bytes 393224 | tf_op jit(solution)/shard_map/ppermute | solution.py:438
  137.8 0.0 collective-permute-done.1
  137.8 0.0 collective-permute-done.3
  137.8 2.3 %collective-permute-done.7 = bf16[64,1024]{1,0:T(8,128)(2,1)S(1)} collective-permute-done((bf16[64,1024]{1,0:T(8,128)(2,1)S(1)}, bf16[64,1024]{1,0:T(8,128)(2,1)S(1)}, u32[]{:S(2)}, u32[]{:S(2)}) %collective-permute-start.7) | collective-permute-done | bytes 131104 | tf_op jit(solution)/shard_map/ppermute | solution.py:438
  140.2 1.4 collective-permute-done.5
  141.6 0.8 pad_maximum_fusion
  (16 shorter events, 0.4 us)
Async XLA Ops:
  0.0 1.6 %copy-start = (bf16[256,4096]{1,0:T(8,128)(2,1)S(1)}, bf16[256,4096]{1,0:T(8,128)(2,1)}, u32[]{:S(2)}) copy-start(bf16[256,4096]{1,0:T(8,128)(2,1)} %param.4) | copy-start | bytes 6291460
  1.6 5.8 %copy-start.1 = (bf16[256,512]{1,0:T(8,128)(2,1)S(1)}, bf16[256,512]{1,0:T(8,128)(2,1)}, u32[]{:S(2)}) copy-start(bf16[256,512]{1,0:T(8,128)(2,1)} %cot_ref.1) | copy-start | bytes 786436
  1.6 5.8 %copy-start.2 = (s32[2,4,256]{2,1,0:T(4,128)S(1)}, s32[2,4,256]{2,1,0:T(4,128)}, u32[]{:S(2)}) copy-start(s32[2,4,256]{2,1,0:T(4,128)} %buckets_ref.1) | copy-start | bytes 24580
  59.5 16.4 %all-to-all-start.1 = ((bf16[32,24,384]{2,1,0:T(8,128)(2,1)}), bf16[32,24,384]{2,1,0:T(8,128)(2,1)S(1)}, u32[]{:S(2)}, u32[]{:S(2)}) async-start(bf16[32,24,384]{2,1,0:T(8,128)(2,1)} %bitcast.5), calls=%async_computation.1 | async-start | bytes 1179648 | tf_op jit(solution)/shard_map/all_to_all | solution.py:424
  85.8 28.8 %all-to-all-start.2 = ((bf16[32,24,1024]{2,1,0:T(8,128)(2,1)}), bf16[32,24,1024]{2,1,0:T(8,128)(2,1)}, u32[]{:S(2)}, u32[]{:S(2)}) async-start(bf16[32,24,1024]{2,1,0:T(8,128)(2,1)} %bitcast.92), calls=%async_computation.2 | async-start | bytes 3145728 | tf_op jit(solution)/shard_map/all_to_all | solution.py:424
  114.7 2.4 %copy-start.6 = (bf16[2,1024,512]{2,0,1:T(2,128)(2,1)S(1)}, bf16[2,1024,512]{2,0,1:T(2,128)(2,1)}, u32[]{:S(2)}) copy-start(bf16[2,1024,512]{2,0,1:T(2,128)(2,1)} %get-tuple-element.29) | copy-start | bytes 6291460
  117.0 2.5 %copy-start.5 = (bf16[2,1024,512]{2,0,1:T(2,128)(2,1)S(1)}, bf16[2,1024,512]{2,0,1:T(2,128)(2,1)}, u32[]{:S(2)}) copy-start(bf16[2,1024,512]{2,0,1:T(2,128)(2,1)} %get-tuple-element.30) | copy-start | bytes 6291460
  117.9 4.8 %copy-start.4 = (bf16[2,1024,512]{2,0,1:T(2,128)(2,1)S(1)}, bf16[2,1024,512]{2,0,1:T(2,128)(2,1)}, u32[]{:S(2)}) copy-start(bf16[2,1024,512]{2,0,1:T(2,128)(2,1)} %get-tuple-element.31) | copy-start | bytes 6291460
  117.9 7.9 %collective-permute-start = (bf16[2,64,1024]{2,1,0:T(8,128)(2,1)S(1)}, bf16[2,64,1024]{2,1,0:T(8,128)(2,1)S(1)}, u32[]{:S(2)}, u32[]{:S(2)}) collective-permute-start(bf16[2,64,1024]{2,1,0:T(8,128)(2,1)S(1)} %bitcast.96), channel_id=1, source_target_pairs={{0,1},{1,0},{2,3},{3,2},{4,5},{5,4},{6,7},{7,6},{8,9},{9,8},{10,11... | collective-permute-start | bytes 786440 | tf_op jit(solution)/shard_map/ppermute | solution.py:438
  120.4 3.0 %copy-start.3 = (bf16[2,1024,512]{2,0,1:T(2,128)(2,1)S(1)}, bf16[2,1024,512]{2,0,1:T(2,128)(2,1)}, u32[]{:S(2)}) copy-start(bf16[2,1024,512]{2,0,1:T(2,128)(2,1)} %get-tuple-element.32) | copy-start | bytes 6291460
  120.4 9.4 %collective-permute-start.2 = (bf16[2,64,1024]{2,1,0:T(8,128)(2,1)S(1)}, bf16[2,64,1024]{2,1,0:T(8,128)(2,1)S(1)}, u32[]{:S(2)}, u32[]{:S(2)}) collective-permute-start(bf16[2,64,1024]{2,1,0:T(8,128)(2,1)S(1)} %pad_maximum_fusion.1), channel_id=1, source_target_pairs={{0,3},{1,2},{2,1},{3,0},{4,7},{5,6},{6,5},{7,4},{8,11},{9,10},{10,... | collective-permute-start | bytes 786440 | tf_op jit(solution)/shard_map/ppermute | solution.py:438
  124.3 10.8 %collective-permute-start.6 = (bf16[2,64,1024]{2,1,0:T(8,128)(2,1)S(1)}, bf16[2,64,1024]{2,1,0:T(8,128)(2,1)S(1)}, u32[]{:S(2)}, u32[]{:S(2)}) collective-permute-start(bf16[2,64,1024]{2,1,0:T(8,128)(2,1)S(1)} %pad_maximum_fusion.2), channel_id=1, source_target_pairs={{0,3},{1,2},{2,1},{3,0},{4,7},{5,6},{6,5},{7,4},{8,11},{9,10},{10,... | collective-permute-start | bytes 786440 | tf_op jit(solution)/shard_map/ppermute | solution.py:438
  125.4 9.8 %collective-permute-start.4 = (bf16[2,64,1024]{2,1,0:T(8,128)(2,1)S(1)}, bf16[2,64,1024]{2,1,0:T(8,128)(2,1)S(1)}, u32[]{:S(2)}, u32[]{:S(2)}) collective-permute-start(bf16[2,64,1024]{2,1,0:T(8,128)(2,1)S(1)} %bitcast.95), channel_id=1, source_target_pairs={{0,1},{1,0},{2,3},{3,2},{4,5},{5,4},{6,7},{7,6},{8,9},{9,8},{10,11... | collective-permute-start | bytes 786440 | tf_op jit(solution)/shard_map/ppermute | solution.py:438
  125.8 11.9 %collective-permute-start.1 = (bf16[64,1024]{1,0:T(8,128)(2,1)S(1)}, bf16[64,1024]{1,0:T(8,128)(2,1)S(1)}, u32[]{:S(2)}, u32[]{:S(2)}) collective-permute-start(bf16[64,1024]{1,0:T(8,128)(2,1)S(1)} %slice_bitcast_fusion.18), channel_id=1, source_target_pairs={{0,3},{1,2},{2,1},{3,0},{4,7},{5,6},{6,5},{7,4},{8,11},{9,10},{10,... | collective-permute-start | bytes 393224 | tf_op jit(solution)/shard_map/ppermute | solution.py:438
  129.9 7.9 %collective-permute-start.3 = (bf16[64,1024]{1,0:T(8,128)(2,1)S(1)}, bf16[64,1024]{1,0:T(8,128)(2,1)S(1)}, u32[]{:S(2)}, u32[]{:S(2)}) collective-permute-start(bf16[64,1024]{1,0:T(8,128)(2,1)S(1)} %slice_bitcast_fusion.12), channel_id=1, source_target_pairs={{0,1},{1,0},{2,3},{3,2},{4,5},{5,4},{6,7},{7,6},{8,9},{9,8},{10,11... | collective-permute-start | bytes 393224 | tf_op jit(solution)/shard_map/ppermute | solution.py:438
  135.1 5.0 %collective-permute-start.7 = (bf16[64,1024]{1,0:T(8,128)(2,1)S(1)}, bf16[64,1024]{1,0:T(8,128)(2,1)S(1)}, u32[]{:S(2)}, u32[]{:S(2)}) collective-permute-start(bf16[64,1024]{1,0:T(8,128)(2,1)S(1)} %slice_bitcast_fusion.4), channel_id=1, source_target_pairs={{0,1},{1,0},{2,3},{3,2},{4,5},{5,4},{6,7},{7,6},{8,9},{9,8},{10,11... | collective-permute-start | bytes 393224 | tf_op jit(solution)/shard_map/ppermute | solution.py:438
  135.3 6.3 %collective-permute-start.5 = (bf16[64,1024]{1,0:T(8,128)(2,1)S(1)}, bf16[64,1024]{1,0:T(8,128)(2,1)S(1)}, u32[]{:S(2)}, u32[]{:S(2)}) collective-permute-start(bf16[64,1024]{1,0:T(8,128)(2,1)S(1)} %slice_bitcast_fusion.10), channel_id=1, source_target_pairs={{0,3},{1,2},{2,1},{3,0},{4,7},{5,6},{6,5},{7,4},{8,11},{9,10},{10,... | collective-permute-start | bytes 393224 | tf_op jit(solution)/shard_map/ppermute | solution.py:438

commit v4 on v3

--- a/solution.py
+++ b/solution.py
@@ -70,22 +70,21 @@
     code_ids = iota((128, TT), 0)
     marks = jnp.zeros((ROWS, 128), F32)
     for h in range(HH):
-        first = (row_ids == rows[h]).astype(BF)
-        second = (row_ids == rows[HH + h]).astype(BF)
-        hot = first + second
-        codes = []
+        hot = ((row_ids == rows[h]) | (row_ids == rows[HH + h])).astype(BF)
+        codes = 0
         for item, other in ((h, HH + h), (HH + h, h)):
-            code = jnp.where((code_ids >= CODES) & (code_ids & 7 == h), 1 + (buckets[item] & 1), 0)
+            bucket = 1 + (buckets[item] & 1)
+            codes = jnp.where((code_ids >= CODES) & (code_ids & 7 == item), bucket, codes)
             owner = lax.shift_right_logical(buckets[other], 1)
-            code = jnp.where(code_ids == OWNERS + item, owner, code)
-            codes.append(jnp.where(code_ids == PLACES + item, ranks[other], code))
-        codes = jnp.concatenate(codes, axis=1).astype(F32).astype(BF)
+            codes = jnp.where(code_ids == OWNERS + item, owner, codes)
+            codes = jnp.where(code_ids == PLACES + item, ranks[other], codes)
+        codes = codes.astype(F32).astype(BF)
         lanes = pl.ds(h * HS, HS)
         source = jnp.concatenate(
             [proj_ref[0, :, lanes], proj_ref[1, :, lanes], cot_ref[:, lanes]], axis=1
         )
         out_ref[:, pl.ds(h * 3 * HS, 3 * HS)] = dot(hot, source).astype(BF)
-        marks += dot(jnp.concatenate([first, second], axis=1), codes, 1, 1)
+        marks += dot(hot, codes, 1, 1)
     out_ref[:, pl.ds(HH * 3 * HS, 128)] = marks.astype(BF)
 
 
@@ -141,117 +140,136 @@
 
 
 def forward_kernel(
-    x_ref, marks_ref, probs_ref, rows_ref, self_ref, wire_ref, mine_ref, bias, spread, far
+    x_ref,
+    probs_ref,
+    rows_ref,
+    self_ref,
+    wire_ref,
+    mine_ref,
+    probs,
+    rows,
+    kept_all,
+    wire,
+    mine,
+    bias,
+    spread,
+    far,
+    sems,
 ):
-    h = pl.program_id(0)
     lane = iota((SLOTS, HS), 1)
-
-    @pl.when(h == 0)
-    def _():
+    for r in range(RR):
+        source_i, slot_i = source_and_slot((SLOTS, 1), 0, r)
+        source_j, slot_j = source_and_slot((1, SLOTS), 1, r)
+        earlier = source_j * CAP + slot_j < source_i * CAP + slot_i
+        bias[r] = jnp.where(earlier, 0.0, FAR)
+    for r, marks in enumerate(split_rounds(x_ref[:, pl.ds(3 * HH * HS, HS)].astype(F32))):
+        held = (lane >= OWNERS) & (lane < CODES) & ((lane & 7) >> 2 == r)
+        spread[r] = jnp.where(held, marks, 0.0)
+        group = lane & (HS - 8)
+        wanted = jnp.where(group == CODES, 1.0, jnp.where(group == CODES + 8, 2.0, 0.0))
+        coded = (group >= CODES) & (group < CODES + 24)
+        far[r, :, :HS] = jnp.where(coded & (marks == wanted), FAR, 0.0).astype(BF)
+        other = coded & ((marks != wanted) | (group == CODES + 16))
+        far[r, :, HS:] = jnp.where(other, 1.0, 0.0).astype(BF)
+
+    copies = []
+    for h in range(HH):
+        rounds = split_rounds(x_ref[:, pl.ds(h * 3 * HS, 3 * HS)].astype(F32))
         for r in range(RR):
-            source_i, slot_i = source_and_slot((SLOTS, 1), 0, r)
-            source_j, slot_j = source_and_slot((1, SLOTS), 1, r)
-            earlier = source_j * CAP + slot_j < source_i * CAP + slot_i
-            bias[r] = jnp.where(earlier, 0.0, FAR)
-        for r, marks in enumerate(split_rounds(marks_ref[...].astype(F32))):
-            spread[r] = jnp.where((lane >= OWNERS) & (lane < CODES), marks, 0.0)
-            group = lane & (HS - 8)
-            wanted = jnp.where(group == CODES, 1.0, jnp.where(group == CODES + 8, 2.0, 0.0))
-            coded = (group >= CODES) & (group < CODES + 24)
-            far[r, :, :HS] = jnp.where(coded & (marks == wanted), FAR, 0.0).astype(BF)
-            other = coded & ((marks != wanted) | (group == CODES + 16))
-            far[r, :, HS:] = jnp.where(other, 1.0, 0.0).astype(BF)
-
-    rounds = split_rounds(x_ref[...].astype(F32))
-    head = ((lane & 7) == h).astype(BF)
+            x = rounds[r].astype(BF)
+            q = rounds[r][:, :HS]
+            u = rounds[r][:, 2 * HS :]
+            v_half = x[:, HS : 2 * HS]
+            scale = lax.rsqrt(jnp.sum(q * q, axis=1, keepdims=True) + 1e-06)
+            unit = (q * scale).astype(BF)
+            far_q = far[r, :, :HS] * ((lane & 7) == r * HH + h).astype(BF)
+            far_k = far[r, :, HS:]
+            scores = dot(
+                jnp.concatenate([x[:, :HS], far_q], axis=1),
+                jnp.concatenate([unit, far_k], axis=1),
+                1,
+                1,
+            )
+            scores = scores + bias[r]
+            top = jnp.maximum(jnp.max(scores, axis=1, keepdims=True), SELF_SCORE / SCALE)
+            shifted = jnp.exp2((scores - top) * POWER).astype(BF)
+            own = jnp.exp2((SELF_SCORE / SCALE - top) * POWER)
+            both = dot(shifted, jnp.concatenate([v_half, jnp.ones_like(v_half)], axis=1))
+            totals = both[:, HS:] + own
+            inverse = 1.0 / totals
+            own = (own * inverse).astype(BF).astype(F32)
+            out = both[:, :HS] * inverse + own * rounds[r][:, HS : 2 * HS]
+            out = out.astype(BF).astype(F32)
+            inner = jnp.sum(u * out, axis=1, keepdims=True)
+            lse = top * SCALE + jnp.log(totals)
+            probs[h, r] = shifted
+            rows[h, r] = x
+            kept = 0.0
+            for at, column in enumerate((own, inner, scale, inverse)):
+                kept = jnp.where(lane == at, column.astype(F32), kept)
+            kept_all[h, r] = kept
+            at = lane - (r * HH + h) * 3
+            sent = jnp.where((at == 0) | (at == 1), lse, spread[r])
+            spread[r] = jnp.where(at == 2, inner, sent)
+        for at, (here, there) in enumerate(
+            ((probs, probs_ref), (rows, rows_ref), (kept_all, self_ref))
+        ):
+            copies.append(
+                pltpu.make_async_copy(here.at[h], there.at[h], sems.at[3 * h + at])
+            )
+            copies[-1].start()
+
+    total = jnp.zeros((HS, SLOTS), F32)
     for r in range(RR):
-        x = rounds[r].astype(BF)
-        q = rounds[r][:, :HS]
-        u = rounds[r][:, 2 * HS :]
-        v_half = x[:, HS : 2 * HS]
-        scale = lax.rsqrt(jnp.sum(q * q, axis=1, keepdims=True) + 1e-06)
-        unit = (q * scale).astype(BF)
-        far_q = far[r, :, :HS] * head
-        far_k = far[r, :, HS:]
-        scores = dot(
-            jnp.concatenate([x[:, :HS], far_q], axis=1),
-            jnp.concatenate([unit, far_k], axis=1),
-            1,
-            1,
-        )
-        scores = scores + bias[r]
-        top = jnp.maximum(jnp.max(scores, axis=1, keepdims=True), SELF_SCORE / SCALE)
-        shifted = jnp.exp2(scores * POWER - top * POWER)
-        own = jnp.exp2((SELF_SCORE / SCALE) * POWER - top * POWER)
-        totals = jnp.sum(shifted, axis=1, keepdims=True) + own
-        inverse = 1.0 / totals
-        probs = (shifted * inverse).astype(BF)
-        own = (own * inverse).astype(BF).astype(F32)
-        out = dot(probs, v_half) + own * rounds[r][:, HS : 2 * HS]
-        out = out.astype(BF).astype(F32)
-        inner = jnp.sum(u * out, axis=1, keepdims=True)
-        lse = top * SCALE + jnp.log(totals)
-        probs_ref[0, r] = probs
-        rows_ref[0, r] = x
-        kept = 0.0
-        for at, column in enumerate((own, inner, scale)):
-            kept = jnp.where(lane == at, column.astype(F32), kept)
-        self_ref[0, r] = kept
-        high, low = halves(lse)
-        sent = 0.0
-        for at, column in enumerate((high, low, inner.astype(BF))):
-            sent = jnp.where(lane == (r * HH + h) * 3 + at, column.astype(F32), sent)
-        spread[r] += sent
-
-    @pl.when(h == HH - 1)
-    def _():
-        total = jnp.zeros((HS, SLOTS), F32)
-        for r in range(RR):
-            source, slot = source_and_slot((SLOTS, 1), 0, r)
-            hot = (iota((SLOTS, SLOTS), 1) == slot * NO + source).astype(BF)
-            total += dot(spread[r].astype(BF), hot, 0, 0)
-        total = total.astype(BF)
-        mine_ref[...] = total
-        total = total[: 3 * ITEMS]
-        for k in range(NO):
-            wire_ref[pl.ds(k * 3 * ITEMS, 3 * ITEMS), :] = total
+        source, slot = source_and_slot((SLOTS, 1), 0, r)
+        hot = (iota((SLOTS, SLOTS), 1) == slot * NO + source).astype(BF)
+        high, low = halves(spread[r])
+        low_lane = (lane < 3 * ITEMS) & (lane % 3 == 1)
+        sent = jnp.where(low_lane, low.astype(F32), high.astype(F32)).astype(BF)
+        total += dot(sent, hot, 0, 0)
+    total = total.astype(BF)
+    mine[...] = total
+    total = total[: 3 * ITEMS]
+    for k in range(NO):
+        wire[pl.ds(k * 3 * ITEMS, 3 * ITEMS), :] = total
+    copies += [
+        pltpu.make_async_copy(mine, mine_ref, sems.at[3 * HH]),
+        pltpu.make_async_copy(wire, wire_ref, sems.at[3 * HH + 1]),
+    ]
+    copies[-1].start()
+    copies[-2].start()
+    for copy in copies:
+        copy.wait()
 
 
 def forward(received):
+    shapes = (
+        ((HH, RR, SLOTS, SLOTS), BF),
+        ((HH, RR, SLOTS, 3 * HS), BF),
+        ((HH, RR, SLOTS, HS), F32),
+        ((NO * 3 * ITEMS, SLOTS), BF),
+        ((HS, SLOTS), BF),
+    )
     return pl.pallas_call(
         forward_kernel,
-        grid=(HH,),
-        out_shape=(
-            pltpu.HBM((HH, RR, SLOTS, SLOTS), BF),
-            pltpu.HBM((HH, RR, SLOTS, 3 * HS), BF),
-            pltpu.HBM((HH, RR, SLOTS, HS), F32),
-            jax.ShapeDtypeStruct((NO * 3 * ITEMS, SLOTS), BF),
-            pltpu.HBM((HS, SLOTS), BF),
-        ),
-        in_specs=[
-            pl.BlockSpec((ROWS, 3 * HS), lambda h: (0, h)),
-            pl.BlockSpec((ROWS, 128), lambda h: (0, 3 * HH)),
-        ],
-        out_specs=(
-            pl.BlockSpec((1, RR, SLOTS, SLOTS), lambda h: (h, 0, 0, 0)),
-            pl.BlockSpec((1, RR, SLOTS, 3 * HS), lambda h: (h, 0, 0, 0)),
-            pl.BlockSpec((1, RR, SLOTS, HS), lambda h: (h, 0, 0, 0)),
-            pl.BlockSpec((NO * 3 * ITEMS, SLOTS), lambda h: (0, 0)),
-            pl.BlockSpec((HS, SLOTS), lambda h: (0, 0)),
-        ),
-        scratch_shapes=[
+        out_shape=tuple(pltpu.HBM(*shape) for shape in shapes),
+        in_specs=[pl.BlockSpec(memory_space=pltpu.VMEM)],
+        out_specs=(pl.BlockSpec(memory_space=pl.ANY),) * len(shapes),
+        scratch_shapes=[pltpu.VMEM(*shape) for shape in shapes]
+        + [
             pltpu.VMEM((RR, SLOTS, SLOTS), F32),
             pltpu.VMEM((RR, SLOTS, HS), F32),
             pltpu.VMEM((RR, SLOTS, 2 * HS), BF),
+            pltpu.SemaphoreType.DMA((3 * HH + 2,)),
         ],
         compiler_params=pltpu.CompilerParams(vmem_limit_bytes=VMEM),
         name="forward",
-    )(received, received)
+    )(received)
 
 
 def between_kernel(probs_ref, rows_ref, self_ref, probs_t_ref, weighted_t_ref, sums_ref):
     for r in range(RR):
-        probs = probs_ref[0, r]
+        probs = (probs_ref[0, r].astype(F32) * self_ref[0, r, :, 3:4]).astype(BF)
         q = rows_ref[0, r, :, :HS]
         v = rows_ref[0, r, :, HS : 2 * HS]
         u = rows_ref[0, r, :, 2 * HS :]
@@ -294,8 +312,8 @@
     for at in range(SLOTS // HS):
         got[at] = got_ref[:, pl.ds(at * HS, HS)].astype(F32)
     mine = mine_ref[...].astype(F32)
-    owner_ids = iota((NO, SLOTS), 0).astype(F32)
-    slot_ids = iota((SLOTS, SLOTS), 0)
+    owner_ids = iota((3 * NO, SLOTS), 0)
+    slot_ids = iota((HS, SLOTS), 0)
     source = iota((1, SLOTS), 1) & (NO - 1)
     mine_lse, mine_inner, other_lse, other_inner = [], [], [], []
     for item in range(ITEMS):
@@ -306,13 +324,14 @@
                     got[i, pl.ds(first_row + at, NO, stride=3 * ITEMS), :]
                     for i in range(SLOTS // HS)
                 ],
-                axis=1,
+                axis=0,
             ).astype(BF)
             for at in range(3)
         )
-        hot = (owner_ids == mine[OWNERS + item : OWNERS + item + 1]).astype(BF)
-        place = mine[PLACES + item : PLACES + item + 1].astype(jnp.int32) * NO + source
-        here = slot_ids == place
+        owner = mine[OWNERS + item : OWNERS + item + 1].astype(jnp.int32)
+        slot = mine[PLACES + item : PLACES + item + 1].astype(jnp.int32)
+        hot = (owner_ids == lax.shift_right_logical(slot, 2) * NO + owner).astype(BF)
+        here = slot_ids == (slot & 3) * NO + source
         table = jnp.concatenate([high, low], axis=0)
         logs = dot(table, jnp.concatenate([hot, hot], axis=0), 0, 0)
         inners = dot(inners, hot, 0, 0)
@@ -343,33 +362,66 @@
 
 
 def backward_kernel(
-    probs_ref, weighted_ref, q_ref, u_ref, sums_ref, mine_ref, got_ref, out_ref, got, put
+    probs_ref,
+    weighted_ref,
+    rows_ref,
+    sums_ref,
+    mine_ref,
+    got_ref,
+    out_ref,
+    probs,
+    weighted,
+    queries,
+    upstream,
+    sums,
+    out,
+    got,
+    put,
+    sems,
 ):
-    h = pl.program_id(0)
-
-    @pl.when(h == 0)
-    def _():
-        round_shares(mine_ref, got_ref, got, put)
-
-    grads = []
-    for r in range(RR):
-        share = put[h, r, :, :HS]
-        shift = put[h, r, :, HS:]
-        q = q_ref[0, r].astype(F32)
-        u_share = share * u_ref[0, r].astype(F32)
-        q_share = share * q
-        right = jnp.concatenate([-shift * q_share, u_share], axis=1).astype(BF)
-        both = dot(probs_ref[0, r], right)
-        unit_grad = (dot(weighted_ref[0, r], q_share.astype(BF)) + both[:, :HS]) * SCALE
-        value_grad = both[:, HS:] + sums_ref[0, r, :, 2 * HS :].astype(F32) * u_share
-        scale = lax.rsqrt(jnp.sum(q * q, axis=1, keepdims=True) + 1e-06)
-        along = jnp.sum(q * unit_grad, axis=1, keepdims=True)
-        first = sums_ref[0, r, :, :HS].astype(F32)
-        second = sums_ref[0, r, :, HS : 2 * HS].astype(F32)
-        query_grad = (share * SCALE) * (first - shift * second)
-        query_grad += scale * unit_grad - q * (scale * scale * scale * along)
-        grads.append(jnp.concatenate([query_grad, value_grad], axis=1))
-    out_ref[...] = join_rounds(grads[0], grads[1]).astype(BF)
+    loads = []
+    for h in range(HH):
+        pairs = (
+            (probs_ref.at[h], probs.at[h]),
+            (weighted_ref.at[h], weighted.at[h]),
+            (rows_ref.at[h, :, :, pl.ds(0, HS)], queries.at[h]),
+            (rows_ref.at[h, :, :, pl.ds(2 * HS, HS)], upstream.at[h]),
+            (sums_ref.at[h], sums.at[h]),
+        )
+        loads.append(
+            [pltpu.make_async_copy(*p, sems.at[6 * h + at]) for at, p in enumerate(pairs)]
+        )
+        for copy in loads[h]:
+            copy.start()
+    round_shares(mine_ref, got_ref, got, put)
+    stores = []
+    for h in range(HH):
+        for copy in loads[h]:
+            copy.wait()
+        grads = []
+        for r in range(RR):
+            share = put[h, r, :, :HS]
+            shift = put[h, r, :, HS:]
+            q = queries[h, r].astype(F32)
+            u_share = share * upstream[h, r].astype(F32)
+            q_share = share * q
+            right = jnp.concatenate([-shift * q_share, u_share], axis=1).astype(BF)
+            both = dot(probs[h, r], right)
+            unit_grad = (dot(weighted[h, r], q_share.astype(BF)) + both[:, :HS]) * SCALE
+            value_grad = both[:, HS:] + sums[h, r, :, 2 * HS :].astype(F32) * u_share
+            scale = lax.rsqrt(jnp.sum(q * q, axis=1, keepdims=True) + 1e-06)
+            along = jnp.sum(q * unit_grad, axis=1, keepdims=True)
+            first = sums[h, r, :, :HS].astype(F32)
+            second = sums[h, r, :, HS : 2 * HS].astype(F32)
+            query_grad = (share * SCALE) * (first - shift * second)
+            query_grad += scale * unit_grad - q * (scale * scale * scale * along)
+            grads.append(jnp.concatenate([query_grad, value_grad], axis=1))
+        out[h] = join_rounds(grads[0], grads[1]).astype(BF)
+        there = out_ref.at[:, pl.ds(h * 2 * HS, 2 * HS)]
+        stores.append(pltpu.make_async_copy(out.at[h], there, sems.at[6 * h + 5]))
+        stores[h].start()
+    for copy in stores:
+        copy.wait()
 
 
 def pinned(x):
@@ -377,36 +429,42 @@
 
 
 def backward(probs, weighted, rows, sums, mine, got):
+    hbm = pl.BlockSpec(memory_space=pl.ANY)
+    vmem = pl.BlockSpec(memory_space=pltpu.VMEM)
     return pl.pallas_call(
         backward_kernel,
-        grid=(HH,),
         out_shape=pltpu.HBM((ROWS, HH * 2 * HS), BF),
-        in_specs=[
-            SQUARE,
-            SQUARE,
-            pl.BlockSpec((1, RR, SLOTS, HS), lambda h: (h, 0, 0, 0)),
-            pl.BlockSpec((1, RR, SLOTS, HS), lambda h: (h, 0, 0, 2)),
-            WIDE,
-            pl.BlockSpec((HS, SLOTS), lambda h: (0, 0)),
-            pl.BlockSpec((NO * 3 * ITEMS, SLOTS), lambda h: (0, 0)),
-        ],
-        out_specs=pl.BlockSpec((ROWS, 2 * HS), lambda h: (0, h)),
+        in_specs=[hbm, hbm, hbm, hbm, vmem, vmem],
+        out_specs=hbm,
         scratch_shapes=[
+            pltpu.VMEM((HH, RR, SLOTS, SLOTS), BF),
+            pltpu.VMEM((HH, RR, SLOTS, SLOTS), BF),
+            pltpu.VMEM((HH, RR, SLOTS, HS), BF),
+            pltpu.VMEM((HH, RR, SLOTS, HS), BF),
+            pltpu.VMEM((HH, RR, SLOTS, 3 * HS), BF),
+            pltpu.VMEM((HH, ROWS, 2 * HS), BF),
             pltpu.VMEM((SLOTS // HS, NO * 3 * ITEMS, HS), F32),
             pltpu.VMEM((HH, RR, SLOTS, 2 * HS), F32),
+            pltpu.SemaphoreType.DMA((6 * HH,)),
         ],
         compiler_params=pltpu.CompilerParams(vmem_limit_bytes=VMEM),
         name="backward",
-    )(pinned(probs), pinned(weighted), pinned(rows), pinned(rows), pinned(sums), pinned(mine), got)
-
-
-def collect_kernel(rows_ref, got_ref, out_ref):
-    row_ids = iota((ROWS, TT), 0)
+    )(pinned(probs), pinned(weighted), pinned(rows), pinned(sums), mine, got)
+
+
+def collect_kernel(rows_ref, got_ref, out_ref, got, sems):
+    loads = []
     for h in range(HH):
-        first = row_ids == rows_ref[h : h + 1, :]
-        second = row_ids == rows_ref[HH + h : HH + h + 1, :]
+        here = got_ref.at[:, pl.ds(h * 2 * HS, 2 * HS)]
+        loads.append(pltpu.make_async_copy(here, got.at[h], sems.at[h]))
+        loads[h].start()
+    row_ids = iota((TT, ROWS), 1)
+    for h in range(HH):
+        first = row_ids == rows_ref[:, h : h + 1]
+        second = row_ids == rows_ref[:, HH + h : HH + h + 1]
         hot = (first | second).astype(BF)
-        sums = dot(hot, got_ref[:, pl.ds(h * 2 * HS, 2 * HS)], 0, 0).astype(BF)
+        loads[h].wait()
+        sums = dot(hot, got[h]).astype(BF)
         out_ref[0, :, pl.ds(h * HS, HS)] = sums[:, :HS]
         out_ref[1, :, pl.ds(h * HS, HS)] = sums[:, HS:]
 
@@ -415,9 +473,15 @@
     return pl.pallas_call(
         collect_kernel,
         out_shape=jax.ShapeDtypeStruct((2, TT, HH * HS), BF),
+        in_specs=[pl.BlockSpec(memory_space=pltpu.VMEM), pl.BlockSpec(memory_space=pl.ANY)],
+        out_specs=pl.BlockSpec(memory_space=pltpu.VMEM),
+        scratch_shapes=[
+            pltpu.VMEM((HH, ROWS, 2 * HS), BF),
+            pltpu.SemaphoreType.DMA((HH,)),
+        ],
         compiler_params=pltpu.CompilerParams(vmem_limit_bytes=VMEM),
         name="collect",
-    )(rows, got)
+    )(rows, pinned(got))
 
 
 def exchange(x):
@@ -449,7 +513,7 @@
     ).astype(jnp.bfloat16)
     rows, send = dispatch(odd, buckets, projected, cotangent)
     received = exchange(send)
-    rows = blocks_of(rows, me)
+    rows = blocks_of(rows, me).T
     probs, held, own, wire, mine = forward(received)
     everyones = exchange(wire)
     probs_t, weighted_t, sums = between(probs, held, own)

time: 143 us -> 137 us (0.958)
  Pallas kernels: 30.2 us -> 24.3 us
    pallas_call x2, Pallas kernels: 18 us -> 12.4 us  [the longest x1 6.27 us: forward(): pl.pallas_call(forward_kernel, out_shape=tuple((pltpu.HBM(*shape) for sha...]
where the time goes in v4:
time: 137 us; the launch traced here: 136 us
  blocking collectives  41.5 us (30%)
  waiting for transfers between devices  29.3 us (21%)
  Pallas kernels  24.3 us (18%)
  starting transfers between devices  19.7 us (14%)
  local copies, waits for them, and re-layouts  11.4 us (8%)
  matrix products  8.73 us (6%)
    all_to_all x1, blocking collectives, exchange(): return lax.all_to_all(x, 'seq', split_axis=0, concat_axis=0, tiled=True)  41.5 us
    all_to_all x2, waiting for transfers between devices, exchange(): return lax.all_to_all(x, 'seq', split_axis=0, concat_axis=0, tiled=True)  19.1 us
    ppermute x8, starting transfers between devices, swap(): return lax.ppermute(x, 'bkt', [(i, i ^ mask) for i in range(4)])  10.9 us
    ppermute x8, waiting for transfers between devices, swap(): return lax.ppermute(x, 'bkt', [(i, i ^ mask) for i in range(4)])  10.2 us
    transpose x1, local copies, waits for them, and re-layouts, per_device(): weights[i * width:(i + 1) * width].transpose(1, 0, 2)  9.38 us
    all_to_all x2, starting transfers between devices, exchange(): return lax.all_to_all(x, 'seq', split_axis=0, concat_axis=0, tiled=True)  8.79 us
    pallas_call x1, Pallas kernels, between(): pl.pallas_call(between_kernel, grid=(HH,), out_shape=(pltpu.HBM((HH, RR,...  7.48 us
    pallas_call x1, Pallas kernels, forward(): pl.pallas_call(forward_kernel, out_shape=tuple((pltpu.HBM(*shape) for sha...  6.27 us
  transfers between devices with their start and end apart: 10, of which 6 were waited for; matrix products, arithmetic and copies ran while one was open for 9% of the time, Pallas kernels for 5%

profile of v4, /device:TPU:0, one launch (start us, length us, event | category | flops | bytes accessed | tf_op | source)
XLA Modules:
  0.0 136.5 jit_solution(4826465728569794061)
XLA Ops:
  0.0 0.0 copy-start
  0.0 1.6 %copy-done = bf16[256,4096]{1,0:T(8,128)(2,1)S(1)} copy-done((bf16[256,4096]{1,0:T(8,128)(2,1)S(1)}, bf16[256,4096]{1,0:T(8,128)(2,1)}, u32[]{:S(2)}) %copy-start) | copy-done | bytes 2097176
  1.6 0.0 copy-start.1
  1.6 0.0 copy-start.3
  1.6 5.7 %fusion.40.proj_ref = bf16[2,256,512]{2,1,0:T(8,128)(2,1)S(1)} fusion(bf16[4096,2,512]{2,1,0:T(2,128)(2,1)} %param.5, bf16[256,4096]{1,0:T(8,128)(2,1)S(1)} %copy-done), kind=kOutput, calls=%fused_computation.24 | convolution fusion | flops 2147745792 | bytes 11010048 | tf_op jit(solution)/shard_map/td,dcf->ctf/dot_general | solution.py:511
  7.4 0.0 copy-done.1
  7.4 0.0 copy-done.3
  7.4 1.7 %dispatch.1 = (s32[8,256]{1,0:T(8,128)S(1)}, bf16[768,1664]{1,0:T(8,128)(2,1)S(1)}) custom-call(s32[1]{0:T(128)} %bitcast.odd_ref, s32[2,4,256]{2,1,0:T(4,128)S(1)} %copy-done.3, bf16[2,256,512]{2,1,0:T(8,128)(2,1)S(1)} %fusion.40.proj_ref, bf16[256,512]{1,0:T(8,128)(2,1)S(1)} %copy-done.1), custom_call_target="tpu_custom_call" | custom-call | tf_op jit(solution)/shard_map/dispatch/pallas_call | solution.py:93
  9.1 41.5 %all_to_all.33 = bf16[32,24,1664]{2,1,0:T(8,128)(2,1)S(1)} all-to-all(bf16[32,24,1664]{2,1,0:T(8,128)(2,1)S(1)} %bitcast.90), channel_id=1, replica_groups=mesh['seq'=32,'bkt'=4] {'seq'}, dimensions={0} | all-to-all | bytes 5111808 | tf_op jit(solution)/shard_map/all_to_all | solution.py:488
  50.6 6.3 %forward.1 = (bf16[4,2,384,384]{3,2,1,0:T(8,128)(2,1)}, bf16[4,2,384,384]{3,2,1,0:T(8,128)(2,1)}, f32[4,2,384,128]{3,2,1,0:T(8,128)}, bf16[768,384]{1,0:T(8,128)(2,1)}, bf16[128,384]{1,0:T(8,128)(2,1)}) custom-call(bf16[768,1664]{1,0:T(8,128)(2,1)S(1)} %bitcast.89), custom_call_target="tpu_custom_call" | custom-call | tf_op jit(solution)/shard_map/forward/pallas_call | solution.py:253
  56.9 4.1 %all-to-all-start.1 = ((bf16[32,24,384]{2,1,0:T(8,128)(2,1)}), bf16[32,24,384]{2,1,0:T(8,128)(2,1)S(1)}, u32[]{:S(2)}, u32[]{:S(2)}) async-start(bf16[32,24,384]{2,1,0:T(8,128)(2,1)} %bitcast.96), calls=%async_computation.1 | async-start | bytes 1179648 | tf_op jit(solution)/shard_map/all_to_all | solution.py:488
  61.0 0.0 copy-start.2
  61.0 7.5 %between.1 = (bf16[4,2,384,384]{3,2,1,0:T(8,128)(2,1)}, bf16[4,2,384,384]{3,2,1,0:T(8,128)(2,1)}, bf16[4,2,384,384]{3,2,1,0:T(8,128)(2,1)}) custom-call(bf16[4,2,384,384]{3,2,1,0:T(8,128)(2,1)} %get-tuple-element.21.probs_ref, bf16[4,2,384,384]{3,2,1,0:T(8,128)(2,1)} %get-tuple-element.22.rows_ref, f32[4,2,384,128]{3,2,1,0:T(8,128)} %get-tuple-element.23.self_ref), custom_call_target="tpu_custom_call" | custom-call | flops 905969664 | bytes 12582912 | tf_op jit(solution)/shard_map/between/pallas_call | solution.py:295
  68.5 4.9 %all-to-all-done.1 = bf16[32,24,384]{2,1,0:T(8,128)(2,1)S(1)} async-done(((bf16[32,24,384]{2,1,0:T(8,128)(2,1)}), bf16[32,24,384]{2,1,0:T(8,128)(2,1)S(1)}, u32[]{:S(2)}, u32[]{:S(2)}) %all-to-all-start.1) | async-done | bytes 589856 | tf_op jit(solution)/shard_map/all_to_all | solution.py:488
  73.3 0.0 copy-done.2
  73.3 6.1 %backward.1 = bf16[768,1024]{1,0:T(8,128)(2,1)} custom-call(bf16[4,2,384,384]{3,2,1,0:T(8,128)(2,1)} %get-tuple-element.24.probs_ref, bf16[4,2,384,384]{3,2,1,0:T(8,128)(2,1)} %get-tuple-element.25.weighted_ref, bf16[4,2,384,384]{3,2,1,0:T(8,128)(2,1)} %get-tuple-element.22.rows_ref, bf16[4,2,384,384]{3,2,1,0:T(8,128)(2,1)} %get-tuple-element.26.sums_ref, ...), custom_call_target="tpu_custom_call" | custom-call | tf_op jit(solution)/shard_map/backward/pallas_call | solution.py:434
  79.4 4.7 %all-to-all-start.2 = ((bf16[32,24,1024]{2,1,0:T(8,128)(2,1)}), bf16[32,24,1024]{2,1,0:T(8,128)(2,1)}, u32[]{:S(2)}, u32[]{:S(2)}) async-start(bf16[32,24,1024]{2,1,0:T(8,128)(2,1)} %bitcast.93), calls=%async_computation.2 | async-start | bytes 3145728 | tf_op jit(solution)/shard_map/all_to_all | solution.py:488
  84.2 0.1 constant_dynamic-slice_fusion.3
  84.3 0.1 pad_add_fusion
  84.3 0.1 copy.17
  84.5 9.4 %slice_bitcast_fusion = (bf16[2,1024,512]{2,0,1:T(2,128)(2,1)}, bf16[2,1024,512]{2,0,1:T(2,128)(2,1)}, bf16[2,1024,512]{2,0,1:T(2,128)(2,1)}, bf16[2,1024,512]{2,0,1:T(2,128)(2,1)}) fusion(bf16[4096,2,512]{2,1,0:T(2,128)(2,1)} %param.5), kind=kLoop, calls=%fused_computation.11 | loop fusion | bytes 16777216 | tf_op jit(solution)/shard_map/transpose | solution.py:524
  93.8 14.2 %all-to-all-done.2 = bf16[32,24,1024]{2,1,0:T(8,128)(2,1)} async-done(((bf16[32,24,1024]{2,1,0:T(8,128)(2,1)}), bf16[32,24,1024]{2,1,0:T(8,128)(2,1)}, u32[]{:S(2)}, u32[]{:S(2)}) %all-to-all-start.2) | async-done | bytes 1572896 | tf_op jit(solution)/shard_map/all_to_all | solution.py:488
  108.1 0.0 copy-start.7
  108.1 2.8 %collect.1 = bf16[2,256,512]{2,1,0:T(8,128)(2,1)S(1)} custom-call(s32[256,8]{1,0:T(8,128)S(1)} %bitcast.92, bf16[768,1024]{1,0:T(8,128)(2,1)} %bitcast.9.got_ref), custom_call_target="tpu_custom_call" | custom-call | tf_op jit(solution)/shard_map/collect/pallas_call | solution.py:473
  110.9 0.0 copy-done.7
  110.9 0.0 copy-start.6
  110.9 0.7 fusion.37
  111.7 0.0 copy-start.5
  111.7 1.7 %collective-permute-start = (bf16[2,64,1024]{2,1,0:T(8,128)(2,1)S(1)}, bf16[2,64,1024]{2,1,0:T(8,128)(2,1)S(1)}, u32[]{:S(2)}, u32[]{:S(2)}) collective-permute-start(bf16[2,64,1024]{2,1,0:T(8,128)(2,1)S(1)} %bitcast.98), channel_id=1, source_target_pairs={{0,1},{1,0},{2,3},{3,2},{4,5},{5,4},{6,7},{7,6},{8,9},{9,8},{10,11... | collective-permute-start | bytes 786440 | tf_op jit(solution)/shard_map/ppermute | solution.py:502
  113.4 0.0 copy-done.6
  113.4 0.7 fusion.34
  114.2 0.0 copy-start.4
  114.2 2.5 %collective-permute-start.2 = (bf16[2,64,1024]{2,1,0:T(8,128)(2,1)S(1)}, bf16[2,64,1024]{2,1,0:T(8,128)(2,1)S(1)}, u32[]{:S(2)}, u32[]{:S(2)}) collective-permute-start(bf16[2,64,1024]{2,1,0:T(8,128)(2,1)S(1)} %pad_maximum_fusion.1), channel_id=1, source_target_pairs={{0,3},{1,2},{2,1},{3,0},{4,7},{5,6},{6,5},{7,4},{8,11},{9,10},{10,... | collective-permute-start | bytes 786440 | tf_op jit(solution)/shard_map/ppermute | solution.py:502
  116.7 0.0 copy-done.5
  116.7 0.7 fusion.31
  117.4 0.0 copy-done.4
  117.4 0.7 fusion.28
  118.3 1.1 collective-permute-start.6
  119.4 0.1 collective-permute-start.4
  119.6 0.0 collective-permute-done
  119.6 0.1 add.40
  119.7 2.2 %collective-permute-start.1 = (bf16[64,1024]{1,0:T(8,128)(2,1)S(1)}, bf16[64,1024]{1,0:T(8,128)(2,1)S(1)}, u32[]{:S(2)}, u32[]{:S(2)}) collective-permute-start(bf16[64,1024]{1,0:T(8,128)(2,1)S(1)} %slice_bitcast_fusion.18), channel_id=1, source_target_pairs={{0,3},{1,2},{2,1},{3,0},{4,7},{5,6},{6,5},{7,4},{8,11},{9,10},{10,... | collective-permute-start | bytes 393224 | tf_op jit(solution)/shard_map/ppermute | solution.py:502
  121.9 2.0 %collective-permute-done.2 = bf16[2,64,1024]{2,1,0:T(8,128)(2,1)S(1)} collective-permute-done((bf16[2,64,1024]{2,1,0:T(8,128)(2,1)S(1)}, bf16[2,64,1024]{2,1,0:T(8,128)(2,1)S(1)}, u32[]{:S(2)}, u32[]{:S(2)}) %collective-permute-start.2) | collective-permute-done | bytes 262176 | tf_op jit(solution)/shard_map/ppermute | solution.py:502
  123.9 0.7 collective-permute-start.3
  124.6 4.5 %collective-permute-done.6 = bf16[2,64,1024]{2,1,0:T(8,128)(2,1)S(1)} collective-permute-done((bf16[2,64,1024]{2,1,0:T(8,128)(2,1)S(1)}, bf16[2,64,1024]{2,1,0:T(8,128)(2,1)S(1)}, u32[]{:S(2)}, u32[]{:S(2)}) %collective-permute-start.6) | collective-permute-done | bytes 262176 | tf_op jit(solution)/shard_map/ppermute | solution.py:502
  129.2 0.1 collective-permute-start.7
  129.3 0.0 collective-permute-done.4
  129.3 0.1 add.44
  129.4 2.5 %collective-permute-start.5 = (bf16[64,1024]{1,0:T(8,128)(2,1)S(1)}, bf16[64,1024]{1,0:T(8,128)(2,1)S(1)}, u32[]{:S(2)}, u32[]{:S(2)}) collective-permute-start(bf16[64,1024]{1,0:T(8,128)(2,1)S(1)} %slice_bitcast_fusion.10), channel_id=1, source_target_pairs={{0,3},{1,2},{2,1},{3,0},{4,7},{5,6},{6,5},{7,4},{8,11},{9,10},{10,... | collective-permute-start | bytes 393224 | tf_op jit(solution)/shard_map/ppermute | solution.py:502
  131.8 0.0 collective-permute-done.1
  131.9 0.0 collective-permute-done.3
  131.9 2.3 %collective-permute-done.7 = bf16[64,1024]{1,0:T(8,128)(2,1)S(1)} collective-permute-done((bf16[64,1024]{1,0:T(8,128)(2,1)S(1)}, bf16[64,1024]{1,0:T(8,128)(2,1)S(1)}, u32[]{:S(2)}, u32[]{:S(2)}) %collective-permute-start.7) | collective-permute-done | bytes 131104 | tf_op jit(solution)/shard_map/ppermute | solution.py:502
  134.2 1.4 %collective-permute-done.5 = bf16[64,1024]{1,0:T(8,128)(2,1)S(1)} collective-permute-done((bf16[64,1024]{1,0:T(8,128)(2,1)S(1)}, bf16[64,1024]{1,0:T(8,128)(2,1)S(1)}, u32[]{:S(2)}, u32[]{:S(2)}) %collective-permute-start.5) | collective-permute-done | bytes 131104 | tf_op jit(solution)/shard_map/ppermute | solution.py:502
  135.6 0.8 pad_maximum_fusion
  (16 shorter events, 0.4 us)
Async XLA Ops:
  0.0 1.6 %copy-start = (bf16[256,4096]{1,0:T(8,128)(2,1)S(1)}, bf16[256,4096]{1,0:T(8,128)(2,1)}, u32[]{:S(2)}) copy-start(bf16[256,4096]{1,0:T(8,128)(2,1)} %param.4) | copy-start | bytes 6291460
  1.6 5.8 %copy-start.1 = (bf16[256,512]{1,0:T(8,128)(2,1)S(1)}, bf16[256,512]{1,0:T(8,128)(2,1)}, u32[]{:S(2)}) copy-start(bf16[256,512]{1,0:T(8,128)(2,1)} %cot_ref.1) | copy-start | bytes 786436
  1.6 5.8 %copy-start.3 = (s32[2,4,256]{2,1,0:T(4,128)S(1)}, s32[2,4,256]{2,1,0:T(4,128)}, u32[]{:S(2)}) copy-start(s32[2,4,256]{2,1,0:T(4,128)} %buckets_ref.1) | copy-start | bytes 24580
  56.9 16.4 %all-to-all-start.1 = ((bf16[32,24,384]{2,1,0:T(8,128)(2,1)}), bf16[32,24,384]{2,1,0:T(8,128)(2,1)S(1)}, u32[]{:S(2)}, u32[]{:S(2)}) async-start(bf16[32,24,384]{2,1,0:T(8,128)(2,1)} %bitcast.96), calls=%async_computation.1 | async-start | bytes 1179648 | tf_op jit(solution)/shard_map/all_to_all | solution.py:488
  61.0 12.4 %copy-start.2 = (bf16[128,384]{1,0:T(8,128)(2,1)S(1)}, bf16[128,384]{1,0:T(8,128)(2,1)}, u32[]{:S(2)}) copy-start(bf16[128,384]{1,0:T(8,128)(2,1)} %get-tuple-element.27.mine_ref) | copy-start | bytes 294916
  79.4 28.6 %all-to-all-start.2 = ((bf16[32,24,1024]{2,1,0:T(8,128)(2,1)}), bf16[32,24,1024]{2,1,0:T(8,128)(2,1)}, u32[]{:S(2)}, u32[]{:S(2)}) async-start(bf16[32,24,1024]{2,1,0:T(8,128)(2,1)} %bitcast.93), calls=%async_computation.2 | async-start | bytes 3145728 | tf_op jit(solution)/shard_map/all_to_all | solution.py:488
  108.1 2.8 %copy-start.7 = (bf16[2,1024,512]{2,0,1:T(2,128)(2,1)S(1)}, bf16[2,1024,512]{2,0,1:T(2,128)(2,1)}, u32[]{:S(2)}) copy-start(bf16[2,1024,512]{2,0,1:T(2,128)(2,1)} %get-tuple-element.29) | copy-start | bytes 6291460
  110.9 2.5 %copy-start.6 = (bf16[2,1024,512]{2,0,1:T(2,128)(2,1)S(1)}, bf16[2,1024,512]{2,0,1:T(2,128)(2,1)}, u32[]{:S(2)}) copy-start(bf16[2,1024,512]{2,0,1:T(2,128)(2,1)} %get-tuple-element.30) | copy-start | bytes 6291460
  111.7 5.0 %copy-start.5 = (bf16[2,1024,512]{2,0,1:T(2,128)(2,1)S(1)}, bf16[2,1024,512]{2,0,1:T(2,128)(2,1)}, u32[]{:S(2)}) copy-start(bf16[2,1024,512]{2,0,1:T(2,128)(2,1)} %get-tuple-element.31) | copy-start | bytes 6291460
  111.7 7.9 %collective-permute-start = (bf16[2,64,1024]{2,1,0:T(8,128)(2,1)S(1)}, bf16[2,64,1024]{2,1,0:T(8,128)(2,1)S(1)}, u32[]{:S(2)}, u32[]{:S(2)}) collective-permute-start(bf16[2,64,1024]{2,1,0:T(8,128)(2,1)S(1)} %bitcast.98), channel_id=1, source_target_pairs={{0,1},{1,0},{2,3},{3,2},{4,5},{5,4},{6,7},{7,6},{8,9},{9,8},{10,11... | collective-permute-start | bytes 786440 | tf_op jit(solution)/shard_map/ppermute | solution.py:502
  114.2 3.2 %copy-start.4 = (bf16[2,1024,512]{2,0,1:T(2,128)(2,1)S(1)}, bf16[2,1024,512]{2,0,1:T(2,128)(2,1)}, u32[]{:S(2)}) copy-start(bf16[2,1024,512]{2,0,1:T(2,128)(2,1)} %get-tuple-element.32) | copy-start | bytes 6291460
  114.2 9.6 %collective-permute-start.2 = (bf16[2,64,1024]{2,1,0:T(8,128)(2,1)S(1)}, bf16[2,64,1024]{2,1,0:T(8,128)(2,1)S(1)}, u32[]{:S(2)}, u32[]{:S(2)}) collective-permute-start(bf16[2,64,1024]{2,1,0:T(8,128)(2,1)S(1)} %pad_maximum_fusion.1), channel_id=1, source_target_pairs={{0,3},{1,2},{2,1},{3,0},{4,7},{5,6},{6,5},{7,4},{8,11},{9,10},{10,... | collective-permute-start | bytes 786440 | tf_op jit(solution)/shard_map/ppermute | solution.py:502
  118.3 10.8 %collective-permute-start.6 = (bf16[2,64,1024]{2,1,0:T(8,128)(2,1)S(1)}, bf16[2,64,1024]{2,1,0:T(8,128)(2,1)S(1)}, u32[]{:S(2)}, u32[]{:S(2)}) collective-permute-start(bf16[2,64,1024]{2,1,0:T(8,128)(2,1)S(1)} %pad_maximum_fusion.2), channel_id=1, source_target_pairs={{0,3},{1,2},{2,1},{3,0},{4,7},{5,6},{6,5},{7,4},{8,11},{9,10},{10,... | collective-permute-start | bytes 786440 | tf_op jit(solution)/shard_map/ppermute | solution.py:502
  119.4 9.8 %collective-permute-start.4 = (bf16[2,64,1024]{2,1,0:T(8,128)(2,1)S(1)}, bf16[2,64,1024]{2,1,0:T(8,128)(2,1)S(1)}, u32[]{:S(2)}, u32[]{:S(2)}) collective-permute-start(bf16[2,64,1024]{2,1,0:T(8,128)(2,1)S(1)} %bitcast.97), channel_id=1, source_target_pairs={{0,1},{1,0},{2,3},{3,2},{4,5},{5,4},{6,7},{7,6},{8,9},{9,8},{10,11... | collective-permute-start | bytes 786440 | tf_op jit(solution)/shard_map/ppermute | solution.py:502
  119.7 12.2 %collective-permute-start.1 = (bf16[64,1024]{1,0:T(8,128)(2,1)S(1)}, bf16[64,1024]{1,0:T(8,128)(2,1)S(1)}, u32[]{:S(2)}, u32[]{:S(2)}) collective-permute-start(bf16[64,1024]{1,0:T(8,128)(2,1)S(1)} %slice_bitcast_fusion.18), channel_id=1, source_target_pairs={{0,3},{1,2},{2,1},{3,0},{4,7},{5,6},{6,5},{7,4},{8,11},{9,10},{10,... | collective-permute-start | bytes 393224 | tf_op jit(solution)/shard_map/ppermute | solution.py:502
  123.9 8.0 %collective-permute-start.3 = (bf16[64,1024]{1,0:T(8,128)(2,1)S(1)}, bf16[64,1024]{1,0:T(8,128)(2,1)S(1)}, u32[]{:S(2)}, u32[]{:S(2)}) collective-permute-start(bf16[64,1024]{1,0:T(8,128)(2,1)S(1)} %slice_bitcast_fusion.12), channel_id=1, source_target_pairs={{0,1},{1,0},{2,3},{3,2},{4,5},{5,4},{6,7},{7,6},{8,9},{9,8},{10,11... | collective-permute-start | bytes 393224 | tf_op jit(solution)/shard_map/ppermute | solution.py:502
  129.2 5.0 %collective-permute-start.7 = (bf16[64,1024]{1,0:T(8,128)(2,1)S(1)}, bf16[64,1024]{1,0:T(8,128)(2,1)S(1)}, u32[]{:S(2)}, u32[]{:S(2)}) collective-permute-start(bf16[64,1024]{1,0:T(8,128)(2,1)S(1)} %slice_bitcast_fusion.4), channel_id=1, source_target_pairs={{0,1},{1,0},{2,3},{3,2},{4,5},{5,4},{6,7},{7,6},{8,9},{9,8},{10,11... | collective-permute-start | bytes 393224 | tf_op jit(solution)/shard_map/ppermute | solution.py:502
  129.4 6.3 %collective-permute-start.5 = (bf16[64,1024]{1,0:T(8,128)(2,1)S(1)}, bf16[64,1024]{1,0:T(8,128)(2,1)S(1)}, u32[]{:S(2)}, u32[]{:S(2)}) collective-permute-start(bf16[64,1024]{1,0:T(8,128)(2,1)S(1)} %slice_bitcast_fusion.10), channel_id=1, source_target_pairs={{0,3},{1,2},{2,1},{3,0},{4,7},{5,6},{6,5},{7,4},{8,11},{9,10},{10,... | collective-permute-start | bytes 393224 | tf_op jit(solution)/shard_map/ppermute | solution.py:502

commit v5 on v4

--- a/solution.py
+++ b/solution.py
@@ -22,6 +22,7 @@
 POWER = SCALE / math.log(2.0)
 SELF_SCORE = -100000.0
 FAR = -(2.0**30)
+LSE_SHIFT = 4.5
 F32 = jnp.float32
 BF = jnp.bfloat16
 VMEM = 24 * 1024 * 1024
@@ -208,9 +209,9 @@
             for at, column in enumerate((own, inner, scale, inverse)):
                 kept = jnp.where(lane == at, column.astype(F32), kept)
             kept_all[h, r] = kept
-            at = lane - (r * HH + h) * 3
-            sent = jnp.where((at == 0) | (at == 1), lse, spread[r])
-            spread[r] = jnp.where(at == 2, inner, sent)
+            at = lane - (r * HH + h) * 2
+            sent = jnp.where(at == 0, lse - LSE_SHIFT, spread[r])
+            spread[r] = jnp.where(at == 1, inner, sent)
         for at, (here, there) in enumerate(
             ((probs, probs_ref), (rows, rows_ref), (kept_all, self_ref))
         ):
@@ -223,15 +224,12 @@
     for r in range(RR):
         source, slot = source_and_slot((SLOTS, 1), 0, r)
         hot = (iota((SLOTS, SLOTS), 1) == slot * NO + source).astype(BF)
-        high, low = halves(spread[r])
-        low_lane = (lane < 3 * ITEMS) & (lane % 3 == 1)
-        sent = jnp.where(low_lane, low.astype(F32), high.astype(F32)).astype(BF)
-        total += dot(sent, hot, 0, 0)
+        total += dot(spread[r].astype(BF), hot, 0, 0)
     total = total.astype(BF)
     mine[...] = total
-    total = total[: 3 * ITEMS]
+    total = total[: 2 * ITEMS]
     for k in range(NO):
-        wire[pl.ds(k * 3 * ITEMS, 3 * ITEMS), :] = total
+        wire[pl.ds(k * 2 * ITEMS, 2 * ITEMS), :] = total
     copies += [
         pltpu.make_async_copy(mine, mine_ref, sems.at[3 * HH]),
         pltpu.make_async_copy(wire, wire_ref, sems.at[3 * HH + 1]),
@@ -247,7 +245,7 @@
         ((HH, RR, SLOTS, SLOTS), BF),
         ((HH, RR, SLOTS, 3 * HS), BF),
         ((HH, RR, SLOTS, HS), F32),
-        ((NO * 3 * ITEMS, SLOTS), BF),
+        ((NO * 2 * ITEMS, SLOTS), BF),
         ((HS, SLOTS), BF),
     )
     return pl.pallas_call(
@@ -317,28 +315,29 @@
     source = iota((1, SLOTS), 1) & (NO - 1)
     mine_lse, mine_inner, other_lse, other_inner = [], [], [], []
     for item in range(ITEMS):
-        first_row = (item ^ HH) * 3
-        high, low, inners = (
-            jnp.concatenate(
-                [
-                    got[i, pl.ds(first_row + at, NO, stride=3 * ITEMS), :]
-                    for i in range(SLOTS // HS)
-                ],
-                axis=0,
-            ).astype(BF)
-            for at in range(3)
+        first_row = (item ^ HH) * 2
+        table = jnp.concatenate(
+            [
+                jnp.concatenate(
+                    [
+                        got[i, pl.ds(first_row + at, NO, stride=2 * ITEMS), :]
+                        for i in range(SLOTS // HS)
+                    ],
+                    axis=0,
+                ).astype(BF)
+                for at in range(2)
+            ],
+            axis=1,
         )
         owner = mine[OWNERS + item : OWNERS + item + 1].astype(jnp.int32)
         slot = mine[PLACES + item : PLACES + item + 1].astype(jnp.int32)
         hot = (owner_ids == lax.shift_right_logical(slot, 2) * NO + owner).astype(BF)
         here = slot_ids == (slot & 3) * NO + source
-        table = jnp.concatenate([high, low], axis=0)
-        logs = dot(table, jnp.concatenate([hot, hot], axis=0), 0, 0)
-        inners = dot(inners, hot, 0, 0)
-        other_lse.append(jnp.sum(jnp.where(here, logs, 0.0), axis=0, keepdims=True))
-        other_inner.append(jnp.sum(jnp.where(here, inners, 0.0), axis=0, keepdims=True))
-        mine_lse.append(mine[item * 3 : item * 3 + 1] + mine[item * 3 + 1 : item * 3 + 2])
-        mine_inner.append(mine[item * 3 + 2 : item * 3 + 3])
+        seen = dot(table, hot, 0, 0)
+        other_lse.append(jnp.sum(jnp.where(here, seen[:HS], 0.0), axis=0, keepdims=True))
+        other_inner.append(jnp.sum(jnp.where(here, seen[HS:], 0.0), axis=0, keepdims=True))
+        mine_lse.append(mine[item * 2 : item * 2 + 1])
+        mine_inner.append(mine[item * 2 + 1 : item * 2 + 2])
     mine_lse, mine_inner, other_lse, other_inner = (
         jnp.concatenate(x, axis=0) for x in (mine_lse, mine_inner, other_lse, other_inner)
     )
@@ -443,7 +442,7 @@
             pltpu.VMEM((HH, RR, SLOTS, HS), BF),
             pltpu.VMEM((HH, RR, SLOTS, 3 * HS), BF),
             pltpu.VMEM((HH, ROWS, 2 * HS), BF),
-            pltpu.VMEM((SLOTS // HS, NO * 3 * ITEMS, HS), F32),
+            pltpu.VMEM((SLOTS // HS, NO * 2 * ITEMS, HS), F32),
             pltpu.VMEM((HH, RR, SLOTS, 2 * HS), F32),
             pltpu.SemaphoreType.DMA((6 * HH,)),
         ],
@@ -454,17 +453,20 @@
 
 def collect_kernel(rows_ref, got_ref, out_ref, got, sems):
     loads = []
-    for h in range(HH):
-        here = got_ref.at[:, pl.ds(h * 2 * HS, 2 * HS)]
-        loads.append(pltpu.make_async_copy(here, got.at[h], sems.at[h]))
-        loads[h].start()
+    for at in range(3):
+        part = pl.ds(at * (ROWS // 3), ROWS // 3)
+        loads.append(pltpu.make_async_copy(got_ref.at[part], got.at[part], sems.at[at]))
+        loads[at].start()
     row_ids = iota((TT, ROWS), 1)
+    hots = []
     for h in range(HH):
         first = row_ids == rows_ref[:, h : h + 1]
         second = row_ids == rows_ref[:, HH + h : HH + h + 1]
-        hot = (first | second).astype(BF)
-        loads[h].wait()
-        sums = dot(hot, got[h]).astype(BF)
+        hots.append((first | second).astype(BF))
+    for copy in loads:
+        copy.wait()
+    for h in range(HH):
+        sums = dot(hots[h], got[:, pl.ds(h * 2 * HS, 2 * HS)]).astype(BF)
         out_ref[0, :, pl.ds(h * HS, HS)] = sums[:, :HS]
         out_ref[1, :, pl.ds(h * HS, HS)] = sums[:, HS:]
 
@@ -476,8 +478,8 @@
         in_specs=[pl.BlockSpec(memory_space=pltpu.VMEM), pl.BlockSpec(memory_space=pl.ANY)],
         out_specs=pl.BlockSpec(memory_space=pltpu.VMEM),
         scratch_shapes=[
-            pltpu.VMEM((HH, ROWS, 2 * HS), BF),
-            pltpu.SemaphoreType.DMA((HH,)),
+            pltpu.VMEM((ROWS, HH * 2 * HS), BF),
+            pltpu.SemaphoreType.DMA((3,)),
         ],
         compiler_params=pltpu.CompilerParams(vmem_limit_bytes=VMEM),
         name="collect",

time: 137 us -> 134 us (0.978)
  waiting for transfers between devices: 29.3 us -> 27.1 us
    all_to_all x2, waiting for transfers between devices: 19.1 us -> 16.9 us  [exchange(): return lax.all_to_all(x, 'seq', split_axis=0, concat_axis=0, tiled=True)]
  transfers between devices with their start and end apart: 10 -> 10, of which waited for: 6 -> 6; matrix products, arithmetic and copies ran while one was open for 9% -> 9% of each run, Pallas kernels for 5% -> 6%
where the time goes in v5:
time: 134 us
  blocking collectives  41.5 us (31%)
  waiting for transfers between devices  27.1 us (20%)
  Pallas kernels  24.1 us (18%)
  starting transfers between devices  19.7 us (15%)
  local copies, waits for them, and re-layouts  11.4 us (9%)
  matrix products  8.72 us (7%)
    all_to_all x1, blocking collectives, exchange(): return lax.all_to_all(x, 'seq', split_axis=0, concat_axis=0, tiled=True)  41.5 us
    all_to_all x2, waiting for transfers between devices, exchange(): return lax.all_to_all(x, 'seq', split_axis=0, concat_axis=0, tiled=True)  16.9 us
    ppermute x8, starting transfers between devices, swap(): return lax.ppermute(x, 'bkt', [(i, i ^ mask) for i in range(4)])  10.9 us
    ppermute x8, waiting for transfers between devices, swap(): return lax.ppermute(x, 'bkt', [(i, i ^ mask) for i in range(4)])  10.2 us
    transpose x1, local copies, waits for them, and re-layouts, per_device(): weights[i * width:(i + 1) * width].transpose(1, 0, 2)  9.38 us
    all_to_all x2, starting transfers between devices, exchange(): return lax.all_to_all(x, 'seq', split_axis=0, concat_axis=0, tiled=True)  8.78 us
    pallas_call x1, Pallas kernels, between(): pl.pallas_call(between_kernel, grid=(HH,), out_shape=(pltpu.HBM((HH, RR,...  7.48 us
    pallas_call x1, Pallas kernels, forward(): pl.pallas_call(forward_kernel, out_shape=tuple((pltpu.HBM(*shape) for sha...  6.13 us
  transfers between devices with their start and end apart: 10, of which 6 were waited for; matrix products, arithmetic and copies ran while one was open for 9% of the time, Pallas kernels for 6%

profile of v5, /device:TPU:0, one launch (start us, length us, event | category | flops | bytes accessed | tf_op | source)
XLA Modules:
  0.0 134.0 jit_solution(1941007441932977192)
XLA Ops:
  0.0 0.0 copy-start
  0.0 1.6 %copy-done = bf16[256,4096]{1,0:T(8,128)(2,1)S(1)} copy-done((bf16[256,4096]{1,0:T(8,128)(2,1)S(1)}, bf16[256,4096]{1,0:T(8,128)(2,1)}, u32[]{:S(2)}) %copy-start) | copy-done | bytes 2097176
  1.6 0.0 copy-start.1
  1.6 0.0 copy-start.3
  1.6 5.7 %fusion.40.proj_ref = bf16[2,256,512]{2,1,0:T(8,128)(2,1)S(1)} fusion(bf16[4096,2,512]{2,1,0:T(2,128)(2,1)} %param.5, bf16[256,4096]{1,0:T(8,128)(2,1)S(1)} %copy-done), kind=kOutput, calls=%fused_computation.24 | convolution fusion | flops 2147745792 | bytes 11010048 | tf_op jit(solution)/shard_map/td,dcf->ctf/dot_general | solution.py:513
  7.4 0.0 copy-done.1
  7.4 0.0 copy-done.3
  7.4 1.7 %dispatch.1 = (s32[8,256]{1,0:T(8,128)S(1)}, bf16[768,1664]{1,0:T(8,128)(2,1)S(1)}) custom-call(s32[1]{0:T(128)} %bitcast.odd_ref, s32[2,4,256]{2,1,0:T(4,128)S(1)} %copy-done.3, bf16[2,256,512]{2,1,0:T(8,128)(2,1)S(1)} %fusion.40.proj_ref, bf16[256,512]{1,0:T(8,128)(2,1)S(1)} %copy-done.1), custom_call_target="tpu_custom_call" | custom-call | tf_op jit(solution)/shard_map/dispatch/pallas_call | solution.py:94
  9.1 41.5 %all_to_all.33 = bf16[32,24,1664]{2,1,0:T(8,128)(2,1)S(1)} all-to-all(bf16[32,24,1664]{2,1,0:T(8,128)(2,1)S(1)} %bitcast.90), channel_id=1, replica_groups=mesh['seq'=32,'bkt'=4] {'seq'}, dimensions={0} | all-to-all | bytes 5111808 | tf_op jit(solution)/shard_map/all_to_all | solution.py:490
  50.6 6.1 %forward.1 = (bf16[4,2,384,384]{3,2,1,0:T(8,128)(2,1)}, bf16[4,2,384,384]{3,2,1,0:T(8,128)(2,1)}, f32[4,2,384,128]{3,2,1,0:T(8,128)}, bf16[512,384]{1,0:T(8,128)(2,1)}, bf16[128,384]{1,0:T(8,128)(2,1)}) custom-call(bf16[768,1664]{1,0:T(8,128)(2,1)S(1)} %bitcast.89), custom_call_target="tpu_custom_call" | custom-call | tf_op jit(solution)/shard_map/forward/pallas_call | solution.py:251
  56.8 4.1 %all-to-all-start.1 = ((bf16[32,16,384]{2,1,0:T(8,128)(2,1)}), bf16[32,16,384]{2,1,0:T(8,128)(2,1)S(1)}, u32[]{:S(2)}, u32[]{:S(2)}) async-start(bf16[32,16,384]{2,1,0:T(8,128)(2,1)} %bitcast.96), calls=%async_computation.1 | async-start | bytes 786432 | tf_op jit(solution)/shard_map/all_to_all | solution.py:490
  60.8 0.0 copy-start.2
  60.8 7.5 %between.1 = (bf16[4,2,384,384]{3,2,1,0:T(8,128)(2,1)}, bf16[4,2,384,384]{3,2,1,0:T(8,128)(2,1)}, bf16[4,2,384,384]{3,2,1,0:T(8,128)(2,1)}) custom-call(bf16[4,2,384,384]{3,2,1,0:T(8,128)(2,1)} %get-tuple-element.21.probs_ref, bf16[4,2,384,384]{3,2,1,0:T(8,128)(2,1)} %get-tuple-element.22.rows_ref, f32[4,2,384,128]{3,2,1,0:T(8,128)} %get-tuple-element.23.self_ref), custom_call_target="tpu_custom_call" | custom-call | flops 905969664 | bytes 12582912 | tf_op jit(solution)/shard_map/between/pallas_call | solution.py:293
  68.3 2.6 %all-to-all-done.1 = bf16[32,16,384]{2,1,0:T(8,128)(2,1)S(1)} async-done(((bf16[32,16,384]{2,1,0:T(8,128)(2,1)}), bf16[32,16,384]{2,1,0:T(8,128)(2,1)S(1)}, u32[]{:S(2)}, u32[]{:S(2)}) %all-to-all-start.1) | async-done | bytes 393248 | tf_op jit(solution)/shard_map/all_to_all | solution.py:490
  71.0 0.0 copy-done.2
  71.0 6.0 %backward.1 = bf16[768,1024]{1,0:T(8,128)(2,1)} custom-call(bf16[4,2,384,384]{3,2,1,0:T(8,128)(2,1)} %get-tuple-element.24.probs_ref, bf16[4,2,384,384]{3,2,1,0:T(8,128)(2,1)} %get-tuple-element.25.weighted_ref, bf16[4,2,384,384]{3,2,1,0:T(8,128)(2,1)} %get-tuple-element.22.rows_ref, bf16[4,2,384,384]{3,2,1,0:T(8,128)(2,1)} %get-tuple-element.26.sums_ref, ...), custom_call_target="tpu_custom_call" | custom-call | tf_op jit(solution)/shard_map/backward/pallas_call | solution.py:433
  77.0 4.7 %all-to-all-start.2 = ((bf16[32,24,1024]{2,1,0:T(8,128)(2,1)}), bf16[32,24,1024]{2,1,0:T(8,128)(2,1)}, u32[]{:S(2)}, u32[]{:S(2)}) async-start(bf16[32,24,1024]{2,1,0:T(8,128)(2,1)} %bitcast.93), calls=%async_computation.2 | async-start | bytes 3145728 | tf_op jit(solution)/shard_map/all_to_all | solution.py:490
  81.7 0.1 constant_dynamic-slice_fusion.3
  81.8 0.1 pad_add_fusion
  81.9 0.1 copy.17
  82.0 9.4 %slice_bitcast_fusion = (bf16[2,1024,512]{2,0,1:T(2,128)(2,1)}, bf16[2,1024,512]{2,0,1:T(2,128)(2,1)}, bf16[2,1024,512]{2,0,1:T(2,128)(2,1)}, bf16[2,1024,512]{2,0,1:T(2,128)(2,1)}) fusion(bf16[4096,2,512]{2,1,0:T(2,128)(2,1)} %param.5), kind=kLoop, calls=%fused_computation.11 | loop fusion | bytes 16777216 | tf_op jit(solution)/shard_map/transpose | solution.py:526
  91.4 14.2 %all-to-all-done.2 = bf16[32,24,1024]{2,1,0:T(8,128)(2,1)} async-done(((bf16[32,24,1024]{2,1,0:T(8,128)(2,1)}), bf16[32,24,1024]{2,1,0:T(8,128)(2,1)}, u32[]{:S(2)}, u32[]{:S(2)}) %all-to-all-start.2) | async-done | bytes 1572896 | tf_op jit(solution)/shard_map/all_to_all | solution.py:490
  105.6 0.0 copy-start.7
  105.6 2.7 %collect.1 = bf16[2,256,512]{2,1,0:T(8,128)(2,1)S(1)} custom-call(s32[256,8]{1,0:T(8,128)S(1)} %bitcast.92, bf16[768,1024]{1,0:T(8,128)(2,1)} %bitcast.9.got_ref), custom_call_target="tpu_custom_call" | custom-call | tf_op jit(solution)/shard_map/collect/pallas_call | solution.py:475
  108.4 0.0 copy-done.7
  108.4 0.0 copy-start.6
  108.4 0.7 fusion.37
  109.2 0.0 copy-start.5
  109.2 1.7 %collective-permute-start = (bf16[2,64,1024]{2,1,0:T(8,128)(2,1)S(1)}, bf16[2,64,1024]{2,1,0:T(8,128)(2,1)S(1)}, u32[]{:S(2)}, u32[]{:S(2)}) collective-permute-start(bf16[2,64,1024]{2,1,0:T(8,128)(2,1)S(1)} %bitcast.98), channel_id=1, source_target_pairs={{0,1},{1,0},{2,3},{3,2},{4,5},{5,4},{6,7},{7,6},{8,9},{9,8},{10,11... | collective-permute-start | bytes 786440 | tf_op jit(solution)/shard_map/ppermute | solution.py:504
  110.8 0.0 copy-done.6
  110.8 0.7 fusion.34
  111.7 0.0 copy-start.4
  111.7 2.5 %collective-permute-start.2 = (bf16[2,64,1024]{2,1,0:T(8,128)(2,1)S(1)}, bf16[2,64,1024]{2,1,0:T(8,128)(2,1)S(1)}, u32[]{:S(2)}, u32[]{:S(2)}) collective-permute-start(bf16[2,64,1024]{2,1,0:T(8,128)(2,1)S(1)} %pad_maximum_fusion.1), channel_id=1, source_target_pairs={{0,3},{1,2},{2,1},{3,0},{4,7},{5,6},{6,5},{7,4},{8,11},{9,10},{10,... | collective-permute-start | bytes 786440 | tf_op jit(solution)/shard_map/ppermute | solution.py:504
  114.2 0.0 copy-done.5
  114.2 0.7 fusion.31
  114.9 0.0 copy-done.4
  114.9 0.7 fusion.28
  115.8 1.1 collective-permute-start.6
  116.9 0.1 collective-permute-start.4
  117.1 0.0 collective-permute-done
  117.1 0.1 add.40
  117.2 2.2 %collective-permute-start.1 = (bf16[64,1024]{1,0:T(8,128)(2,1)S(1)}, bf16[64,1024]{1,0:T(8,128)(2,1)S(1)}, u32[]{:S(2)}, u32[]{:S(2)}) collective-permute-start(bf16[64,1024]{1,0:T(8,128)(2,1)S(1)} %slice_bitcast_fusion.18), channel_id=1, source_target_pairs={{0,3},{1,2},{2,1},{3,0},{4,7},{5,6},{6,5},{7,4},{8,11},{9,10},{10,... | collective-permute-start | bytes 393224 | tf_op jit(solution)/shard_map/ppermute | solution.py:504
  119.4 2.0 %collective-permute-done.2 = bf16[2,64,1024]{2,1,0:T(8,128)(2,1)S(1)} collective-permute-done((bf16[2,64,1024]{2,1,0:T(8,128)(2,1)S(1)}, bf16[2,64,1024]{2,1,0:T(8,128)(2,1)S(1)}, u32[]{:S(2)}, u32[]{:S(2)}) %collective-permute-start.2) | collective-permute-done | bytes 262176 | tf_op jit(solution)/shard_map/ppermute | solution.py:504
  121.5 0.7 collective-permute-start.3
  122.2 4.5 %collective-permute-done.6 = bf16[2,64,1024]{2,1,0:T(8,128)(2,1)S(1)} collective-permute-done((bf16[2,64,1024]{2,1,0:T(8,128)(2,1)S(1)}, bf16[2,64,1024]{2,1,0:T(8,128)(2,1)S(1)}, u32[]{:S(2)}, u32[]{:S(2)}) %collective-permute-start.6) | collective-permute-done | bytes 262176 | tf_op jit(solution)/shard_map/ppermute | solution.py:504
  126.7 0.1 collective-permute-start.7
  126.8 0.0 collective-permute-done.4
  126.8 0.1 add.44
  126.9 2.5 %collective-permute-start.5 = (bf16[64,1024]{1,0:T(8,128)(2,1)S(1)}, bf16[64,1024]{1,0:T(8,128)(2,1)S(1)}, u32[]{:S(2)}, u32[]{:S(2)}) collective-permute-start(bf16[64,1024]{1,0:T(8,128)(2,1)S(1)} %slice_bitcast_fusion.10), channel_id=1, source_target_pairs={{0,3},{1,2},{2,1},{3,0},{4,7},{5,6},{6,5},{7,4},{8,11},{9,10},{10,... | collective-permute-start | bytes 393224 | tf_op jit(solution)/shard_map/ppermute | solution.py:504
  129.4 0.0 collective-permute-done.1
  129.4 0.0 collective-permute-done.3
  129.5 2.3 %collective-permute-done.7 = bf16[64,1024]{1,0:T(8,128)(2,1)S(1)} collective-permute-done((bf16[64,1024]{1,0:T(8,128)(2,1)S(1)}, bf16[64,1024]{1,0:T(8,128)(2,1)S(1)}, u32[]{:S(2)}, u32[]{:S(2)}) %collective-permute-start.7) | collective-permute-done | bytes 131104 | tf_op jit(solution)/shard_map/ppermute | solution.py:504
  131.8 1.4 %collective-permute-done.5 = bf16[64,1024]{1,0:T(8,128)(2,1)S(1)} collective-permute-done((bf16[64,1024]{1,0:T(8,128)(2,1)S(1)}, bf16[64,1024]{1,0:T(8,128)(2,1)S(1)}, u32[]{:S(2)}, u32[]{:S(2)}) %collective-permute-start.5) | collective-permute-done | bytes 131104 | tf_op jit(solution)/shard_map/ppermute | solution.py:504
  133.2 0.8 pad_maximum_fusion
  (16 shorter events, 0.4 us)
Async XLA Ops:
  0.0 1.6 %copy-start = (bf16[256,4096]{1,0:T(8,128)(2,1)S(1)}, bf16[256,4096]{1,0:T(8,128)(2,1)}, u32[]{:S(2)}) copy-start(bf16[256,4096]{1,0:T(8,128)(2,1)} %param.4) | copy-start | bytes 6291460
  1.6 5.8 %copy-start.1 = (bf16[256,512]{1,0:T(8,128)(2,1)S(1)}, bf16[256,512]{1,0:T(8,128)(2,1)}, u32[]{:S(2)}) copy-start(bf16[256,512]{1,0:T(8,128)(2,1)} %cot_ref.1) | copy-start | bytes 786436
  1.6 5.8 %copy-start.3 = (s32[2,4,256]{2,1,0:T(4,128)S(1)}, s32[2,4,256]{2,1,0:T(4,128)}, u32[]{:S(2)}) copy-start(s32[2,4,256]{2,1,0:T(4,128)} %buckets_ref.1) | copy-start | bytes 24580
  56.8 14.2 %all-to-all-start.1 = ((bf16[32,16,384]{2,1,0:T(8,128)(2,1)}), bf16[32,16,384]{2,1,0:T(8,128)(2,1)S(1)}, u32[]{:S(2)}, u32[]{:S(2)}) async-start(bf16[32,16,384]{2,1,0:T(8,128)(2,1)} %bitcast.96), calls=%async_computation.1 | async-start | bytes 786432 | tf_op jit(solution)/shard_map/all_to_all | solution.py:490
  60.8 10.1 %copy-start.2 = (bf16[128,384]{1,0:T(8,128)(2,1)S(1)}, bf16[128,384]{1,0:T(8,128)(2,1)}, u32[]{:S(2)}) copy-start(bf16[128,384]{1,0:T(8,128)(2,1)} %get-tuple-element.27.mine_ref) | copy-start | bytes 294916
  77.0 28.6 %all-to-all-start.2 = ((bf16[32,24,1024]{2,1,0:T(8,128)(2,1)}), bf16[32,24,1024]{2,1,0:T(8,128)(2,1)}, u32[]{:S(2)}, u32[]{:S(2)}) async-start(bf16[32,24,1024]{2,1,0:T(8,128)(2,1)} %bitcast.93), calls=%async_computation.2 | async-start | bytes 3145728 | tf_op jit(solution)/shard_map/all_to_all | solution.py:490
  105.6 2.7 %copy-start.7 = (bf16[2,1024,512]{2,0,1:T(2,128)(2,1)S(1)}, bf16[2,1024,512]{2,0,1:T(2,128)(2,1)}, u32[]{:S(2)}) copy-start(bf16[2,1024,512]{2,0,1:T(2,128)(2,1)} %get-tuple-element.29) | copy-start | bytes 6291460
  108.4 2.5 %copy-start.6 = (bf16[2,1024,512]{2,0,1:T(2,128)(2,1)S(1)}, bf16[2,1024,512]{2,0,1:T(2,128)(2,1)}, u32[]{:S(2)}) copy-start(bf16[2,1024,512]{2,0,1:T(2,128)(2,1)} %get-tuple-element.30) | copy-start | bytes 6291460
  109.2 5.0 %copy-start.5 = (bf16[2,1024,512]{2,0,1:T(2,128)(2,1)S(1)}, bf16[2,1024,512]{2,0,1:T(2,128)(2,1)}, u32[]{:S(2)}) copy-start(bf16[2,1024,512]{2,0,1:T(2,128)(2,1)} %get-tuple-element.31) | copy-start | bytes 6291460
  109.2 7.9 %collective-permute-start = (bf16[2,64,1024]{2,1,0:T(8,128)(2,1)S(1)}, bf16[2,64,1024]{2,1,0:T(8,128)(2,1)S(1)}, u32[]{:S(2)}, u32[]{:S(2)}) collective-permute-start(bf16[2,64,1024]{2,1,0:T(8,128)(2,1)S(1)} %bitcast.98), channel_id=1, source_target_pairs={{0,1},{1,0},{2,3},{3,2},{4,5},{5,4},{6,7},{7,6},{8,9},{9,8},{10,11... | collective-permute-start | bytes 786440 | tf_op jit(solution)/shard_map/ppermute | solution.py:504
  111.7 3.2 %copy-start.4 = (bf16[2,1024,512]{2,0,1:T(2,128)(2,1)S(1)}, bf16[2,1024,512]{2,0,1:T(2,128)(2,1)}, u32[]{:S(2)}) copy-start(bf16[2,1024,512]{2,0,1:T(2,128)(2,1)} %get-tuple-element.32) | copy-start | bytes 6291460
  111.7 9.7 %collective-permute-start.2 = (bf16[2,64,1024]{2,1,0:T(8,128)(2,1)S(1)}, bf16[2,64,1024]{2,1,0:T(8,128)(2,1)S(1)}, u32[]{:S(2)}, u32[]{:S(2)}) collective-permute-start(bf16[2,64,1024]{2,1,0:T(8,128)(2,1)S(1)} %pad_maximum_fusion.1), channel_id=1, source_target_pairs={{0,3},{1,2},{2,1},{3,0},{4,7},{5,6},{6,5},{7,4},{8,11},{9,10},{10,... | collective-permute-start | bytes 786440 | tf_op jit(solution)/shard_map/ppermute | solution.py:504
  115.8 10.9 %collective-permute-start.6 = (bf16[2,64,1024]{2,1,0:T(8,128)(2,1)S(1)}, bf16[2,64,1024]{2,1,0:T(8,128)(2,1)S(1)}, u32[]{:S(2)}, u32[]{:S(2)}) collective-permute-start(bf16[2,64,1024]{2,1,0:T(8,128)(2,1)S(1)} %pad_maximum_fusion.2), channel_id=1, source_target_pairs={{0,3},{1,2},{2,1},{3,0},{4,7},{5,6},{6,5},{7,4},{8,11},{9,10},{10,... | collective-permute-start | bytes 786440 | tf_op jit(solution)/shard_map/ppermute | solution.py:504
  116.9 9.9 %collective-permute-start.4 = (bf16[2,64,1024]{2,1,0:T(8,128)(2,1)S(1)}, bf16[2,64,1024]{2,1,0:T(8,128)(2,1)S(1)}, u32[]{:S(2)}, u32[]{:S(2)}) collective-permute-start(bf16[2,64,1024]{2,1,0:T(8,128)(2,1)S(1)} %bitcast.97), channel_id=1, source_target_pairs={{0,1},{1,0},{2,3},{3,2},{4,5},{5,4},{6,7},{7,6},{8,9},{9,8},{10,11... | collective-permute-start | bytes 786440 | tf_op jit(solution)/shard_map/ppermute | solution.py:504
  117.2 12.2 %collective-permute-start.1 = (bf16[64,1024]{1,0:T(8,128)(2,1)S(1)}, bf16[64,1024]{1,0:T(8,128)(2,1)S(1)}, u32[]{:S(2)}, u32[]{:S(2)}) collective-permute-start(bf16[64,1024]{1,0:T(8,128)(2,1)S(1)} %slice_bitcast_fusion.18), channel_id=1, source_target_pairs={{0,3},{1,2},{2,1},{3,0},{4,7},{5,6},{6,5},{7,4},{8,11},{9,10},{10,... | collective-permute-start | bytes 393224 | tf_op jit(solution)/shard_map/ppermute | solution.py:504
  121.5 8.0 %collective-permute-start.3 = (bf16[64,1024]{1,0:T(8,128)(2,1)S(1)}, bf16[64,1024]{1,0:T(8,128)(2,1)S(1)}, u32[]{:S(2)}, u32[]{:S(2)}) collective-permute-start(bf16[64,1024]{1,0:T(8,128)(2,1)S(1)} %slice_bitcast_fusion.12), channel_id=1, source_target_pairs={{0,1},{1,0},{2,3},{3,2},{4,5},{5,4},{6,7},{7,6},{8,9},{9,8},{10,11... | collective-permute-start | bytes 393224 | tf_op jit(solution)/shard_map/ppermute | solution.py:504
  126.7 5.0 %collective-permute-start.7 = (bf16[64,1024]{1,0:T(8,128)(2,1)S(1)}, bf16[64,1024]{1,0:T(8,128)(2,1)S(1)}, u32[]{:S(2)}, u32[]{:S(2)}) collective-permute-start(bf16[64,1024]{1,0:T(8,128)(2,1)S(1)} %slice_bitcast_fusion.4), channel_id=1, source_target_pairs={{0,1},{1,0},{2,3},{3,2},{4,5},{5,4},{6,7},{7,6},{8,9},{9,8},{10,11... | collective-permute-start | bytes 393224 | tf_op jit(solution)/shard_map/ppermute | solution.py:504
  126.9 6.3 %collective-permute-start.5 = (bf16[64,1024]{1,0:T(8,128)(2,1)S(1)}, bf16[64,1024]{1,0:T(8,128)(2,1)S(1)}, u32[]{:S(2)}, u32[]{:S(2)}) collective-permute-start(bf16[64,1024]{1,0:T(8,128)(2,1)S(1)} %slice_bitcast_fusion.10), channel_id=1, source_target_pairs={{0,3},{1,2},{2,1},{3,0},{4,7},{5,6},{6,5},{7,4},{8,11},{9,10},{10,... | collective-permute-start | bytes 393224 | tf_op jit(solution)/shard_map/ppermute | solution.py:504

commit v6 on v5

--- a/solution.py
+++ b/solution.py
@@ -308,7 +308,7 @@
 
 def round_shares(mine_ref, got_ref, got, put):
     for at in range(SLOTS // HS):
-        got[at] = got_ref[:, pl.ds(at * HS, HS)].astype(F32)
+        got[at, : NO * 2 * ITEMS] = got_ref[:, pl.ds(at * HS, HS)].astype(F32)
     mine = mine_ref[...].astype(F32)
     owner_ids = iota((3 * NO, SLOTS), 0)
     slot_ids = iota((HS, SLOTS), 0)
@@ -442,7 +442,7 @@
             pltpu.VMEM((HH, RR, SLOTS, HS), BF),
             pltpu.VMEM((HH, RR, SLOTS, 3 * HS), BF),
             pltpu.VMEM((HH, ROWS, 2 * HS), BF),
-            pltpu.VMEM((SLOTS // HS, NO * 2 * ITEMS, HS), F32),
+            pltpu.VMEM((SLOTS // HS, (NO + 1) * 2 * ITEMS, HS), F32),
             pltpu.VMEM((HH, RR, SLOTS, 2 * HS), F32),
             pltpu.SemaphoreType.DMA((6 * HH,)),
         ],
@@ -451,39 +451,27 @@
     )(pinned(probs), pinned(weighted), pinned(rows), pinned(sums), mine, got)
 
 
-def collect_kernel(rows_ref, got_ref, out_ref, got, sems):
-    loads = []
-    for at in range(3):
-        part = pl.ds(at * (ROWS // 3), ROWS // 3)
-        loads.append(pltpu.make_async_copy(got_ref.at[part], got.at[part], sems.at[at]))
-        loads[at].start()
+def collect_kernel(rows_ref, got_ref, out_ref):
     row_ids = iota((TT, ROWS), 1)
-    hots = []
     for h in range(HH):
         first = row_ids == rows_ref[:, h : h + 1]
         second = row_ids == rows_ref[:, HH + h : HH + h + 1]
-        hots.append((first | second).astype(BF))
-    for copy in loads:
-        copy.wait()
-    for h in range(HH):
-        sums = dot(hots[h], got[:, pl.ds(h * 2 * HS, 2 * HS)]).astype(BF)
+        hot = (first | second).astype(BF)
+        sums = dot(hot, got_ref[:, pl.ds(h * 2 * HS, 2 * HS)]).astype(BF)
         out_ref[0, :, pl.ds(h * HS, HS)] = sums[:, :HS]
         out_ref[1, :, pl.ds(h * HS, HS)] = sums[:, HS:]
 
 
 def collect(rows, got):
+    vmem = pl.BlockSpec(memory_space=pltpu.VMEM)
     return pl.pallas_call(
         collect_kernel,
         out_shape=jax.ShapeDtypeStruct((2, TT, HH * HS), BF),
-        in_specs=[pl.BlockSpec(memory_space=pltpu.VMEM), pl.BlockSpec(memory_space=pl.ANY)],
-        out_specs=pl.BlockSpec(memory_space=pltpu.VMEM),
-        scratch_shapes=[
-            pltpu.VMEM((ROWS, HH * 2 * HS), BF),
-            pltpu.SemaphoreType.DMA((3,)),
-        ],
-        compiler_params=pltpu.CompilerParams(vmem_limit_bytes=VMEM),
+        in_specs=[vmem, vmem],
+        out_specs=vmem,
+        compiler_params=pltpu.CompilerParams(vmem_limit_bytes=12 * 1024 * 1024),
         name="collect",
-    )(rows, pinned(got))
+    )(rows, got)
 
 
 def exchange(x):

time: 134 us -> 134 us (level)
  no operation moved by 1% of the time
where the time goes in v6:
time: 134 us
  blocking collectives  41.5 us (31%)
  waiting for transfers between devices  27.1 us (20%)
  Pallas kernels  23.9 us (18%)
  starting transfers between devices  19.7 us (15%)
  local copies, waits for them, and re-layouts  11.4 us (9%)
  matrix products  8.73 us (7%)
    all_to_all x1, blocking collectives, exchange(): return lax.all_to_all(x, 'seq', split_axis=0, concat_axis=0, tiled=True)  41.5 us
    all_to_all x2, waiting for transfers between devices, exchange(): return lax.all_to_all(x, 'seq', split_axis=0, concat_axis=0, tiled=True)  16.9 us
    ppermute x8, starting transfers between devices, swap(): return lax.ppermute(x, 'bkt', [(i, i ^ mask) for i in range(4)])  10.9 us
    ppermute x8, waiting for transfers between devices, swap(): return lax.ppermute(x, 'bkt', [(i, i ^ mask) for i in range(4)])  10.2 us
    transpose x1, local copies, waits for them, and re-layouts, per_device(): weights[i * width:(i + 1) * width].transpose(1, 0, 2)  9.38 us
    all_to_all x2, starting transfers between devices, exchange(): return lax.all_to_all(x, 'seq', split_axis=0, concat_axis=0, tiled=True)  8.78 us
    pallas_call x1, Pallas kernels, between(): pl.pallas_call(between_kernel, grid=(HH,), out_shape=(pltpu.HBM((HH, RR,...  7.48 us
    pallas_call x1, Pallas kernels, forward(): pl.pallas_call(forward_kernel, out_shape=tuple((pltpu.HBM(*shape) for sha...  6.13 us
  transfers between devices with their start and end apart: 10, of which 6 were waited for; matrix products, arithmetic and copies ran while one was open for 9% of the time, Pallas kernels for 6%

profile of v6, /device:TPU:0, one launch (start us, length us, event | category | flops | bytes accessed | tf_op | source)
XLA Modules:
  0.0 133.9 jit_solution(12332230646927615077)
XLA Ops:
  0.0 0.0 copy-start
  0.0 1.6 %copy-done = bf16[256,4096]{1,0:T(8,128)(2,1)S(1)} copy-done((bf16[256,4096]{1,0:T(8,128)(2,1)S(1)}, bf16[256,4096]{1,0:T(8,128)(2,1)}, u32[]{:S(2)}) %copy-start) | copy-done | bytes 2097176
  1.6 0.0 copy-start.1
  1.6 0.0 copy-start.3
  1.6 5.7 %fusion.40.proj_ref = bf16[2,256,512]{2,1,0:T(8,128)(2,1)S(1)} fusion(bf16[4096,2,512]{2,1,0:T(2,128)(2,1)} %param.5, bf16[256,4096]{1,0:T(8,128)(2,1)S(1)} %copy-done), kind=kOutput, calls=%fused_computation.24 | convolution fusion | flops 2147745792 | bytes 11010048 | tf_op jit(solution)/shard_map/td,dcf->ctf/dot_general | solution.py:501
  7.4 0.0 copy-done.1
  7.4 0.0 copy-done.3
  7.4 1.7 %dispatch.1 = (s32[8,256]{1,0:T(8,128)S(1)}, bf16[768,1664]{1,0:T(8,128)(2,1)S(1)}) custom-call(s32[1]{0:T(128)} %bitcast.odd_ref, s32[2,4,256]{2,1,0:T(4,128)S(1)} %copy-done.3, bf16[2,256,512]{2,1,0:T(8,128)(2,1)S(1)} %fusion.40.proj_ref, bf16[256,512]{1,0:T(8,128)(2,1)S(1)} %copy-done.1), custom_call_target="tpu_custom_call" | custom-call | tf_op jit(solution)/shard_map/dispatch/pallas_call | solution.py:94
  9.1 41.5 %all_to_all.33 = bf16[32,24,1664]{2,1,0:T(8,128)(2,1)S(1)} all-to-all(bf16[32,24,1664]{2,1,0:T(8,128)(2,1)S(1)} %bitcast.90), channel_id=1, replica_groups=mesh['seq'=32,'bkt'=4] {'seq'}, dimensions={0} | all-to-all | bytes 5111808 | tf_op jit(solution)/shard_map/all_to_all | solution.py:478
  50.6 6.1 %forward.1 = (bf16[4,2,384,384]{3,2,1,0:T(8,128)(2,1)}, bf16[4,2,384,384]{3,2,1,0:T(8,128)(2,1)}, f32[4,2,384,128]{3,2,1,0:T(8,128)}, bf16[512,384]{1,0:T(8,128)(2,1)}, bf16[128,384]{1,0:T(8,128)(2,1)}) custom-call(bf16[768,1664]{1,0:T(8,128)(2,1)S(1)} %bitcast.89), custom_call_target="tpu_custom_call" | custom-call | tf_op jit(solution)/shard_map/forward/pallas_call | solution.py:251
  56.8 4.1 %all-to-all-start.1 = ((bf16[32,16,384]{2,1,0:T(8,128)(2,1)}), bf16[32,16,384]{2,1,0:T(8,128)(2,1)S(1)}, u32[]{:S(2)}, u32[]{:S(2)}) async-start(bf16[32,16,384]{2,1,0:T(8,128)(2,1)} %bitcast.96), calls=%async_computation.1 | async-start | bytes 786432 | tf_op jit(solution)/shard_map/all_to_all | solution.py:478
  60.8 0.0 copy-start.2
  60.8 7.5 %between.1 = (bf16[4,2,384,384]{3,2,1,0:T(8,128)(2,1)}, bf16[4,2,384,384]{3,2,1,0:T(8,128)(2,1)}, bf16[4,2,384,384]{3,2,1,0:T(8,128)(2,1)}) custom-call(bf16[4,2,384,384]{3,2,1,0:T(8,128)(2,1)} %get-tuple-element.21.probs_ref, bf16[4,2,384,384]{3,2,1,0:T(8,128)(2,1)} %get-tuple-element.22.rows_ref, f32[4,2,384,128]{3,2,1,0:T(8,128)} %get-tuple-element.23.self_ref), custom_call_target="tpu_custom_call" | custom-call | flops 905969664 | bytes 12582912 | tf_op jit(solution)/shard_map/between/pallas_call | solution.py:293
  68.3 2.6 %all-to-all-done.1 = bf16[32,16,384]{2,1,0:T(8,128)(2,1)S(1)} async-done(((bf16[32,16,384]{2,1,0:T(8,128)(2,1)}), bf16[32,16,384]{2,1,0:T(8,128)(2,1)S(1)}, u32[]{:S(2)}, u32[]{:S(2)}) %all-to-all-start.1) | async-done | bytes 393248 | tf_op jit(solution)/shard_map/all_to_all | solution.py:478
  71.0 0.0 copy-done.2
  71.0 6.0 %backward.1 = bf16[768,1024]{1,0:T(8,128)(2,1)} custom-call(bf16[4,2,384,384]{3,2,1,0:T(8,128)(2,1)} %get-tuple-element.24.probs_ref, bf16[4,2,384,384]{3,2,1,0:T(8,128)(2,1)} %get-tuple-element.25.weighted_ref, bf16[4,2,384,384]{3,2,1,0:T(8,128)(2,1)} %get-tuple-element.22.rows_ref, bf16[4,2,384,384]{3,2,1,0:T(8,128)(2,1)} %get-tuple-element.26.sums_ref, ...), custom_call_target="tpu_custom_call" | custom-call | tf_op jit(solution)/shard_map/backward/pallas_call | solution.py:433
  77.0 4.7 %all-to-all-start.2 = ((bf16[32,24,1024]{2,1,0:T(8,128)(2,1)}), bf16[32,24,1024]{2,1,0:T(8,128)(2,1)}, u32[]{:S(2)}, u32[]{:S(2)}) async-start(bf16[32,24,1024]{2,1,0:T(8,128)(2,1)} %bitcast.93), calls=%async_computation.2 | async-start | bytes 3145728 | tf_op jit(solution)/shard_map/all_to_all | solution.py:478
  81.7 0.1 constant_dynamic-slice_fusion.3
  81.8 0.1 pad_add_fusion
  81.9 0.1 copy.17
  82.0 9.4 %slice_bitcast_fusion = (bf16[2,1024,512]{2,0,1:T(2,128)(2,1)}, bf16[2,1024,512]{2,0,1:T(2,128)(2,1)}, bf16[2,1024,512]{2,0,1:T(2,128)(2,1)}, bf16[2,1024,512]{2,0,1:T(2,128)(2,1)}) fusion(bf16[4096,2,512]{2,1,0:T(2,128)(2,1)} %param.5), kind=kLoop, calls=%fused_computation.11 | loop fusion | bytes 16777216 | tf_op jit(solution)/shard_map/transpose | solution.py:514
  91.4 14.2 %all-to-all-done.2 = bf16[32,24,1024]{2,1,0:T(8,128)(2,1)} async-done(((bf16[32,24,1024]{2,1,0:T(8,128)(2,1)}), bf16[32,24,1024]{2,1,0:T(8,128)(2,1)}, u32[]{:S(2)}, u32[]{:S(2)}) %all-to-all-start.2) | async-done | bytes 1572896 | tf_op jit(solution)/shard_map/all_to_all | solution.py:478
  105.6 0.0 copy-start.7
  105.6 2.5 %collect.1 = bf16[2,256,512]{2,1,0:T(8,128)(2,1)S(1)} custom-call(s32[256,8]{1,0:T(8,128)S(1)} %bitcast.92, bf16[768,1024]{1,0:T(8,128)(2,1)} %bitcast.9.got_ref), custom_call_target="tpu_custom_call" | custom-call | tf_op jit(solution)/shard_map/collect/pallas_call | solution.py:467
  108.2 0.0 copy-done.7
  108.2 0.0 copy-start.6
  108.2 0.7 fusion.37
  109.0 0.0 copy-start.5
  109.0 1.7 %collective-permute-start = (bf16[2,64,1024]{2,1,0:T(8,128)(2,1)S(1)}, bf16[2,64,1024]{2,1,0:T(8,128)(2,1)S(1)}, u32[]{:S(2)}, u32[]{:S(2)}) collective-permute-start(bf16[2,64,1024]{2,1,0:T(8,128)(2,1)S(1)} %bitcast.98), channel_id=1, source_target_pairs={{0,1},{1,0},{2,3},{3,2},{4,5},{5,4},{6,7},{7,6},{8,9},{9,8},{10,11... | collective-permute-start | bytes 786440 | tf_op jit(solution)/shard_map/ppermute | solution.py:492
  110.7 0.0 copy-done.6
  110.7 0.7 fusion.34
  111.5 0.0 copy-start.4
  111.5 2.5 %collective-permute-start.2 = (bf16[2,64,1024]{2,1,0:T(8,128)(2,1)S(1)}, bf16[2,64,1024]{2,1,0:T(8,128)(2,1)S(1)}, u32[]{:S(2)}, u32[]{:S(2)}) collective-permute-start(bf16[2,64,1024]{2,1,0:T(8,128)(2,1)S(1)} %pad_maximum_fusion.1), channel_id=1, source_target_pairs={{0,3},{1,2},{2,1},{3,0},{4,7},{5,6},{6,5},{7,4},{8,11},{9,10},{10,... | collective-permute-start | bytes 786440 | tf_op jit(solution)/shard_map/ppermute | solution.py:492
  114.0 0.0 copy-done.5
  114.0 0.7 fusion.31
  114.7 0.0 copy-done.4
  114.8 0.7 fusion.28
  115.6 1.1 collective-permute-start.6
  116.8 0.1 collective-permute-start.4
  116.9 0.0 collective-permute-done
  116.9 0.1 add.40
  117.0 2.2 %collective-permute-start.1 = (bf16[64,1024]{1,0:T(8,128)(2,1)S(1)}, bf16[64,1024]{1,0:T(8,128)(2,1)S(1)}, u32[]{:S(2)}, u32[]{:S(2)}) collective-permute-start(bf16[64,1024]{1,0:T(8,128)(2,1)S(1)} %slice_bitcast_fusion.18), channel_id=1, source_target_pairs={{0,3},{1,2},{2,1},{3,0},{4,7},{5,6},{6,5},{7,4},{8,11},{9,10},{10,... | collective-permute-start | bytes 393224 | tf_op jit(solution)/shard_map/ppermute | solution.py:492
  119.2 2.0 %collective-permute-done.2 = bf16[2,64,1024]{2,1,0:T(8,128)(2,1)S(1)} collective-permute-done((bf16[2,64,1024]{2,1,0:T(8,128)(2,1)S(1)}, bf16[2,64,1024]{2,1,0:T(8,128)(2,1)S(1)}, u32[]{:S(2)}, u32[]{:S(2)}) %collective-permute-start.2) | collective-permute-done | bytes 262176 | tf_op jit(solution)/shard_map/ppermute | solution.py:492
  121.3 0.7 collective-permute-start.3
  122.0 4.5 %collective-permute-done.6 = bf16[2,64,1024]{2,1,0:T(8,128)(2,1)S(1)} collective-permute-done((bf16[2,64,1024]{2,1,0:T(8,128)(2,1)S(1)}, bf16[2,64,1024]{2,1,0:T(8,128)(2,1)S(1)}, u32[]{:S(2)}, u32[]{:S(2)}) %collective-permute-start.6) | collective-permute-done | bytes 262176 | tf_op jit(solution)/shard_map/ppermute | solution.py:492
  126.6 0.1 collective-permute-start.7
  126.6 0.0 collective-permute-done.4
  126.7 0.1 add.44
  126.8 2.5 %collective-permute-start.5 = (bf16[64,1024]{1,0:T(8,128)(2,1)S(1)}, bf16[64,1024]{1,0:T(8,128)(2,1)S(1)}, u32[]{:S(2)}, u32[]{:S(2)}) collective-permute-start(bf16[64,1024]{1,0:T(8,128)(2,1)S(1)} %slice_bitcast_fusion.10), channel_id=1, source_target_pairs={{0,3},{1,2},{2,1},{3,0},{4,7},{5,6},{6,5},{7,4},{8,11},{9,10},{10,... | collective-permute-start | bytes 393224 | tf_op jit(solution)/shard_map/ppermute | solution.py:492
  129.2 0.0 collective-permute-done.1
  129.3 0.0 collective-permute-done.3
  129.3 2.3 %collective-permute-done.7 = bf16[64,1024]{1,0:T(8,128)(2,1)S(1)} collective-permute-done((bf16[64,1024]{1,0:T(8,128)(2,1)S(1)}, bf16[64,1024]{1,0:T(8,128)(2,1)S(1)}, u32[]{:S(2)}, u32[]{:S(2)}) %collective-permute-start.7) | collective-permute-done | bytes 131104 | tf_op jit(solution)/shard_map/ppermute | solution.py:492
  131.6 1.4 %collective-permute-done.5 = bf16[64,1024]{1,0:T(8,128)(2,1)S(1)} collective-permute-done((bf16[64,1024]{1,0:T(8,128)(2,1)S(1)}, bf16[64,1024]{1,0:T(8,128)(2,1)S(1)}, u32[]{:S(2)}, u32[]{:S(2)}) %collective-permute-start.5) | collective-permute-done | bytes 131104 | tf_op jit(solution)/shard_map/ppermute | solution.py:492
  133.0 0.8 pad_maximum_fusion
  (16 shorter events, 0.4 us)
Async XLA Ops:
  0.0 1.6 %copy-start = (bf16[256,4096]{1,0:T(8,128)(2,1)S(1)}, bf16[256,4096]{1,0:T(8,128)(2,1)}, u32[]{:S(2)}) copy-start(bf16[256,4096]{1,0:T(8,128)(2,1)} %param.4) | copy-start | bytes 6291460
  1.6 5.8 %copy-start.1 = (bf16[256,512]{1,0:T(8,128)(2,1)S(1)}, bf16[256,512]{1,0:T(8,128)(2,1)}, u32[]{:S(2)}) copy-start(bf16[256,512]{1,0:T(8,128)(2,1)} %cot_ref.1) | copy-start | bytes 786436
  1.6 5.8 %copy-start.3 = (s32[2,4,256]{2,1,0:T(4,128)S(1)}, s32[2,4,256]{2,1,0:T(4,128)}, u32[]{:S(2)}) copy-start(s32[2,4,256]{2,1,0:T(4,128)} %buckets_ref.1) | copy-start | bytes 24580
  56.8 14.2 %all-to-all-start.1 = ((bf16[32,16,384]{2,1,0:T(8,128)(2,1)}), bf16[32,16,384]{2,1,0:T(8,128)(2,1)S(1)}, u32[]{:S(2)}, u32[]{:S(2)}) async-start(bf16[32,16,384]{2,1,0:T(8,128)(2,1)} %bitcast.96), calls=%async_computation.1 | async-start | bytes 786432 | tf_op jit(solution)/shard_map/all_to_all | solution.py:478
  60.8 10.1 %copy-start.2 = (bf16[128,384]{1,0:T(8,128)(2,1)S(1)}, bf16[128,384]{1,0:T(8,128)(2,1)}, u32[]{:S(2)}) copy-start(bf16[128,384]{1,0:T(8,128)(2,1)} %get-tuple-element.27.mine_ref) | copy-start | bytes 294916
  77.0 28.6 %all-to-all-start.2 = ((bf16[32,24,1024]{2,1,0:T(8,128)(2,1)}), bf16[32,24,1024]{2,1,0:T(8,128)(2,1)}, u32[]{:S(2)}, u32[]{:S(2)}) async-start(bf16[32,24,1024]{2,1,0:T(8,128)(2,1)} %bitcast.93), calls=%async_computation.2 | async-start | bytes 3145728 | tf_op jit(solution)/shard_map/all_to_all | solution.py:478
  105.6 2.5 %copy-start.7 = (bf16[2,1024,512]{2,0,1:T(2,128)(2,1)S(1)}, bf16[2,1024,512]{2,0,1:T(2,128)(2,1)}, u32[]{:S(2)}) copy-start(bf16[2,1024,512]{2,0,1:T(2,128)(2,1)} %get-tuple-element.29) | copy-start | bytes 6291460
  108.2 2.5 %copy-start.6 = (bf16[2,1024,512]{2,0,1:T(2,128)(2,1)S(1)}, bf16[2,1024,512]{2,0,1:T(2,128)(2,1)}, u32[]{:S(2)}) copy-start(bf16[2,1024,512]{2,0,1:T(2,128)(2,1)} %get-tuple-element.30) | copy-start | bytes 6291460
  109.0 5.0 %copy-start.5 = (bf16[2,1024,512]{2,0,1:T(2,128)(2,1)S(1)}, bf16[2,1024,512]{2,0,1:T(2,128)(2,1)}, u32[]{:S(2)}) copy-start(bf16[2,1024,512]{2,0,1:T(2,128)(2,1)} %get-tuple-element.31) | copy-start | bytes 6291460
  109.0 7.9 %collective-permute-start = (bf16[2,64,1024]{2,1,0:T(8,128)(2,1)S(1)}, bf16[2,64,1024]{2,1,0:T(8,128)(2,1)S(1)}, u32[]{:S(2)}, u32[]{:S(2)}) collective-permute-start(bf16[2,64,1024]{2,1,0:T(8,128)(2,1)S(1)} %bitcast.98), channel_id=1, source_target_pairs={{0,1},{1,0},{2,3},{3,2},{4,5},{5,4},{6,7},{7,6},{8,9},{9,8},{10,11... | collective-permute-start | bytes 786440 | tf_op jit(solution)/shard_map/ppermute | solution.py:492
  111.5 3.2 %copy-start.4 = (bf16[2,1024,512]{2,0,1:T(2,128)(2,1)S(1)}, bf16[2,1024,512]{2,0,1:T(2,128)(2,1)}, u32[]{:S(2)}) copy-start(bf16[2,1024,512]{2,0,1:T(2,128)(2,1)} %get-tuple-element.32) | copy-start | bytes 6291460
  111.5 9.7 %collective-permute-start.2 = (bf16[2,64,1024]{2,1,0:T(8,128)(2,1)S(1)}, bf16[2,64,1024]{2,1,0:T(8,128)(2,1)S(1)}, u32[]{:S(2)}, u32[]{:S(2)}) collective-permute-start(bf16[2,64,1024]{2,1,0:T(8,128)(2,1)S(1)} %pad_maximum_fusion.1), channel_id=1, source_target_pairs={{0,3},{1,2},{2,1},{3,0},{4,7},{5,6},{6,5},{7,4},{8,11},{9,10},{10,... | collective-permute-start | bytes 786440 | tf_op jit(solution)/shard_map/ppermute | solution.py:492
  115.6 10.9 %collective-permute-start.6 = (bf16[2,64,1024]{2,1,0:T(8,128)(2,1)S(1)}, bf16[2,64,1024]{2,1,0:T(8,128)(2,1)S(1)}, u32[]{:S(2)}, u32[]{:S(2)}) collective-permute-start(bf16[2,64,1024]{2,1,0:T(8,128)(2,1)S(1)} %pad_maximum_fusion.2), channel_id=1, source_target_pairs={{0,3},{1,2},{2,1},{3,0},{4,7},{5,6},{6,5},{7,4},{8,11},{9,10},{10,... | collective-permute-start | bytes 786440 | tf_op jit(solution)/shard_map/ppermute | solution.py:492
  116.8 9.9 %collective-permute-start.4 = (bf16[2,64,1024]{2,1,0:T(8,128)(2,1)S(1)}, bf16[2,64,1024]{2,1,0:T(8,128)(2,1)S(1)}, u32[]{:S(2)}, u32[]{:S(2)}) collective-permute-start(bf16[2,64,1024]{2,1,0:T(8,128)(2,1)S(1)} %bitcast.97), channel_id=1, source_target_pairs={{0,1},{1,0},{2,3},{3,2},{4,5},{5,4},{6,7},{7,6},{8,9},{9,8},{10,11... | collective-permute-start | bytes 786440 | tf_op jit(solution)/shard_map/ppermute | solution.py:492
  117.0 12.2 %collective-permute-start.1 = (bf16[64,1024]{1,0:T(8,128)(2,1)S(1)}, bf16[64,1024]{1,0:T(8,128)(2,1)S(1)}, u32[]{:S(2)}, u32[]{:S(2)}) collective-permute-start(bf16[64,1024]{1,0:T(8,128)(2,1)S(1)} %slice_bitcast_fusion.18), channel_id=1, source_target_pairs={{0,3},{1,2},{2,1},{3,0},{4,7},{5,6},{6,5},{7,4},{8,11},{9,10},{10,... | collective-permute-start | bytes 393224 | tf_op jit(solution)/shard_map/ppermute | solution.py:492
  121.3 8.0 %collective-permute-start.3 = (bf16[64,1024]{1,0:T(8,128)(2,1)S(1)}, bf16[64,1024]{1,0:T(8,128)(2,1)S(1)}, u32[]{:S(2)}, u32[]{:S(2)}) collective-permute-start(bf16[64,1024]{1,0:T(8,128)(2,1)S(1)} %slice_bitcast_fusion.12), channel_id=1, source_target_pairs={{0,1},{1,0},{2,3},{3,2},{4,5},{5,4},{6,7},{7,6},{8,9},{9,8},{10,11... | collective-permute-start | bytes 393224 | tf_op jit(solution)/shard_map/ppermute | solution.py:492
  126.6 5.0 %collective-permute-start.7 = (bf16[64,1024]{1,0:T(8,128)(2,1)S(1)}, bf16[64,1024]{1,0:T(8,128)(2,1)S(1)}, u32[]{:S(2)}, u32[]{:S(2)}) collective-permute-start(bf16[64,1024]{1,0:T(8,128)(2,1)S(1)} %slice_bitcast_fusion.4), channel_id=1, source_target_pairs={{0,1},{1,0},{2,3},{3,2},{4,5},{5,4},{6,7},{7,6},{8,9},{9,8},{10,11... | collective-permute-start | bytes 393224 | tf_op jit(solution)/shard_map/ppermute | solution.py:492
  126.8 6.3 %collective-permute-start.5 = (bf16[64,1024]{1,0:T(8,128)(2,1)S(1)}, bf16[64,1024]{1,0:T(8,128)(2,1)S(1)}, u32[]{:S(2)}, u32[]{:S(2)}) collective-permute-start(bf16[64,1024]{1,0:T(8,128)(2,1)S(1)} %slice_bitcast_fusion.10), channel_id=1, source_target_pairs={{0,3},{1,2},{2,1},{3,0},{4,7},{5,6},{6,5},{7,4},{8,11},{9,10},{10,... | collective-permute-start | bytes 393224 | tf_op jit(solution)/shard_map/ppermute | solution.py:492

commit v7 on v6

--- a/solution.py
+++ b/solution.py
@@ -174,10 +174,17 @@
         far[r, :, HS:] = jnp.where(other, 1.0, 0.0).astype(BF)
 
     copies = []
+
+    def send(here, there):
+        copies.append(pltpu.make_async_copy(here, there, sems.at[len(copies)]))
+        copies[-1].start()
+
     for h in range(HH):
         rounds = split_rounds(x_ref[:, pl.ds(h * 3 * HS, 3 * HS)].astype(F32))
         for r in range(RR):
             x = rounds[r].astype(BF)
+            rows[h, r] = x
+            send(rows.at[h, r], rows_ref.at[h, r])
             q = rounds[r][:, :HS]
             u = rounds[r][:, 2 * HS :]
             v_half = x[:, HS : 2 * HS]
@@ -194,6 +201,8 @@
             scores = scores + bias[r]
             top = jnp.maximum(jnp.max(scores, axis=1, keepdims=True), SELF_SCORE / SCALE)
             shifted = jnp.exp2((scores - top) * POWER).astype(BF)
+            probs[h, r] = shifted
+            send(probs.at[h, r], probs_ref.at[h, r])
             own = jnp.exp2((SELF_SCORE / SCALE - top) * POWER)
             both = dot(shifted, jnp.concatenate([v_half, jnp.ones_like(v_half)], axis=1))
             totals = both[:, HS:] + own
@@ -203,22 +212,14 @@
             out = out.astype(BF).astype(F32)
             inner = jnp.sum(u * out, axis=1, keepdims=True)
             lse = top * SCALE + jnp.log(totals)
-            probs[h, r] = shifted
-            rows[h, r] = x
             kept = 0.0
             for at, column in enumerate((own, inner, scale, inverse)):
                 kept = jnp.where(lane == at, column.astype(F32), kept)
             kept_all[h, r] = kept
+            send(kept_all.at[h, r], self_ref.at[h, r])
             at = lane - (r * HH + h) * 2
             sent = jnp.where(at == 0, lse - LSE_SHIFT, spread[r])
             spread[r] = jnp.where(at == 1, inner, sent)
-        for at, (here, there) in enumerate(
-            ((probs, probs_ref), (rows, rows_ref), (kept_all, self_ref))
-        ):
-            copies.append(
-                pltpu.make_async_copy(here.at[h], there.at[h], sems.at[3 * h + at])
-            )
-            copies[-1].start()
 
     total = jnp.zeros((HS, SLOTS), F32)
     for r in range(RR):
@@ -230,12 +231,8 @@
     total = total[: 2 * ITEMS]
     for k in range(NO):
         wire[pl.ds(k * 2 * ITEMS, 2 * ITEMS), :] = total
-    copies += [
-        pltpu.make_async_copy(mine, mine_ref, sems.at[3 * HH]),
-        pltpu.make_async_copy(wire, wire_ref, sems.at[3 * HH + 1]),
-    ]
-    copies[-1].start()
-    copies[-2].start()
+    send(wire, wire_ref)
+    send(mine, mine_ref)
     for copy in copies:
         copy.wait()
 
@@ -258,7 +255,7 @@
             pltpu.VMEM((RR, SLOTS, SLOTS), F32),
             pltpu.VMEM((RR, SLOTS, HS), F32),
             pltpu.VMEM((RR, SLOTS, 2 * HS), BF),
-            pltpu.SemaphoreType.DMA((3 * HH + 2,)),
+            pltpu.SemaphoreType.DMA((3 * ITEMS + 2,)),
         ],
         compiler_params=pltpu.CompilerParams(vmem_limit_bytes=VMEM),
         name="forward",

time: 134 us -> 135 us (level)
  no operation moved by 1% of the time
where the time goes in v7:
time: 135 us; the launch traced here: 134 us
  blocking collectives  41.5 us (31%)
  waiting for transfers between devices  27.1 us (20%)
  Pallas kernels  24.1 us (18%)
  starting transfers between devices  19.7 us (15%)
  local copies, waits for them, and re-layouts  11.4 us (8%)
  matrix products  8.72 us (6%)
    all_to_all x1, blocking collectives, exchange(): return lax.all_to_all(x, 'seq', split_axis=0, concat_axis=0, tiled=True)  41.5 us
    all_to_all x2, waiting for transfers between devices, exchange(): return lax.all_to_all(x, 'seq', split_axis=0, concat_axis=0, tiled=True)  16.9 us
    ppermute x8, starting transfers between devices, swap(): return lax.ppermute(x, 'bkt', [(i, i ^ mask) for i in range(4)])  10.9 us
    ppermute x8, waiting for transfers between devices, swap(): return lax.ppermute(x, 'bkt', [(i, i ^ mask) for i in range(4)])  10.2 us
    transpose x1, local copies, waits for them, and re-layouts, per_device(): weights[i * width:(i + 1) * width].transpose(1, 0, 2)  9.38 us
    all_to_all x2, starting transfers between devices, exchange(): return lax.all_to_all(x, 'seq', split_axis=0, concat_axis=0, tiled=True)  8.78 us
    pallas_call x1, Pallas kernels, between(): pl.pallas_call(between_kernel, grid=(HH,), out_shape=(pltpu.HBM((HH, RR,...  7.48 us
    pallas_call x1, Pallas kernels, forward(): pl.pallas_call(forward_kernel, out_shape=tuple((pltpu.HBM(*shape) for sha...  6.35 us
  transfers between devices with their start and end apart: 10, of which 6 were waited for; matrix products, arithmetic and copies ran while one was open for 9% of the time, Pallas kernels for 6%

profile of v7, /device:TPU:0, one launch (start us, length us, event | category | flops | bytes accessed | tf_op | source)
XLA Modules:
  0.0 134.1 jit_solution(2913720759455829352)
XLA Ops:
  0.0 0.0 copy-start
  0.0 1.6 %copy-done = bf16[256,4096]{1,0:T(8,128)(2,1)S(1)} copy-done((bf16[256,4096]{1,0:T(8,128)(2,1)S(1)}, bf16[256,4096]{1,0:T(8,128)(2,1)}, u32[]{:S(2)}) %copy-start) | copy-done | bytes 2097176
  1.6 0.0 copy-start.1
  1.6 0.0 copy-start.3
  1.6 5.7 %fusion.40.proj_ref = bf16[2,256,512]{2,1,0:T(8,128)(2,1)S(1)} fusion(bf16[4096,2,512]{2,1,0:T(2,128)(2,1)} %param.5, bf16[256,4096]{1,0:T(8,128)(2,1)S(1)} %copy-done), kind=kOutput, calls=%fused_computation.24 | convolution fusion | flops 2147745792 | bytes 11010048 | tf_op jit(solution)/shard_map/td,dcf->ctf/dot_general | solution.py:498
  7.4 0.0 copy-done.1
  7.4 0.0 copy-done.3
  7.4 1.7 %dispatch.1 = (s32[8,256]{1,0:T(8,128)S(1)}, bf16[768,1664]{1,0:T(8,128)(2,1)S(1)}) custom-call(s32[1]{0:T(128)} %bitcast.odd_ref, s32[2,4,256]{2,1,0:T(4,128)S(1)} %copy-done.3, bf16[2,256,512]{2,1,0:T(8,128)(2,1)S(1)} %fusion.40.proj_ref, bf16[256,512]{1,0:T(8,128)(2,1)S(1)} %copy-done.1), custom_call_target="tpu_custom_call" | custom-call | tf_op jit(solution)/shard_map/dispatch/pallas_call | solution.py:94
  9.1 41.5 %all_to_all.33 = bf16[32,24,1664]{2,1,0:T(8,128)(2,1)S(1)} all-to-all(bf16[32,24,1664]{2,1,0:T(8,128)(2,1)S(1)} %bitcast.90), channel_id=1, replica_groups=mesh['seq'=32,'bkt'=4] {'seq'}, dimensions={0} | all-to-all | bytes 5111808 | tf_op jit(solution)/shard_map/all_to_all | solution.py:475
  50.6 6.4 %forward.1 = (bf16[4,2,384,384]{3,2,1,0:T(8,128)(2,1)}, bf16[4,2,384,384]{3,2,1,0:T(8,128)(2,1)}, f32[4,2,384,128]{3,2,1,0:T(8,128)}, bf16[512,384]{1,0:T(8,128)(2,1)}, bf16[128,384]{1,0:T(8,128)(2,1)}) custom-call(bf16[768,1664]{1,0:T(8,128)(2,1)S(1)} %bitcast.89), custom_call_target="tpu_custom_call" | custom-call | tf_op jit(solution)/shard_map/forward/pallas_call | solution.py:248
  57.0 4.1 %all-to-all-start.1 = ((bf16[32,16,384]{2,1,0:T(8,128)(2,1)}), bf16[32,16,384]{2,1,0:T(8,128)(2,1)S(1)}, u32[]{:S(2)}, u32[]{:S(2)}) async-start(bf16[32,16,384]{2,1,0:T(8,128)(2,1)} %bitcast.96), calls=%async_computation.1 | async-start | bytes 786432 | tf_op jit(solution)/shard_map/all_to_all | solution.py:475
  61.1 0.0 copy-start.2
  61.1 7.5 %between.1 = (bf16[4,2,384,384]{3,2,1,0:T(8,128)(2,1)}, bf16[4,2,384,384]{3,2,1,0:T(8,128)(2,1)}, bf16[4,2,384,384]{3,2,1,0:T(8,128)(2,1)}) custom-call(bf16[4,2,384,384]{3,2,1,0:T(8,128)(2,1)} %get-tuple-element.21.probs_ref, bf16[4,2,384,384]{3,2,1,0:T(8,128)(2,1)} %get-tuple-element.22.rows_ref, f32[4,2,384,128]{3,2,1,0:T(8,128)} %get-tuple-element.23.self_ref), custom_call_target="tpu_custom_call" | custom-call | flops 905969664 | bytes 12582912 | tf_op jit(solution)/shard_map/between/pallas_call | solution.py:290
  68.6 2.6 %all-to-all-done.1 = bf16[32,16,384]{2,1,0:T(8,128)(2,1)S(1)} async-done(((bf16[32,16,384]{2,1,0:T(8,128)(2,1)}), bf16[32,16,384]{2,1,0:T(8,128)(2,1)S(1)}, u32[]{:S(2)}, u32[]{:S(2)}) %all-to-all-start.1) | async-done | bytes 393248 | tf_op jit(solution)/shard_map/all_to_all | solution.py:475
  71.2 0.0 copy-done.2
  71.2 6.0 %backward.1 = bf16[768,1024]{1,0:T(8,128)(2,1)} custom-call(bf16[4,2,384,384]{3,2,1,0:T(8,128)(2,1)} %get-tuple-element.24.probs_ref, bf16[4,2,384,384]{3,2,1,0:T(8,128)(2,1)} %get-tuple-element.25.weighted_ref, bf16[4,2,384,384]{3,2,1,0:T(8,128)(2,1)} %get-tuple-element.22.rows_ref, bf16[4,2,384,384]{3,2,1,0:T(8,128)(2,1)} %get-tuple-element.26.sums_ref, ...), custom_call_target="tpu_custom_call" | custom-call | tf_op jit(solution)/shard_map/backward/pallas_call | solution.py:430
  77.2 4.7 %all-to-all-start.2 = ((bf16[32,24,1024]{2,1,0:T(8,128)(2,1)}), bf16[32,24,1024]{2,1,0:T(8,128)(2,1)}, u32[]{:S(2)}, u32[]{:S(2)}) async-start(bf16[32,24,1024]{2,1,0:T(8,128)(2,1)} %bitcast.93), calls=%async_computation.2 | async-start | bytes 3145728 | tf_op jit(solution)/shard_map/all_to_all | solution.py:475
  82.0 0.1 constant_dynamic-slice_fusion.3
  82.0 0.1 pad_add_fusion
  82.1 0.1 copy.17
  82.2 9.4 %slice_bitcast_fusion = (bf16[2,1024,512]{2,0,1:T(2,128)(2,1)}, bf16[2,1024,512]{2,0,1:T(2,128)(2,1)}, bf16[2,1024,512]{2,0,1:T(2,128)(2,1)}, bf16[2,1024,512]{2,0,1:T(2,128)(2,1)}) fusion(bf16[4096,2,512]{2,1,0:T(2,128)(2,1)} %param.5), kind=kLoop, calls=%fused_computation.11 | loop fusion | bytes 16777216 | tf_op jit(solution)/shard_map/transpose | solution.py:511
  91.6 14.2 %all-to-all-done.2 = bf16[32,24,1024]{2,1,0:T(8,128)(2,1)} async-done(((bf16[32,24,1024]{2,1,0:T(8,128)(2,1)}), bf16[32,24,1024]{2,1,0:T(8,128)(2,1)}, u32[]{:S(2)}, u32[]{:S(2)}) %all-to-all-start.2) | async-done | bytes 1572896 | tf_op jit(solution)/shard_map/all_to_all | solution.py:475
  105.9 0.0 copy-start.7
  105.9 2.5 %collect.1 = bf16[2,256,512]{2,1,0:T(8,128)(2,1)S(1)} custom-call(s32[256,8]{1,0:T(8,128)S(1)} %bitcast.92, bf16[768,1024]{1,0:T(8,128)(2,1)} %bitcast.9.got_ref), custom_call_target="tpu_custom_call" | custom-call | tf_op jit(solution)/shard_map/collect/pallas_call | solution.py:464
  108.4 0.0 copy-done.7
  108.4 0.0 copy-start.6
  108.4 0.7 fusion.37
  109.2 0.0 copy-start.5
  109.2 1.7 %collective-permute-start = (bf16[2,64,1024]{2,1,0:T(8,128)(2,1)S(1)}, bf16[2,64,1024]{2,1,0:T(8,128)(2,1)S(1)}, u32[]{:S(2)}, u32[]{:S(2)}) collective-permute-start(bf16[2,64,1024]{2,1,0:T(8,128)(2,1)S(1)} %bitcast.98), channel_id=1, source_target_pairs={{0,1},{1,0},{2,3},{3,2},{4,5},{5,4},{6,7},{7,6},{8,9},{9,8},{10,11... | collective-permute-start | bytes 786440 | tf_op jit(solution)/shard_map/ppermute | solution.py:489
  110.9 0.0 copy-done.6
  110.9 0.7 fusion.34
  111.7 0.0 copy-start.4
  111.7 2.5 %collective-permute-start.2 = (bf16[2,64,1024]{2,1,0:T(8,128)(2,1)S(1)}, bf16[2,64,1024]{2,1,0:T(8,128)(2,1)S(1)}, u32[]{:S(2)}, u32[]{:S(2)}) collective-permute-start(bf16[2,64,1024]{2,1,0:T(8,128)(2,1)S(1)} %pad_maximum_fusion.1), channel_id=1, source_target_pairs={{0,3},{1,2},{2,1},{3,0},{4,7},{5,6},{6,5},{7,4},{8,11},{9,10},{10,... | collective-permute-start | bytes 786440 | tf_op jit(solution)/shard_map/ppermute | solution.py:489
  114.2 0.0 copy-done.5
  114.2 0.7 fusion.31
  115.0 0.0 copy-done.4
  115.0 0.7 fusion.28
  115.8 1.1 collective-permute-start.6
  117.0 0.1 collective-permute-start.4
  117.1 0.0 collective-permute-done
  117.1 0.1 add.40
  117.2 2.2 %collective-permute-start.1 = (bf16[64,1024]{1,0:T(8,128)(2,1)S(1)}, bf16[64,1024]{1,0:T(8,128)(2,1)S(1)}, u32[]{:S(2)}, u32[]{:S(2)}) collective-permute-start(bf16[64,1024]{1,0:T(8,128)(2,1)S(1)} %slice_bitcast_fusion.18), channel_id=1, source_target_pairs={{0,3},{1,2},{2,1},{3,0},{4,7},{5,6},{6,5},{7,4},{8,11},{9,10},{10,... | collective-permute-start | bytes 393224 | tf_op jit(solution)/shard_map/ppermute | solution.py:489
  119.4 2.0 %collective-permute-done.2 = bf16[2,64,1024]{2,1,0:T(8,128)(2,1)S(1)} collective-permute-done((bf16[2,64,1024]{2,1,0:T(8,128)(2,1)S(1)}, bf16[2,64,1024]{2,1,0:T(8,128)(2,1)S(1)}, u32[]{:S(2)}, u32[]{:S(2)}) %collective-permute-start.2) | collective-permute-done | bytes 262176 | tf_op jit(solution)/shard_map/ppermute | solution.py:489
  121.5 0.7 collective-permute-start.3
  122.2 4.5 %collective-permute-done.6 = bf16[2,64,1024]{2,1,0:T(8,128)(2,1)S(1)} collective-permute-done((bf16[2,64,1024]{2,1,0:T(8,128)(2,1)S(1)}, bf16[2,64,1024]{2,1,0:T(8,128)(2,1)S(1)}, u32[]{:S(2)}, u32[]{:S(2)}) %collective-permute-start.6) | collective-permute-done | bytes 262176 | tf_op jit(solution)/shard_map/ppermute | solution.py:489
  126.8 0.1 collective-permute-start.7
  126.9 0.0 collective-permute-done.4
  126.9 0.1 add.44
  127.0 2.5 %collective-permute-start.5 = (bf16[64,1024]{1,0:T(8,128)(2,1)S(1)}, bf16[64,1024]{1,0:T(8,128)(2,1)S(1)}, u32[]{:S(2)}, u32[]{:S(2)}) collective-permute-start(bf16[64,1024]{1,0:T(8,128)(2,1)S(1)} %slice_bitcast_fusion.10), channel_id=1, source_target_pairs={{0,3},{1,2},{2,1},{3,0},{4,7},{5,6},{6,5},{7,4},{8,11},{9,10},{10,... | collective-permute-start | bytes 393224 | tf_op jit(solution)/shard_map/ppermute | solution.py:489
  129.5 0.0 collective-permute-done.1
  129.5 0.0 collective-permute-done.3
  129.5 2.3 %collective-permute-done.7 = bf16[64,1024]{1,0:T(8,128)(2,1)S(1)} collective-permute-done((bf16[64,1024]{1,0:T(8,128)(2,1)S(1)}, bf16[64,1024]{1,0:T(8,128)(2,1)S(1)}, u32[]{:S(2)}, u32[]{:S(2)}) %collective-permute-start.7) | collective-permute-done | bytes 131104 | tf_op jit(solution)/shard_map/ppermute | solution.py:489
  131.8 1.4 %collective-permute-done.5 = bf16[64,1024]{1,0:T(8,128)(2,1)S(1)} collective-permute-done((bf16[64,1024]{1,0:T(8,128)(2,1)S(1)}, bf16[64,1024]{1,0:T(8,128)(2,1)S(1)}, u32[]{:S(2)}, u32[]{:S(2)}) %collective-permute-start.5) | collective-permute-done | bytes 131104 | tf_op jit(solution)/shard_map/ppermute | solution.py:489
  133.2 0.8 pad_maximum_fusion
  (16 shorter events, 0.4 us)
Async XLA Ops:
  0.0 1.6 %copy-start = (bf16[256,4096]{1,0:T(8,128)(2,1)S(1)}, bf16[256,4096]{1,0:T(8,128)(2,1)}, u32[]{:S(2)}) copy-start(bf16[256,4096]{1,0:T(8,128)(2,1)} %param.4) | copy-start | bytes 6291460
  1.6 5.8 %copy-start.1 = (bf16[256,512]{1,0:T(8,128)(2,1)S(1)}, bf16[256,512]{1,0:T(8,128)(2,1)}, u32[]{:S(2)}) copy-start(bf16[256,512]{1,0:T(8,128)(2,1)} %cot_ref.1) | copy-start | bytes 786436
  1.6 5.8 %copy-start.3 = (s32[2,4,256]{2,1,0:T(4,128)S(1)}, s32[2,4,256]{2,1,0:T(4,128)}, u32[]{:S(2)}) copy-start(s32[2,4,256]{2,1,0:T(4,128)} %buckets_ref.1) | copy-start | bytes 24580
  57.0 14.2 %all-to-all-start.1 = ((bf16[32,16,384]{2,1,0:T(8,128)(2,1)}), bf16[32,16,384]{2,1,0:T(8,128)(2,1)S(1)}, u32[]{:S(2)}, u32[]{:S(2)}) async-start(bf16[32,16,384]{2,1,0:T(8,128)(2,1)} %bitcast.96), calls=%async_computation.1 | async-start | bytes 786432 | tf_op jit(solution)/shard_map/all_to_all | solution.py:475
  61.1 10.1 %copy-start.2 = (bf16[128,384]{1,0:T(8,128)(2,1)S(1)}, bf16[128,384]{1,0:T(8,128)(2,1)}, u32[]{:S(2)}) copy-start(bf16[128,384]{1,0:T(8,128)(2,1)} %get-tuple-element.27.mine_ref) | copy-start | bytes 294916
  77.2 28.6 %all-to-all-start.2 = ((bf16[32,24,1024]{2,1,0:T(8,128)(2,1)}), bf16[32,24,1024]{2,1,0:T(8,128)(2,1)}, u32[]{:S(2)}, u32[]{:S(2)}) async-start(bf16[32,24,1024]{2,1,0:T(8,128)(2,1)} %bitcast.93), calls=%async_computation.2 | async-start | bytes 3145728 | tf_op jit(solution)/shard_map/all_to_all | solution.py:475
  105.9 2.5 %copy-start.7 = (bf16[2,1024,512]{2,0,1:T(2,128)(2,1)S(1)}, bf16[2,1024,512]{2,0,1:T(2,128)(2,1)}, u32[]{:S(2)}) copy-start(bf16[2,1024,512]{2,0,1:T(2,128)(2,1)} %get-tuple-element.29) | copy-start | bytes 6291460
  108.4 2.5 %copy-start.6 = (bf16[2,1024,512]{2,0,1:T(2,128)(2,1)S(1)}, bf16[2,1024,512]{2,0,1:T(2,128)(2,1)}, u32[]{:S(2)}) copy-start(bf16[2,1024,512]{2,0,1:T(2,128)(2,1)} %get-tuple-element.30) | copy-start | bytes 6291460
  109.2 5.0 %copy-start.5 = (bf16[2,1024,512]{2,0,1:T(2,128)(2,1)S(1)}, bf16[2,1024,512]{2,0,1:T(2,128)(2,1)}, u32[]{:S(2)}) copy-start(bf16[2,1024,512]{2,0,1:T(2,128)(2,1)} %get-tuple-element.31) | copy-start | bytes 6291460
  109.2 7.9 %collective-permute-start = (bf16[2,64,1024]{2,1,0:T(8,128)(2,1)S(1)}, bf16[2,64,1024]{2,1,0:T(8,128)(2,1)S(1)}, u32[]{:S(2)}, u32[]{:S(2)}) collective-permute-start(bf16[2,64,1024]{2,1,0:T(8,128)(2,1)S(1)} %bitcast.98), channel_id=1, source_target_pairs={{0,1},{1,0},{2,3},{3,2},{4,5},{5,4},{6,7},{7,6},{8,9},{9,8},{10,11... | collective-permute-start | bytes 786440 | tf_op jit(solution)/shard_map/ppermute | solution.py:489
  111.7 3.2 %copy-start.4 = (bf16[2,1024,512]{2,0,1:T(2,128)(2,1)S(1)}, bf16[2,1024,512]{2,0,1:T(2,128)(2,1)}, u32[]{:S(2)}) copy-start(bf16[2,1024,512]{2,0,1:T(2,128)(2,1)} %get-tuple-element.32) | copy-start | bytes 6291460
  111.7 9.7 %collective-permute-start.2 = (bf16[2,64,1024]{2,1,0:T(8,128)(2,1)S(1)}, bf16[2,64,1024]{2,1,0:T(8,128)(2,1)S(1)}, u32[]{:S(2)}, u32[]{:S(2)}) collective-permute-start(bf16[2,64,1024]{2,1,0:T(8,128)(2,1)S(1)} %pad_maximum_fusion.1), channel_id=1, source_target_pairs={{0,3},{1,2},{2,1},{3,0},{4,7},{5,6},{6,5},{7,4},{8,11},{9,10},{10,... | collective-permute-start | bytes 786440 | tf_op jit(solution)/shard_map/ppermute | solution.py:489
  115.8 10.9 %collective-permute-start.6 = (bf16[2,64,1024]{2,1,0:T(8,128)(2,1)S(1)}, bf16[2,64,1024]{2,1,0:T(8,128)(2,1)S(1)}, u32[]{:S(2)}, u32[]{:S(2)}) collective-permute-start(bf16[2,64,1024]{2,1,0:T(8,128)(2,1)S(1)} %pad_maximum_fusion.2), channel_id=1, source_target_pairs={{0,3},{1,2},{2,1},{3,0},{4,7},{5,6},{6,5},{7,4},{8,11},{9,10},{10,... | collective-permute-start | bytes 786440 | tf_op jit(solution)/shard_map/ppermute | solution.py:489
  117.0 9.9 %collective-permute-start.4 = (bf16[2,64,1024]{2,1,0:T(8,128)(2,1)S(1)}, bf16[2,64,1024]{2,1,0:T(8,128)(2,1)S(1)}, u32[]{:S(2)}, u32[]{:S(2)}) collective-permute-start(bf16[2,64,1024]{2,1,0:T(8,128)(2,1)S(1)} %bitcast.97), channel_id=1, source_target_pairs={{0,1},{1,0},{2,3},{3,2},{4,5},{5,4},{6,7},{7,6},{8,9},{9,8},{10,11... | collective-permute-start | bytes 786440 | tf_op jit(solution)/shard_map/ppermute | solution.py:489
  117.2 12.2 %collective-permute-start.1 = (bf16[64,1024]{1,0:T(8,128)(2,1)S(1)}, bf16[64,1024]{1,0:T(8,128)(2,1)S(1)}, u32[]{:S(2)}, u32[]{:S(2)}) collective-permute-start(bf16[64,1024]{1,0:T(8,128)(2,1)S(1)} %slice_bitcast_fusion.18), channel_id=1, source_target_pairs={{0,3},{1,2},{2,1},{3,0},{4,7},{5,6},{6,5},{7,4},{8,11},{9,10},{10,... | collective-permute-start | bytes 393224 | tf_op jit(solution)/shard_map/ppermute | solution.py:489
  121.5 8.0 %collective-permute-start.3 = (bf16[64,1024]{1,0:T(8,128)(2,1)S(1)}, bf16[64,1024]{1,0:T(8,128)(2,1)S(1)}, u32[]{:S(2)}, u32[]{:S(2)}) collective-permute-start(bf16[64,1024]{1,0:T(8,128)(2,1)S(1)} %slice_bitcast_fusion.12), channel_id=1, source_target_pairs={{0,1},{1,0},{2,3},{3,2},{4,5},{5,4},{6,7},{7,6},{8,9},{9,8},{10,11... | collective-permute-start | bytes 393224 | tf_op jit(solution)/shard_map/ppermute | solution.py:489
  126.8 5.0 %collective-permute-start.7 = (bf16[64,1024]{1,0:T(8,128)(2,1)S(1)}, bf16[64,1024]{1,0:T(8,128)(2,1)S(1)}, u32[]{:S(2)}, u32[]{:S(2)}) collective-permute-start(bf16[64,1024]{1,0:T(8,128)(2,1)S(1)} %slice_bitcast_fusion.4), channel_id=1, source_target_pairs={{0,1},{1,0},{2,3},{3,2},{4,5},{5,4},{6,7},{7,6},{8,9},{9,8},{10,11... | collective-permute-start | bytes 393224 | tf_op jit(solution)/shard_map/ppermute | solution.py:489
  127.0 6.3 %collective-permute-start.5 = (bf16[64,1024]{1,0:T(8,128)(2,1)S(1)}, bf16[64,1024]{1,0:T(8,128)(2,1)S(1)}, u32[]{:S(2)}, u32[]{:S(2)}) collective-permute-start(bf16[64,1024]{1,0:T(8,128)(2,1)S(1)} %slice_bitcast_fusion.10), channel_id=1, source_target_pairs={{0,3},{1,2},{2,1},{3,0},{4,7},{5,6},{6,5},{7,4},{8,11},{9,10},{10,... | collective-permute-start | bytes 393224 | tf_op jit(solution)/shard_map/ppermute | solution.py:489

commit v8 on v7

--- a/solution.py
+++ b/solution.py
@@ -231,7 +231,10 @@
     total = total[: 2 * ITEMS]
     for k in range(NO):
         wire[pl.ds(k * 2 * ITEMS, 2 * ITEMS), :] = total
-    send(wire, wire_ref)
+    quarter = NO * 2 * ITEMS // 4
+    for at in range(4):
+        part = pl.ds(at * quarter, quarter)
+        send(wire.at[part], wire_ref.at[part])
     send(mine, mine_ref)
     for copy in copies:
         copy.wait()
@@ -255,7 +258,7 @@
             pltpu.VMEM((RR, SLOTS, SLOTS), F32),
             pltpu.VMEM((RR, SLOTS, HS), F32),
             pltpu.VMEM((RR, SLOTS, 2 * HS), BF),
-            pltpu.SemaphoreType.DMA((3 * ITEMS + 2,)),
+            pltpu.SemaphoreType.DMA((3 * ITEMS + 5,)),
         ],
         compiler_params=pltpu.CompilerParams(vmem_limit_bytes=VMEM),
         name="forward",
@@ -385,7 +388,7 @@
             (sums_ref.at[h], sums.at[h]),
         )
         loads.append(
-            [pltpu.make_async_copy(*p, sems.at[6 * h + at]) for at, p in enumerate(pairs)]
+            [pltpu.make_async_copy(*p, sems.at[5 * h + at]) for at, p in enumerate(pairs)]
         )
         for copy in loads[h]:
             copy.start()
@@ -413,9 +416,12 @@
             query_grad += scale * unit_grad - q * (scale * scale * scale * along)
             grads.append(jnp.concatenate([query_grad, value_grad], axis=1))
         out[h] = join_rounds(grads[0], grads[1]).astype(BF)
-        there = out_ref.at[:, pl.ds(h * 2 * HS, 2 * HS)]
-        stores.append(pltpu.make_async_copy(out.at[h], there, sems.at[6 * h + 5]))
-        stores[h].start()
+        for at in range(2):
+            part = pl.ds(at * (ROWS // 2), ROWS // 2)
+            there = out_ref.at[part, pl.ds(h * 2 * HS, 2 * HS)]
+            sem = sems.at[5 * HH + 2 * h + at]
+            stores.append(pltpu.make_async_copy(out.at[h, part], there, sem))
+            stores[-1].start()
     for copy in stores:
         copy.wait()
 
@@ -441,7 +447,7 @@
             pltpu.VMEM((HH, ROWS, 2 * HS), BF),
             pltpu.VMEM((SLOTS // HS, (NO + 1) * 2 * ITEMS, HS), F32),
             pltpu.VMEM((HH, RR, SLOTS, 2 * HS), F32),
-            pltpu.SemaphoreType.DMA((6 * HH,)),
+            pltpu.SemaphoreType.DMA((7 * HH,)),
         ],
         compiler_params=pltpu.CompilerParams(vmem_limit_bytes=VMEM),
         name="backward",

time: 135 us -> 135 us (level)
  no operation moved by 1% of the time
where the time goes in v8:
time: 135 us; the launch traced here: 134 us
  blocking collectives  41.5 us (31%)
  waiting for transfers between devices  27.1 us (20%)
  Pallas kernels  24.2 us (18%)
  starting transfers between devices  19.7 us (15%)
  local copies, waits for them, and re-layouts  11.4 us (8%)
  matrix products  8.74 us (6%)
    all_to_all x1, blocking collectives, exchange(): return lax.all_to_all(x, 'seq', split_axis=0, concat_axis=0, tiled=True)  41.5 us
    all_to_all x2, waiting for transfers between devices, exchange(): return lax.all_to_all(x, 'seq', split_axis=0, concat_axis=0, tiled=True)  16.9 us
    ppermute x8, starting transfers between devices, swap(): return lax.ppermute(x, 'bkt', [(i, i ^ mask) for i in range(4)])  10.9 us
    ppermute x8, waiting for transfers between devices, swap(): return lax.ppermute(x, 'bkt', [(i, i ^ mask) for i in range(4)])  10.2 us
    transpose x1, local copies, waits for them, and re-layouts, per_device(): weights[i * width:(i + 1) * width].transpose(1, 0, 2)  9.38 us
    all_to_all x2, starting transfers between devices, exchange(): return lax.all_to_all(x, 'seq', split_axis=0, concat_axis=0, tiled=True)  8.78 us
    pallas_call x1, Pallas kernels, between(): pl.pallas_call(between_kernel, grid=(HH,), out_shape=(pltpu.HBM((HH, RR,...  7.48 us
    pallas_call x1, Pallas kernels, forward(): pl.pallas_call(forward_kernel, out_shape=tuple((pltpu.HBM(*shape) for sha...  6.38 us
  transfers between devices with their start and end apart: 10, of which 6 were waited for; matrix products, arithmetic and copies ran while one was open for 9% of the time, Pallas kernels for 6%

profile of v8, /device:TPU:0, one launch (start us, length us, event | category | flops | bytes accessed | tf_op | source)
XLA Modules:
  0.0 134.1 jit_solution(6628925405535992278)
XLA Ops:
  0.0 0.0 copy-start
  0.0 1.6 %copy-done = bf16[256,4096]{1,0:T(8,128)(2,1)S(1)} copy-done((bf16[256,4096]{1,0:T(8,128)(2,1)S(1)}, bf16[256,4096]{1,0:T(8,128)(2,1)}, u32[]{:S(2)}) %copy-start) | copy-done | bytes 2097176
  1.6 0.0 copy-start.1
  1.6 0.0 copy-start.3
  1.6 5.7 %fusion.40.proj_ref = bf16[2,256,512]{2,1,0:T(8,128)(2,1)S(1)} fusion(bf16[4096,2,512]{2,1,0:T(2,128)(2,1)} %param.5, bf16[256,4096]{1,0:T(8,128)(2,1)S(1)} %copy-done), kind=kOutput, calls=%fused_computation.24 | convolution fusion | flops 2147745792 | bytes 11010048 | tf_op jit(solution)/shard_map/td,dcf->ctf/dot_general | solution.py:504
  7.4 0.0 copy-done.1
  7.4 0.0 copy-done.3
  7.4 1.7 %dispatch.1 = (s32[8,256]{1,0:T(8,128)S(1)}, bf16[768,1664]{1,0:T(8,128)(2,1)S(1)}) custom-call(s32[1]{0:T(128)} %bitcast.odd_ref, s32[2,4,256]{2,1,0:T(4,128)S(1)} %copy-done.3, bf16[2,256,512]{2,1,0:T(8,128)(2,1)S(1)} %fusion.40.proj_ref, bf16[256,512]{1,0:T(8,128)(2,1)S(1)} %copy-done.1), custom_call_target="tpu_custom_call" | custom-call | tf_op jit(solution)/shard_map/dispatch/pallas_call | solution.py:94
  9.1 41.5 %all_to_all.33 = bf16[32,24,1664]{2,1,0:T(8,128)(2,1)S(1)} all-to-all(bf16[32,24,1664]{2,1,0:T(8,128)(2,1)S(1)} %bitcast.90), channel_id=1, replica_groups=mesh['seq'=32,'bkt'=4] {'seq'}, dimensions={0} | all-to-all | bytes 5111808 | tf_op jit(solution)/shard_map/all_to_all | solution.py:481
  50.6 6.4 %forward.1 = (bf16[4,2,384,384]{3,2,1,0:T(8,128)(2,1)}, bf16[4,2,384,384]{3,2,1,0:T(8,128)(2,1)}, f32[4,2,384,128]{3,2,1,0:T(8,128)}, bf16[512,384]{1,0:T(8,128)(2,1)}, bf16[128,384]{1,0:T(8,128)(2,1)}) custom-call(bf16[768,1664]{1,0:T(8,128)(2,1)S(1)} %bitcast.89), custom_call_target="tpu_custom_call" | custom-call | tf_op jit(solution)/shard_map/forward/pallas_call | solution.py:251
  57.0 4.1 %all-to-all-start.1 = ((bf16[32,16,384]{2,1,0:T(8,128)(2,1)}), bf16[32,16,384]{2,1,0:T(8,128)(2,1)S(1)}, u32[]{:S(2)}, u32[]{:S(2)}) async-start(bf16[32,16,384]{2,1,0:T(8,128)(2,1)} %bitcast.96), calls=%async_computation.1 | async-start | bytes 786432 | tf_op jit(solution)/shard_map/all_to_all | solution.py:481
  61.1 0.0 copy-start.2
  61.1 7.5 %between.1 = (bf16[4,2,384,384]{3,2,1,0:T(8,128)(2,1)}, bf16[4,2,384,384]{3,2,1,0:T(8,128)(2,1)}, bf16[4,2,384,384]{3,2,1,0:T(8,128)(2,1)}) custom-call(bf16[4,2,384,384]{3,2,1,0:T(8,128)(2,1)} %get-tuple-element.21.probs_ref, bf16[4,2,384,384]{3,2,1,0:T(8,128)(2,1)} %get-tuple-element.22.rows_ref, f32[4,2,384,128]{3,2,1,0:T(8,128)} %get-tuple-element.23.self_ref), custom_call_target="tpu_custom_call" | custom-call | flops 905969664 | bytes 12582912 | tf_op jit(solution)/shard_map/between/pallas_call | solution.py:293
  68.6 2.6 %all-to-all-done.1 = bf16[32,16,384]{2,1,0:T(8,128)(2,1)S(1)} async-done(((bf16[32,16,384]{2,1,0:T(8,128)(2,1)}), bf16[32,16,384]{2,1,0:T(8,128)(2,1)S(1)}, u32[]{:S(2)}, u32[]{:S(2)}) %all-to-all-start.1) | async-done | bytes 393248 | tf_op jit(solution)/shard_map/all_to_all | solution.py:481
  71.2 0.0 copy-done.2
  71.2 6.1 %backward.1 = bf16[768,1024]{1,0:T(8,128)(2,1)} custom-call(bf16[4,2,384,384]{3,2,1,0:T(8,128)(2,1)} %get-tuple-element.24.probs_ref, bf16[4,2,384,384]{3,2,1,0:T(8,128)(2,1)} %get-tuple-element.25.weighted_ref, bf16[4,2,384,384]{3,2,1,0:T(8,128)(2,1)} %get-tuple-element.22.rows_ref, bf16[4,2,384,384]{3,2,1,0:T(8,128)(2,1)} %get-tuple-element.26.sums_ref, ...), custom_call_target="tpu_custom_call" | custom-call | tf_op jit(solution)/shard_map/backward/pallas_call | solution.py:436
  77.3 4.7 %all-to-all-start.2 = ((bf16[32,24,1024]{2,1,0:T(8,128)(2,1)}), bf16[32,24,1024]{2,1,0:T(8,128)(2,1)}, u32[]{:S(2)}, u32[]{:S(2)}) async-start(bf16[32,24,1024]{2,1,0:T(8,128)(2,1)} %bitcast.93), calls=%async_computation.2 | async-start | bytes 3145728 | tf_op jit(solution)/shard_map/all_to_all | solution.py:481
  82.0 0.1 constant_dynamic-slice_fusion.3
  82.1 0.1 pad_add_fusion
  82.2 0.1 copy.17
  82.3 9.4 %slice_bitcast_fusion = (bf16[2,1024,512]{2,0,1:T(2,128)(2,1)}, bf16[2,1024,512]{2,0,1:T(2,128)(2,1)}, bf16[2,1024,512]{2,0,1:T(2,128)(2,1)}, bf16[2,1024,512]{2,0,1:T(2,128)(2,1)}) fusion(bf16[4096,2,512]{2,1,0:T(2,128)(2,1)} %param.5), kind=kLoop, calls=%fused_computation.11 | loop fusion | bytes 16777216 | tf_op jit(solution)/shard_map/transpose | solution.py:517
  91.7 14.2 %all-to-all-done.2 = bf16[32,24,1024]{2,1,0:T(8,128)(2,1)} async-done(((bf16[32,24,1024]{2,1,0:T(8,128)(2,1)}), bf16[32,24,1024]{2,1,0:T(8,128)(2,1)}, u32[]{:S(2)}, u32[]{:S(2)}) %all-to-all-start.2) | async-done | bytes 1572896 | tf_op jit(solution)/shard_map/all_to_all | solution.py:481
  105.9 0.0 copy-start.7
  105.9 2.5 %collect.1 = bf16[2,256,512]{2,1,0:T(8,128)(2,1)S(1)} custom-call(s32[256,8]{1,0:T(8,128)S(1)} %bitcast.92, bf16[768,1024]{1,0:T(8,128)(2,1)} %bitcast.9.got_ref), custom_call_target="tpu_custom_call" | custom-call | tf_op jit(solution)/shard_map/collect/pallas_call | solution.py:470
  108.5 0.0 copy-done.7
  108.5 0.0 copy-start.6
  108.5 0.7 fusion.37
  109.3 0.0 copy-start.5
  109.3 1.7 %collective-permute-start = (bf16[2,64,1024]{2,1,0:T(8,128)(2,1)S(1)}, bf16[2,64,1024]{2,1,0:T(8,128)(2,1)S(1)}, u32[]{:S(2)}, u32[]{:S(2)}) collective-permute-start(bf16[2,64,1024]{2,1,0:T(8,128)(2,1)S(1)} %bitcast.98), channel_id=1, source_target_pairs={{0,1},{1,0},{2,3},{3,2},{4,5},{5,4},{6,7},{7,6},{8,9},{9,8},{10,11... | collective-permute-start | bytes 786440 | tf_op jit(solution)/shard_map/ppermute | solution.py:495
  111.0 0.0 copy-done.6
  111.0 0.7 fusion.34
  111.8 0.0 copy-start.4
  111.8 2.5 %collective-permute-start.2 = (bf16[2,64,1024]{2,1,0:T(8,128)(2,1)S(1)}, bf16[2,64,1024]{2,1,0:T(8,128)(2,1)S(1)}, u32[]{:S(2)}, u32[]{:S(2)}) collective-permute-start(bf16[2,64,1024]{2,1,0:T(8,128)(2,1)S(1)} %pad_maximum_fusion.1), channel_id=1, source_target_pairs={{0,3},{1,2},{2,1},{3,0},{4,7},{5,6},{6,5},{7,4},{8,11},{9,10},{10,... | collective-permute-start | bytes 786440 | tf_op jit(solution)/shard_map/ppermute | solution.py:495
  114.3 0.0 copy-done.5
  114.3 0.7 fusion.31
  115.0 0.0 copy-done.4
  115.0 0.7 fusion.28
  115.9 1.1 collective-permute-start.6
  117.0 0.1 collective-permute-start.4
  117.2 0.0 collective-permute-done
  117.2 0.1 add.40
  117.3 2.2 %collective-permute-start.1 = (bf16[64,1024]{1,0:T(8,128)(2,1)S(1)}, bf16[64,1024]{1,0:T(8,128)(2,1)S(1)}, u32[]{:S(2)}, u32[]{:S(2)}) collective-permute-start(bf16[64,1024]{1,0:T(8,128)(2,1)S(1)} %slice_bitcast_fusion.18), channel_id=1, source_target_pairs={{0,3},{1,2},{2,1},{3,0},{4,7},{5,6},{6,5},{7,4},{8,11},{9,10},{10,... | collective-permute-start | bytes 393224 | tf_op jit(solution)/shard_map/ppermute | solution.py:495
  119.5 2.0 %collective-permute-done.2 = bf16[2,64,1024]{2,1,0:T(8,128)(2,1)S(1)} collective-permute-done((bf16[2,64,1024]{2,1,0:T(8,128)(2,1)S(1)}, bf16[2,64,1024]{2,1,0:T(8,128)(2,1)S(1)}, u32[]{:S(2)}, u32[]{:S(2)}) %collective-permute-start.2) | collective-permute-done | bytes 262176 | tf_op jit(solution)/shard_map/ppermute | solution.py:495
  121.5 0.7 collective-permute-start.3
  122.3 4.5 %collective-permute-done.6 = bf16[2,64,1024]{2,1,0:T(8,128)(2,1)S(1)} collective-permute-done((bf16[2,64,1024]{2,1,0:T(8,128)(2,1)S(1)}, bf16[2,64,1024]{2,1,0:T(8,128)(2,1)S(1)}, u32[]{:S(2)}, u32[]{:S(2)}) %collective-permute-start.6) | collective-permute-done | bytes 262176 | tf_op jit(solution)/shard_map/ppermute | solution.py:495
  126.8 0.1 collective-permute-start.7
  126.9 0.0 collective-permute-done.4
  126.9 0.1 add.44
  127.0 2.5 %collective-permute-start.5 = (bf16[64,1024]{1,0:T(8,128)(2,1)S(1)}, bf16[64,1024]{1,0:T(8,128)(2,1)S(1)}, u32[]{:S(2)}, u32[]{:S(2)}) collective-permute-start(bf16[64,1024]{1,0:T(8,128)(2,1)S(1)} %slice_bitcast_fusion.10), channel_id=1, source_target_pairs={{0,3},{1,2},{2,1},{3,0},{4,7},{5,6},{6,5},{7,4},{8,11},{9,10},{10,... | collective-permute-start | bytes 393224 | tf_op jit(solution)/shard_map/ppermute | solution.py:495
  129.5 0.0 collective-permute-done.1
  129.6 0.0 collective-permute-done.3
  129.6 2.3 %collective-permute-done.7 = bf16[64,1024]{1,0:T(8,128)(2,1)S(1)} collective-permute-done((bf16[64,1024]{1,0:T(8,128)(2,1)S(1)}, bf16[64,1024]{1,0:T(8,128)(2,1)S(1)}, u32[]{:S(2)}, u32[]{:S(2)}) %collective-permute-start.7) | collective-permute-done | bytes 131104 | tf_op jit(solution)/shard_map/ppermute | solution.py:495
  131.9 1.4 %collective-permute-done.5 = bf16[64,1024]{1,0:T(8,128)(2,1)S(1)} collective-permute-done((bf16[64,1024]{1,0:T(8,128)(2,1)S(1)}, bf16[64,1024]{1,0:T(8,128)(2,1)S(1)}, u32[]{:S(2)}, u32[]{:S(2)}) %collective-permute-start.5) | collective-permute-done | bytes 131104 | tf_op jit(solution)/shard_map/ppermute | solution.py:495
  133.3 0.8 pad_maximum_fusion
  (16 shorter events, 0.4 us)
Async XLA Ops:
  0.0 1.6 %copy-start = (bf16[256,4096]{1,0:T(8,128)(2,1)S(1)}, bf16[256,4096]{1,0:T(8,128)(2,1)}, u32[]{:S(2)}) copy-start(bf16[256,4096]{1,0:T(8,128)(2,1)} %param.4) | copy-start | bytes 6291460
  1.6 5.8 %copy-start.1 = (bf16[256,512]{1,0:T(8,128)(2,1)S(1)}, bf16[256,512]{1,0:T(8,128)(2,1)}, u32[]{:S(2)}) copy-start(bf16[256,512]{1,0:T(8,128)(2,1)} %cot_ref.1) | copy-start | bytes 786436
  1.6 5.8 %copy-start.3 = (s32[2,4,256]{2,1,0:T(4,128)S(1)}, s32[2,4,256]{2,1,0:T(4,128)}, u32[]{:S(2)}) copy-start(s32[2,4,256]{2,1,0:T(4,128)} %buckets_ref.1) | copy-start | bytes 24580
  57.0 14.2 %all-to-all-start.1 = ((bf16[32,16,384]{2,1,0:T(8,128)(2,1)}), bf16[32,16,384]{2,1,0:T(8,128)(2,1)S(1)}, u32[]{:S(2)}, u32[]{:S(2)}) async-start(bf16[32,16,384]{2,1,0:T(8,128)(2,1)} %bitcast.96), calls=%async_computation.1 | async-start | bytes 786432 | tf_op jit(solution)/shard_map/all_to_all | solution.py:481
  61.1 10.1 %copy-start.2 = (bf16[128,384]{1,0:T(8,128)(2,1)S(1)}, bf16[128,384]{1,0:T(8,128)(2,1)}, u32[]{:S(2)}) copy-start(bf16[128,384]{1,0:T(8,128)(2,1)} %get-tuple-element.27.mine_ref) | copy-start | bytes 294916
  77.3 28.6 %all-to-all-start.2 = ((bf16[32,24,1024]{2,1,0:T(8,128)(2,1)}), bf16[32,24,1024]{2,1,0:T(8,128)(2,1)}, u32[]{:S(2)}, u32[]{:S(2)}) async-start(bf16[32,24,1024]{2,1,0:T(8,128)(2,1)} %bitcast.93), calls=%async_computation.2 | async-start | bytes 3145728 | tf_op jit(solution)/shard_map/all_to_all | solution.py:481
  105.9 2.5 %copy-start.7 = (bf16[2,1024,512]{2,0,1:T(2,128)(2,1)S(1)}, bf16[2,1024,512]{2,0,1:T(2,128)(2,1)}, u32[]{:S(2)}) copy-start(bf16[2,1024,512]{2,0,1:T(2,128)(2,1)} %get-tuple-element.29) | copy-start | bytes 6291460
  108.5 2.5 %copy-start.6 = (bf16[2,1024,512]{2,0,1:T(2,128)(2,1)S(1)}, bf16[2,1024,512]{2,0,1:T(2,128)(2,1)}, u32[]{:S(2)}) copy-start(bf16[2,1024,512]{2,0,1:T(2,128)(2,1)} %get-tuple-element.30) | copy-start | bytes 6291460
  109.3 5.0 %copy-start.5 = (bf16[2,1024,512]{2,0,1:T(2,128)(2,1)S(1)}, bf16[2,1024,512]{2,0,1:T(2,128)(2,1)}, u32[]{:S(2)}) copy-start(bf16[2,1024,512]{2,0,1:T(2,128)(2,1)} %get-tuple-element.31) | copy-start | bytes 6291460
  109.3 7.9 %collective-permute-start = (bf16[2,64,1024]{2,1,0:T(8,128)(2,1)S(1)}, bf16[2,64,1024]{2,1,0:T(8,128)(2,1)S(1)}, u32[]{:S(2)}, u32[]{:S(2)}) collective-permute-start(bf16[2,64,1024]{2,1,0:T(8,128)(2,1)S(1)} %bitcast.98), channel_id=1, source_target_pairs={{0,1},{1,0},{2,3},{3,2},{4,5},{5,4},{6,7},{7,6},{8,9},{9,8},{10,11... | collective-permute-start | bytes 786440 | tf_op jit(solution)/shard_map/ppermute | solution.py:495
  111.8 3.3 %copy-start.4 = (bf16[2,1024,512]{2,0,1:T(2,128)(2,1)S(1)}, bf16[2,1024,512]{2,0,1:T(2,128)(2,1)}, u32[]{:S(2)}) copy-start(bf16[2,1024,512]{2,0,1:T(2,128)(2,1)} %get-tuple-element.32) | copy-start | bytes 6291460
  111.8 9.7 %collective-permute-start.2 = (bf16[2,64,1024]{2,1,0:T(8,128)(2,1)S(1)}, bf16[2,64,1024]{2,1,0:T(8,128)(2,1)S(1)}, u32[]{:S(2)}, u32[]{:S(2)}) collective-permute-start(bf16[2,64,1024]{2,1,0:T(8,128)(2,1)S(1)} %pad_maximum_fusion.1), channel_id=1, source_target_pairs={{0,3},{1,2},{2,1},{3,0},{4,7},{5,6},{6,5},{7,4},{8,11},{9,10},{10,... | collective-permute-start | bytes 786440 | tf_op jit(solution)/shard_map/ppermute | solution.py:495
  115.9 10.9 %collective-permute-start.6 = (bf16[2,64,1024]{2,1,0:T(8,128)(2,1)S(1)}, bf16[2,64,1024]{2,1,0:T(8,128)(2,1)S(1)}, u32[]{:S(2)}, u32[]{:S(2)}) collective-permute-start(bf16[2,64,1024]{2,1,0:T(8,128)(2,1)S(1)} %pad_maximum_fusion.2), channel_id=1, source_target_pairs={{0,3},{1,2},{2,1},{3,0},{4,7},{5,6},{6,5},{7,4},{8,11},{9,10},{10,... | collective-permute-start | bytes 786440 | tf_op jit(solution)/shard_map/ppermute | solution.py:495
  117.0 9.9 %collective-permute-start.4 = (bf16[2,64,1024]{2,1,0:T(8,128)(2,1)S(1)}, bf16[2,64,1024]{2,1,0:T(8,128)(2,1)S(1)}, u32[]{:S(2)}, u32[]{:S(2)}) collective-permute-start(bf16[2,64,1024]{2,1,0:T(8,128)(2,1)S(1)} %bitcast.97), channel_id=1, source_target_pairs={{0,1},{1,0},{2,3},{3,2},{4,5},{5,4},{6,7},{7,6},{8,9},{9,8},{10,11... | collective-permute-start | bytes 786440 | tf_op jit(solution)/shard_map/ppermute | solution.py:495
  117.3 12.2 %collective-permute-start.1 = (bf16[64,1024]{1,0:T(8,128)(2,1)S(1)}, bf16[64,1024]{1,0:T(8,128)(2,1)S(1)}, u32[]{:S(2)}, u32[]{:S(2)}) collective-permute-start(bf16[64,1024]{1,0:T(8,128)(2,1)S(1)} %slice_bitcast_fusion.18), channel_id=1, source_target_pairs={{0,3},{1,2},{2,1},{3,0},{4,7},{5,6},{6,5},{7,4},{8,11},{9,10},{10,... | collective-permute-start | bytes 393224 | tf_op jit(solution)/shard_map/ppermute | solution.py:495
  121.5 8.0 %collective-permute-start.3 = (bf16[64,1024]{1,0:T(8,128)(2,1)S(1)}, bf16[64,1024]{1,0:T(8,128)(2,1)S(1)}, u32[]{:S(2)}, u32[]{:S(2)}) collective-permute-start(bf16[64,1024]{1,0:T(8,128)(2,1)S(1)} %slice_bitcast_fusion.12), channel_id=1, source_target_pairs={{0,1},{1,0},{2,3},{3,2},{4,5},{5,4},{6,7},{7,6},{8,9},{9,8},{10,11... | collective-permute-start | bytes 393224 | tf_op jit(solution)/shard_map/ppermute | solution.py:495
  126.8 5.0 %collective-permute-start.7 = (bf16[64,1024]{1,0:T(8,128)(2,1)S(1)}, bf16[64,1024]{1,0:T(8,128)(2,1)S(1)}, u32[]{:S(2)}, u32[]{:S(2)}) collective-permute-start(bf16[64,1024]{1,0:T(8,128)(2,1)S(1)} %slice_bitcast_fusion.4), channel_id=1, source_target_pairs={{0,1},{1,0},{2,3},{3,2},{4,5},{5,4},{6,7},{7,6},{8,9},{9,8},{10,11... | collective-permute-start | bytes 393224 | tf_op jit(solution)/shard_map/ppermute | solution.py:495
  127.0 6.3 %collective-permute-start.5 = (bf16[64,1024]{1,0:T(8,128)(2,1)S(1)}, bf16[64,1024]{1,0:T(8,128)(2,1)S(1)}, u32[]{:S(2)}, u32[]{:S(2)}) collective-permute-start(bf16[64,1024]{1,0:T(8,128)(2,1)S(1)} %slice_bitcast_fusion.10), channel_id=1, source_target_pairs={{0,3},{1,2},{2,1},{3,0},{4,7},{5,6},{6,5},{7,4},{8,11},{9,10},{10,... | collective-permute-start | bytes 393224 | tf_op jit(solution)/shard_map/ppermute | solution.py:495
